TPU v7x, 32 devices: a whole 2x2x4 slice. The times are simulated.
32 devices in a mesh: groups: 2 (over y), wide: 4 (over x, core), narrow: 4 (over z).
Axes of the slice: x: 2, y: 2, z: 4, core: 2. Of those that a mesh axis runs over, the one named last changes fastest.
Arguments:
- hidden_in: bfloat16 [2, 64, 16384], P(None, ('groups', 'wide'), 'narrow'), parts along dimension 1, may hold values from -400 to 400
- norm_gain: bfloat16 [16384], P('narrow'), may hold values from 0.5 to 1.5
- qkv_weight: bfloat16 [16384, 9216], P('narrow', 'wide'), may hold values from -0.046875 to 0.046875
- out_weight: bfloat16 [8192, 16384], P('wide', 'narrow'), may hold values from -0.0625 to 0.0625
- lengths: int32 [64], P(('groups', 'wide', 'narrow')), parts along dimension 0, may hold values from 1 to 2048, as said below
- key_cache: bfloat16 [64, 4, 2048, 128], P(('groups', 'wide', 'narrow')), parts along dimension 0, may hold values from -330 to 330
- cache_of_values: bfloat16 [64, 4, 2048, 128], P(('groups', 'wide', 'narrow')), parts along dimension 0, may hold values from -6 to 6
Outputs:
- block_out: bfloat16 [2, 64, 16384], P(None, ('groups', 'wide'), 'narrow'), parts along dimension 1
There are 2 independent parts, one for each index of `groups`. A program takes and returns all parts, laid end to end along the dimension named above; an argument that names none is the same for every part. Nothing has to cross between parts.
Inputs may be any that keep to these rules, and one draw needn't show every extreme that they name: Sequence r has cache slots 0 to lengths[r] - 1 filled; some sequence of every draw has all 2048 filled.
All inputs are finite; a program needn't handle non-finite values.
Results may differ from a plain program's by a relative error of at most 0.012.
Values may be sent and summed in bfloat16 or wider, within the bound.
No kernel may reach another device: no remote copies, remote signals or barrier semaphores. Data moves between devices by JAX's collectives and lax.ppermute only.
A program may use at most 128 MiB of HBM per device.

v0:
```python
import jax
import jax.numpy as jnp
from jax import lax
from jax.sharding import PartitionSpec as P

BLK = 512


norm_epsilon = 1e-05
rope_base = 500000.0


def rope_angles(positions, head_dim):
    half = head_dim // 2
    freqs = rope_base ** (-(jnp.arange(half, dtype=jnp.float32) * 2.0 / head_dim))
    angles = positions.astype(jnp.float32)[..., None] * freqs
    return (jnp.cos(angles), jnp.sin(angles))


def rotate(vectors, cosine, sine):
    half = vectors.shape[-1] // 2
    first = vectors[..., :half]
    second = vectors[..., half:]
    cosine = cosine[..., None, :]
    sine = sine[..., None, :]
    return jnp.concatenate(
        [first * cosine - second * sine, second * cosine + first * sine], axis=-1
    )


def body(hidden_in, norm_gain, qkv_weight, out_weight, lengths, key_cache, cache_of_values):
    wide_size = lax.axis_size("wide")
    narrow_size = lax.axis_size("narrow")
    row_count = lengths.shape[0]
    kv_heads = key_cache.shape[1]
    slots = key_cache.shape[2]
    head_dim = key_cache.shape[3]
    slice_width = out_weight.shape[0]
    width_query = slice_width * wide_size
    key_value_width = kv_heads * head_dim
    head_group = width_query // head_dim // kv_heads

    def project(tokens):
        step_count = tokens.shape[0]
        local_width = tokens.shape[2]
        hidden = tokens.astype(jnp.float32)
        squares = lax.psum(jnp.sum(hidden * hidden, axis=-1), "narrow")
        factor = lax.rsqrt(squares / (local_width * narrow_size) + norm_epsilon)
        normed = (hidden * factor[..., None] * norm_gain.astype(jnp.float32)).astype(jnp.bfloat16)
        ordered = normed.reshape(step_count, narrow_size, row_count, local_width).transpose(
            1, 0, 2, 3
        )[:, :, None]
        gathered = lax.all_gather(ordered, "wide", axis=2, tiled=True)
        flat_rows = gathered.reshape(-1, local_width)
        summed = lax.psum_scatter(
            jnp.dot(flat_rows, qkv_weight, preferred_element_type=jnp.float32),
            "narrow",
            scatter_dimension=0,
            tiled=True,
        )
        pieces = summed.astype(jnp.bfloat16).reshape(step_count, wide_size, row_count, -1)
        mixed = lax.all_to_all(pieces, "wide", split_axis=1, concat_axis=3, tiled=True)
        return mixed.reshape(step_count, row_count, -1)

    def prepare(projected_rows, first):
        step_count = projected_rows.shape[0]
        query_rows = (
            projected_rows[..., :width_query]
            .astype(jnp.float32)
            .reshape(step_count, row_count, -1, head_dim)
        )
        fresh_keys = projected_rows[..., width_query : width_query + key_value_width].astype(
            jnp.float32
        )
        fresh_keys = fresh_keys.reshape(step_count, row_count, kv_heads, head_dim)
        fresh_values = projected_rows[..., width_query + key_value_width :].reshape(
            step_count, row_count, kv_heads, head_dim
        )
        positions = lengths[None, :] + first + jnp.arange(step_count, dtype=jnp.int32)[:, None]
        cosine, sine = rope_angles(positions, head_dim)
        query_rows = rotate(query_rows, cosine, sine).astype(jnp.bfloat16)
        query_rows = query_rows.reshape(step_count, row_count, kv_heads, head_group, head_dim)
        fresh_keys = rotate(fresh_keys, cosine, sine).astype(jnp.bfloat16)
        return (query_rows, fresh_keys, fresh_values)

    def attend(query_rows, fresh_keys, fresh_values, first):
        step_count = query_rows.shape[0]
        scale = head_dim ** (-0.5)
        block_count = (jnp.max(lengths) + BLK - 1) // BLK
        empty = jnp.full(query_rows.shape[:4] + (slots,), -jnp.inf, jnp.float32)

        def score_block(index, scores):
            offset = index * BLK
            keys = lax.dynamic_slice_in_dim(key_cache, offset, BLK, 2)
            products = (
                jnp.einsum(
                    "srkgd,rkcd->srkgc", query_rows, keys, preferred_element_type=jnp.float32
                )
                * scale
            )
            return lax.dynamic_update_slice_in_dim(scores, products, offset, 4)

        scores = lax.fori_loop(0, block_count, score_block, empty)
        valid = jnp.arange(slots, dtype=jnp.int32)[None, :] < lengths[:, None]
        cached = jnp.where(valid[None, :, None, None, :], scores, -jnp.inf)
        newest = (
            jnp.einsum(
                "srkgd,jrkd->srkgj", query_rows, fresh_keys, preferred_element_type=jnp.float32
            )
            * scale
        )
        allowed = (
            jnp.arange(fresh_keys.shape[0])[None, :] <= first + jnp.arange(step_count)[:, None]
        )
        newest = jnp.where(allowed[:, None, None, None, :], newest, -jnp.inf)
        highest = jnp.maximum(jnp.max(cached, axis=-1), jnp.max(newest, axis=-1))
        weights_cache = jnp.exp(cached - highest[..., None])
        weights_new = jnp.exp(newest - highest[..., None])
        denominator = jnp.sum(weights_cache, axis=-1) + jnp.sum(weights_new, axis=-1)
        rounded_cache = weights_cache.astype(jnp.bfloat16)
        rounded_new = weights_new.astype(jnp.bfloat16)
        initial = jnp.einsum(
            "srkgj,jrkd->srkgd", rounded_new, fresh_values, preferred_element_type=jnp.float32
        )

        def value_block(index, totals):
            offset = index * BLK
            stored = lax.dynamic_slice_in_dim(cache_of_values, offset, BLK, 2)
            weights_block = lax.dynamic_slice_in_dim(rounded_cache, offset, BLK, 4)
            return totals + jnp.einsum(
                "srkgc,rkcd->srkgd", weights_block, stored, preferred_element_type=jnp.float32
            )

        totals = lax.fori_loop(0, block_count, value_block, initial)
        return (
            (totals / denominator[..., None])
            .astype(jnp.bfloat16)
            .reshape(step_count, row_count, width_query)
        )

    def finish(attended):
        step_count = attended.shape[0]
        parted = lax.all_to_all(attended[None], "wide", split_axis=3, concat_axis=0, tiled=True)
        spread = lax.all_gather(parted[:, :, None], "narrow", axis=2, tiled=True)
        flat_rows = spread.reshape(-1, slice_width)
        summed = lax.psum_scatter(
            jnp.dot(flat_rows, out_weight, preferred_element_type=jnp.float32).astype(jnp.bfloat16),
            "wide",
            scatter_dimension=0,
            tiled=True,
        )
        return summed.reshape(step_count, narrow_size * row_count, -1)

    first_queries, first_keys, first_values = prepare(project(hidden_in[0:1]), 0)
    first_out = finish(attend(first_queries, first_keys, first_values, 0))
    second_queries, second_keys, second_values = prepare(project(hidden_in[1:2]), 1)
    joined_keys = jnp.concatenate([first_keys, second_keys], axis=0)
    joined_values = jnp.concatenate([first_values, second_values], axis=0)
    second_out = finish(attend(second_queries, joined_keys, joined_values, 1))
    return jnp.concatenate([first_out, second_out], axis=0)


def solution(mesh):
    in_specs = (
        P(None, ("groups", "wide"), "narrow"),
        P("narrow"),
        P("narrow", "wide"),
        P("wide", "narrow"),
        P(("groups", "wide", "narrow")),
        P(("groups", "wide", "narrow"), None, None, None),
        P(("groups", "wide", "narrow"), None, None, None),
    )
    out_specs = P(None, ("groups", "wide"), "narrow")
    return jax.shard_map(body, mesh=mesh, in_specs=in_specs, out_specs=out_specs, check_vma=False)
```

profile of v0, /device:TPU:0, one launch (start us, length us, event | category | flops | bytes accessed | tf_op | source)
XLA Modules:
  0.0 334.3 jit_solution(16881088704470995619)
XLA Ops:
  6.5 1.0 fusion.27
  8.3 13.4 %all-reduce = (f32[1,8]{1,0:T(1,128)S(1)}, f32[1,8]{1,0:T(1,128)S(1)}) all-reduce(f32[1,8]{1,0:T(1,128)S(1)} %bitcast.182, f32[1,8]{1,0:T(1,128)S(1)} %bitcast.181), channel_id=1, replica_groups=mesh['groups'=2,'wide'=4,'narrow'=4] {'narrow'}, use_global_device_ids=true, to_apply=%region_12.13 | all-reduce | flops 16 | bytes 128 | tf_op jit(solution)/shard_map/psum | solution.py:47
  22.8 5.8 %all_gather.14 = bf16[4,1,4,2,4096]{4,3,2,0,1:T(2,128)(2,1)S(1)} all-gather(bf16[4,1,1,2,4096]{4,3,2,0,1:T(2,128)(2,1)S(1)} %bitcast.163), channel_id=1, replica_groups=mesh['groups'=2,'wide'=4,'narrow'=4] {'wide'}, dimensions={2}, use_global_device_ids=true | all-gather | bytes 327680 | tf_op jit(solution)/shard_map/all_gather | solution.py:53
  28.7 10.4 %fusion.64 = f32[32,2304]{1,0:T(8,128)} fusion(bf16[32,4096]{1,0:T(8,128)(2,1)S(1)} %reshape.526, bf16[4096,2304]{1,0:T(8,128)(2,1)} %param.17), kind=kOutput, calls=%fused_computation.117 | convolution fusion | flops 603979776 | bytes 19431424 | tf_op jit(solution)/shard_map/dot_general | solution.py:56
  39.1 5.9 %all_gather.12 = bf16[4,1,4,2,4096]{4,3,2,0,1:T(2,128)(2,1)S(1)} all-gather(bf16[4,1,1,2,4096]{4,3,2,0,1:T(2,128)(2,1)S(1)} %bitcast.164), channel_id=1, replica_groups=mesh['groups'=2,'wide'=4,'narrow'=4] {'wide'}, dimensions={2}, use_global_device_ids=true | all-gather | bytes 327680 | tf_op jit(solution)/shard_map/all_gather | solution.py:53
  45.1 10.4 %fusion.63 = f32[32,2304]{1,0:T(8,128)} fusion(bf16[32,4096]{1,0:T(8,128)(2,1)S(1)} %reshape.515, bf16[4096,2304]{1,0:T(8,128)(2,1)} %param.17), kind=kOutput, calls=%fused_computation.116 | convolution fusion | flops 603979776 | bytes 19431424 | tf_op jit(solution)/shard_map/dot_general | solution.py:56
  58.9 3.3 all-to-all-start.2
  62.9 14.9 %reduce-scatter.5.cloned.1.call-done = f32[8,2304]{1,0:T(8,128)} async-done(((f32[32,2304]{1,0:T(8,128)}), f32[8,2304]{1,0:T(8,128)}) %reduce-scatter.5.cloned.1.call-update) | async-done | bytes 73744 | tf_op jit(solution)/shard_map/reduce_scatter | solution.py:55
  79.3 3.3 all-to-all-start
  82.6 3.9 %all-to-all-done = bf16[1,4,2,2304]{3,2,0,1:T(2,128)(2,1)S(1)} async-done(((bf16[1,4,2,2304]{3,2,0,1:T(2,128)(2,1)}), bf16[1,4,2,2304]{3,2,0,1:T(2,128)(2,1)S(1)}, u32[]{:S(2)}, u32[]{:S(2)}) %all-to-all-start) | async-done | bytes 36896 | tf_op jit(solution)/shard_map/all_to_all | solution.py:62
  87.2 6.5 %while.40 = (s32[]{:T(128)}, f32[1,2,4,16,2048]{4,3,2,1,0:T(8,128)S(1)}, s32[]{:T(128)}, bf16[2,4,2048,128]{3,2,1,0:T(8,128)(2,1)}, bf16[1,2,4,16,128]{4,3,2,1,0...) while((s32[]{:T(128)}, f32[1,2,4,16,2048]{4,3,2,1,0:T(8,128)S(1)}, s32[]{:T(128)}, ...), condition=%wide.region_5.6_spmd, body=%wide.region_4.5_spmd.sunk | while | flops 16842756 | bytes 1344651 | solution.py:103
  87.2 1.6 fusion.87
  88.8 1.6 fusion.87
  90.5 1.6 fusion.87
  92.1 1.6 fusion.87
  93.9 6.5 %while.42 = (s32[]{:T(128)}, f32[1,2,4,16,2048]{4,3,2,1,0:T(8,128)S(1)}, s32[]{:T(128)}, bf16[2,4,2048,128]{3,2,1,0:T(8,128)(2,1)}, bf16[1,2,4,16,128]{4,3,2,1,0...) while((s32[]{:T(128)}, f32[1,2,4,16,2048]{4,3,2,1,0:T(8,128)S(1)}, s32[]{:T(128)}, ...), condition=%wide.region_15.16_spmd, body=%wide.region_14.15_spmd.sunk | while | flops 16842756 | bytes 1344651 | solution.py:103
  93.9 1.6 fusion.93
  95.5 1.6 fusion.93
  97.1 1.6 fusion.93
  98.8 1.6 fusion.93
  102.1 6.0 %while.43 = (s32[]{:T(128)}, f32[1,2,4,16,128]{4,3,2,1,0:T(8,128)S(1)}, s32[]{:T(128)}, bf16[2,4,2048,128]{3,2,1,0:T(8,128)(2,1)}, bf16[1,2,4,16,2048]{4,3,2,1,0...) while((s32[]{:T(128)}, f32[1,2,4,16,128]{4,3,2,1,0:T(8,128)S(1)}, s32[]{:T(128)}, ...), condition=%wide.region_19.20_spmd, body=%wide.region_18.19_spmd.sunk | while | flops 16793604 | bytes 1311883 | solution.py:134
  102.1 1.5 fusion.96
  103.6 1.5 fusion.96
  105.1 1.5 fusion.96
  106.6 1.5 fusion.96
  108.1 6.2 %while.41 = (s32[]{:T(128)}, f32[1,2,4,16,128]{4,3,2,1,0:T(8,128)S(1)}, s32[]{:T(128)}, bf16[2,4,2048,128]{3,2,1,0:T(8,128)(2,1)}, bf16[1,2,4,16,2048]{4,3,2,1,0...) while((s32[]{:T(128)}, f32[1,2,4,16,128]{4,3,2,1,0:T(8,128)S(1)}, s32[]{:T(128)}, ...), condition=%wide.region_8.9_spmd, body=%wide.region_7.8_spmd.sunk | while | flops 16793604 | bytes 1311883 | solution.py:134
  108.2 1.5 fusion.90
  109.7 1.5 fusion.90
  111.2 1.5 fusion.90
  112.7 1.5 fusion.90
  114.5 6.8 %copy.42 = bf16[1,1,2,8192]{2,1,0,3:T(2,128)(2,1)} copy(bf16[1,1,2,8192]{3,2,1,0:T(2,128)(2,1)S(1)} %broadcast_in_dim_reshape.6) | data formatting | bytes 65536 | tf_op jit(solution)/shard_map/broadcast_in_dim;reshape | solution.py:143
  121.8 45.2 %reduce.9 = bf16[8192,2]{1,0:T(8,128)(2,1)S(1)} reduce(bf16[8192,1,1,2]{3,2,1,0:T(2,128)(2,1)} %bitcast.155, bf16[]{:T(256)} %broadcast.203), dimensions={1,2}, to_apply=%bitcast.125.reduce_sub_computation | reduce | bytes 65538
  167.0 3.8 %reshape.556 = bf16[4,2,2048]{2,1,0:T(2,128)(2,1)} reshape(bf16[8192,2]{1,0:T(8,128)(2,1)S(1)} %reduce.9) | data formatting | bytes 65536
  170.8 3.5 %all-to-all-start.1 = ((bf16[4,2,2048]{2,1,0:T(2,128)(2,1)}), bf16[4,2,2048]{2,1,0:T(2,128)(2,1)S(1)}, u32[]{:S(2)}, u32[]{:S(2)}) async-start(bf16[4,2,2048]{2,1,0:T(2,128)(2,1)} %reshape.556), calls=%async_computation.2 | async-start | bytes 65536 | tf_op jit(solution)/shard_map/all_to_all | solution.py:143
  174.4 6.8 %copy.50 = bf16[1,1,2,8192]{2,1,0,3:T(2,128)(2,1)} copy(bf16[1,1,2,8192]{3,2,1,0:T(2,128)(2,1)S(1)} %broadcast_in_dim_reshape.7) | data formatting | bytes 65536 | tf_op jit(solution)/shard_map/broadcast_in_dim;reshape | solution.py:143
  181.2 45.2 %reduce.8 = bf16[8192,2]{1,0:T(8,128)(2,1)S(1)} reduce(bf16[8192,1,1,2]{3,2,1,0:T(2,128)(2,1)} %bitcast.156, bf16[]{:T(256)} %broadcast.203), dimensions={1,2}, to_apply=%bitcast.123.reduce_sub_computation | reduce | bytes 65538
  226.5 3.8 %reshape.554 = bf16[4,2,2048]{2,1,0:T(2,128)(2,1)} reshape(bf16[8192,2]{1,0:T(8,128)(2,1)S(1)} %reduce.8) | data formatting | bytes 65536
  230.3 3.3 all-to-all-start.3
  233.6 5.9 %reshape.557 = bf16[8192,1,1,2]{3,2,1,0:T(2,128)(2,1)} reshape(bf16[4,2,2048]{2,1,0:T(2,128)(2,1)S(1)} %all-to-all-done.1) | data formatting | bytes 65536
  239.6 8.1 %copy.43 = bf16[1,1,2,8192]{3,2,1,0:T(2,128)(2,1)S(1)} copy(bf16[1,1,2,8192]{2,1,0,3:T(2,128)(2,1)} %bitcast.157) | data formatting | bytes 65536 | tf_op jit(solution)/shard_map/all_to_all | solution.py:143
  247.7 13.4 %all_gather.13 = bf16[4,1,4,2,2048]{4,0,3,1,2:T(4,128)(2,1)S(1)} all-gather(bf16[4,1,1,2,2048]{4,0,3,1,2:T(4,128)(2,1)S(1)} %bitcast.173), channel_id=1, replica_groups=mesh['groups'=2,'wide'=4,'narrow'=4] {'narrow'}, dimensions={2}, use_global_device_ids=true | all-gather | bytes 163840 | tf_op jit(solution)/shard_map/all_gather | solution.py:144
  261.3 9.4 %convolution_convert_fusion.1 = bf16[32,4096]{1,0:T(8,128)(2,1)} fusion(bf16[32,2048]{1,0:T(8,128)(2,1)S(1)} %reshape.523, bf16[2048,4096]{1,0:T(8,128)(2,1)} %param.18), kind=kOutput, calls=%fused_computation.25 | convolution fusion | flops 537001984 | bytes 17170432 | tf_op jit(solution)/shard_map/dot_general | solution.py:147
  271.1 5.9 %reshape.555 = bf16[8192,1,1,2]{3,2,1,0:T(2,128)(2,1)} reshape(bf16[4,2,2048]{2,1,0:T(2,128)(2,1)S(1)} %all-to-all-done.3) | data formatting | bytes 65536
  277.1 8.1 %copy.51 = bf16[1,1,2,8192]{3,2,1,0:T(2,128)(2,1)S(1)} copy(bf16[1,1,2,8192]{2,1,0,3:T(2,128)(2,1)} %bitcast.158) | data formatting | bytes 65536 | tf_op jit(solution)/shard_map/all_to_all | solution.py:143
  285.2 13.3 %all_gather.15 = bf16[4,1,4,2,2048]{4,0,3,1,2:T(4,128)(2,1)S(1)} all-gather(bf16[4,1,1,2,2048]{4,0,3,1,2:T(4,128)(2,1)S(1)} %bitcast.174), channel_id=1, replica_groups=mesh['groups'=2,'wide'=4,'narrow'=4] {'narrow'}, dimensions={2}, use_global_device_ids=true | all-gather | bytes 163840 | tf_op jit(solution)/shard_map/all_gather | solution.py:144
  298.7 9.4 %convolution_convert_fusion = bf16[32,4096]{1,0:T(8,128)(2,1)} fusion(bf16[32,2048]{1,0:T(8,128)(2,1)S(1)} %reshape.535, bf16[2048,4096]{1,0:T(8,128)(2,1)} %param.18), kind=kOutput, calls=%fused_computation.24 | convolution fusion | flops 537001984 | bytes 17170432 | tf_op jit(solution)/shard_map/dot_general | solution.py:147
  308.2 18.0 %reduce-scatter.11.cloned.1.call-done = bf16[8,4096]{1,0:T(8,128)(2,1)} async-done(((bf16[32,4096]{1,0:T(8,128)(2,1)}), bf16[8,4096]{1,0:T(8,128)(2,1)}) %reduce-scatter.11.cloned.1.call-update) | async-done | bytes 65552 | tf_op jit(solution)/shard_map/reduce_scatter | solution.py:146
  326.2 1.5 pad_maximum_fusion
  (76 shorter events, 11.1 us)
Async XLA Ops:
  6.5 50.8 %reduce-scatter.9.cloned.1.call-start = ((), (), s32[]{:S(2)}) async-start(), calls=%async_computation.10 | async-start | bytes 368640 | tf_op jit(solution)/shard_map/reduce_scatter | solution.py:55
  39.0 38.7 %reduce-scatter.5.cloned.1.call-start = ((), (), s32[]{:S(2)}) async-start(), calls=%async_computation.8 | async-start | bytes 368640 | tf_op jit(solution)/shard_map/reduce_scatter | solution.py:55
  45.1 10.5 %copy-start = (s32[2]{0:T(128)S(1)}, s32[2]{0:T(128)}, u32[]{:S(2)}) copy-start(s32[2]{0:T(128)} %param.19) | copy-start | bytes 28
  58.9 20.4 %all-to-all-start.2 = ((bf16[1,4,2,2304]{3,2,0,1:T(2,128)(2,1)}), bf16[1,4,2,2304]{3,2,0,1:T(2,128)(2,1)S(1)}, u32[]{:S(2)}, u32[]{:S(2)}) async-start(bf16[1,4,2,2304]{3,2,0,1:T(2,128)(2,1)} %bitcast.36), calls=%async_computation.5 | async-start | bytes 73728 | tf_op jit(solution)/shard_map/all_to_all | solution.py:62
  79.3 7.2 %all-to-all-start = ((bf16[1,4,2,2304]{3,2,0,1:T(2,128)(2,1)}), bf16[1,4,2,2304]{3,2,0,1:T(2,128)(2,1)S(1)}, u32[]{:S(2)}, u32[]{:S(2)}) async-start(bf16[1,4,2,2304]{3,2,0,1:T(2,128)(2,1)} %bitcast.15), calls=%async_computation.1 | async-start | bytes 73728 | tf_op jit(solution)/shard_map/all_to_all | solution.py:62
  170.8 59.5 %all-to-all-start.1 = ((bf16[4,2,2048]{2,1,0:T(2,128)(2,1)}), bf16[4,2,2048]{2,1,0:T(2,128)(2,1)S(1)}, u32[]{:S(2)}, u32[]{:S(2)}) async-start(bf16[4,2,2048]{2,1,0:T(2,128)(2,1)} %reshape.556), calls=%async_computation.2 | async-start | bytes 65536 | tf_op jit(solution)/shard_map/all_to_all | solution.py:143
  230.3 40.8 %all-to-all-start.3 = ((bf16[4,2,2048]{2,1,0:T(2,128)(2,1)}), bf16[4,2,2048]{2,1,0:T(2,128)(2,1)S(1)}, u32[]{:S(2)}, u32[]{:S(2)}) async-start(bf16[4,2,2048]{2,1,0:T(2,128)(2,1)} %reshape.554), calls=%async_computation.6 | async-start | bytes 65536 | tf_op jit(solution)/shard_map/all_to_all | solution.py:143
  233.6 74.7 %reduce-scatter.7.cloned.1.call-start = ((), (), s32[]{:S(2)}) async-start(), calls=%async_computation.9 | async-start | bytes 327680 | tf_op jit(solution)/shard_map/reduce_scatter | solution.py:146
  270.8 55.4 %reduce-scatter.11.cloned.1.call-start = ((), (), s32[]{:S(2)}) async-start(), calls=%async_computation.11 | async-start | bytes 327680 | tf_op jit(solution)/shard_map/reduce_scatter | solution.py:146
Sparse Core Ops, SparseCore 0:
  39.2 18.1 reduce-scatter.8
  59.6 18.0 reduce-scatter.4
  270.9 17.7 reduce-scatter.6
  308.3 17.8 reduce-scatter.10
where the time goes:
time: 336 us; the launch traced here: 334 us
  other arithmetic  99.3 us (30%)
  matrix products  65 us (19%)
  local copies, waits for them, and re-layouts  52.1 us (16%)
  blocking collectives  51.9 us (15%)
  waiting for transfers between devices  37.7 us (11%)
  between operations  14.2 us (4%)
  starting transfers between devices  13.7 us (4%)
    unnamed x4, other arithmetic  90.5 us
    all_gather x2, blocking collectives, finish(): spread = lax.all_gather(parted[:, :, None], 'narrow', axis=2, tiled=True)  26.8 us
    dot_general x2, matrix products, project(): jnp.dot(flat_rows, qkv_weight, preferred_element_type=jnp.float32)  20.8 us
    unnamed x11, local copies, waits for them, and re-layouts  20.1 us
    dot_general x2, matrix products, finish(): jnp.dot(flat_rows, out_weight, preferred_element_type=jnp.float32)  18.9 us
    reduce_scatter x2, waiting for transfers between devices, finish(): lax.psum_scatter(jnp.dot(flat_rows, out_weight, preferred_element_type=jn...  18 us
    all_to_all x4, local copies, waits for them, and re-layouts, finish(): lax.all_to_all(attended[None], 'wide', split_axis=3, concat_axis=0, tiled...  16.2 us
    reduce_scatter x2, waiting for transfers between devices, project(): lax.psum_scatter(jnp.dot(flat_rows, qkv_weight, preferred_element_type=jn...  15.8 us
  transfers between devices with their start and end apart: 8, of which 4 were waited for; matrix products, arithmetic and copies ran while one was open for 35% of the time, Pallas kernels for 0%

commit v1 on v0

v1 whole, which is shorter than its diff:
```python
import functools

import jax
import jax.numpy as jnp
import numpy as np
from jax import lax
from jax.experimental import pallas as pl
from jax.experimental.pallas import tpu as pltpu
from jax.sharding import PartitionSpec as P

F32 = jnp.float32
BF16 = jnp.bfloat16
LANES = 128
MIB = 1 << 20
norm_epsilon = 1e-05
rope_base = 500000.0


def row_order(tokens, steps, narrow, rows, owner_major):
    out = lax.broadcasted_iota(jnp.int32, (tokens, tokens), 0)
    src = lax.broadcasted_iota(jnp.int32, (tokens, tokens), 1)
    block = steps * narrow * rows
    row = lax.rem(out, rows)
    inner = lax.div(lax.rem(out, block), rows)
    if owner_major:
        step, owner = lax.rem(inner, steps), lax.div(inner, steps)
        want = (step * narrow + owner) * rows + row
    else:
        owner, step = lax.rem(inner, narrow), lax.div(inner, narrow)
        want = (owner * steps + step) * rows + row
    want = want + lax.div(out, block) * block
    return (src == want).astype(BF16)


def chunks(total, size):
    return [(at, min(size, total - at)) for at in range(0, total, size)]


def project_kernel(steps, narrow, rows, x_ref, gain_ref, w_ref, o_ref, scaled):
    tokens, depth = x_ref.shape
    width = w_ref.shape[1]
    per = steps * rows
    order = row_order(tokens, steps, narrow, rows, True)
    squares = jnp.zeros((tokens, 1), F32)
    for at, size in chunks(depth, 512):
        part = jnp.dot(order, x_ref[:, at : at + size], preferred_element_type=F32)
        squares = squares + jnp.sum(part * part, axis=1, keepdims=True)
        scaled[:, at : at + size] = (part * gain_ref[:, at : at + size].astype(F32)).astype(BF16)
    high = squares.astype(BF16).astype(F32)
    lane = lax.broadcasted_iota(jnp.int32, (tokens, LANES), 1)
    head = jnp.where(lane == 0, high, jnp.where(lane == 1, squares - high, 0.0)).astype(BF16)
    for d in range(tokens // per):
        o_ref[d, :, :LANES] = head[d * per : (d + 1) * per]
    for at, size in chunks(width, 768):
        y = jnp.dot(scaled[...], w_ref[:, at : at + size], preferred_element_type=F32).astype(BF16)
        for d in range(tokens // per):
            o_ref[d, :, LANES + at : LANES + at + size] = y[d * per : (d + 1) * per]


def attend_kernel(
    wide, narrow, steps, model, slice_width,
    lengths_ref, part_ref, cos_ref, sin_ref, key_ref, value_ref, o_ref, proj, query, total,
):
    rows, kv_heads, slots, head_dim = key_ref.shape
    per = steps * rows
    width = part_ref.shape[2] - LANES
    width_query = slice_width * wide
    heads = width_query // head_dim
    group = heads // kv_heads
    scale = head_dim ** (-0.5)

    head = part_ref[0:narrow, :, 0:LANES].astype(F32)
    head = jnp.sum(head, axis=0)
    squares = head[:, 0:1] + head[:, 1:2]
    factor = lax.rsqrt(squares / model + norm_epsilon)
    for w in range(wide):
        part = part_ref[w * narrow, :, LANES:].astype(F32)
        for n in range(1, narrow):
            part = part + part_ref[w * narrow + n, :, LANES:].astype(F32)
        proj[:, w * width : (w + 1) * width] = (part * factor).astype(BF16).astype(F32)

    cosine = cos_ref[...]
    sine = sin_ref[...]

    def turned(at):
        x = proj[:, at : at + head_dim]
        return (x * cosine + pltpu.roll(x, head_dim // 2, 1) * sine).astype(BF16).astype(F32)

    for h in range(heads):
        q = turned(h * head_dim)
        for s in range(steps):
            for r in range(rows):
                i = s * rows + r
                query[h // group, r, s * group + h % group : s * group + h % group + 1, :] = q[i : i + 1]
    lane = lax.broadcasted_iota(jnp.int32, (steps * group, slots), 1)
    sub = lax.broadcasted_iota(jnp.int32, (steps * group, 1), 0)
    step_of = lax.div(sub, group)
    for k in range(kv_heads):
        fresh_key = turned(width_query + k * head_dim)
        at = width_query + (kv_heads + k) * head_dim
        fresh_value = proj[:, at : at + head_dim]
        for r in range(rows):
            q = query[k, r]
            scores = lax.dot_general(
                q.astype(BF16), key_ref[r, k], (((1,), (1,)), ((), ())), preferred_element_type=F32
            ) * scale
            scores = jnp.where(lane < lengths_ref[r], scores, -jnp.inf)
            highest = jnp.max(scores, axis=1, keepdims=True)
            newest = []
            for j in range(steps):
                i = j * rows + r
                dot = jnp.sum(q * fresh_key[i : i + 1], axis=1, keepdims=True) * scale
                dot = jnp.where(step_of >= j, dot, -jnp.inf)
                newest.append(dot)
                highest = jnp.maximum(highest, dot)
            weights = jnp.exp(scores - highest)
            denominator = jnp.sum(weights, axis=1, keepdims=True)
            out = jnp.dot(weights.astype(BF16), value_ref[r, k], preferred_element_type=F32)
            for j in range(steps):
                i = j * rows + r
                weight = jnp.exp(newest[j] - highest)
                denominator = denominator + weight
                out = out + weight.astype(BF16).astype(F32) * fresh_value[i : i + 1]
            out = out / denominator
            for s in range(steps):
                for g in range(group):
                    at = (k * group + g) * head_dim
                    w, col = at // slice_width, at % slice_width
                    total[w, s * rows + r : s * rows + r + 1, col : col + head_dim] = out[
                        s * group + g : s * group + g + 1
                    ]
    for w in range(wide):
        message = total[w].astype(BF16)
        for n in range(narrow):
            o_ref[w * narrow + n] = message


def output_kernel(steps, narrow, rows, x_ref, w_ref, o_ref, gathered, ordered):
    sources, per, depth = x_ref.shape
    tokens = sources * per
    for d in range(sources):
        gathered[d * per : (d + 1) * per] = x_ref[d].astype(F32)
    order = row_order(tokens, steps, narrow, rows, False)
    for at, size in chunks(depth, 512):
        ordered[:, at : at + size] = jnp.dot(
            order, gathered[:, at : at + size].astype(BF16), preferred_element_type=F32
        ).astype(BF16)
    for at, size in chunks(w_ref.shape[1], 512):
        o_ref[:, at : at + size] = jnp.dot(
            ordered[...], w_ref[:, at : at + size], preferred_element_type=F32
        ).astype(BF16)


def whole():
    return pl.BlockSpec(memory_space=pltpu.VMEM)


def resident(array):
    return pltpu.with_memory_space_constraint(array, pltpu.VMEM)


def body(hidden_in, norm_gain, qkv_weight, out_weight, lengths, key_cache, cache_of_values):
    wide = lax.axis_size("wide")
    narrow = lax.axis_size("narrow")
    steps, block_rows, depth = hidden_in.shape
    rows, kv_heads, slots, head_dim = key_cache.shape
    width = qkv_weight.shape[1]
    slice_width, out_width = out_weight.shape
    tokens = steps * block_rows * wide
    sources = wide * narrow
    per = steps * rows
    heads = slice_width * wide // head_dim

    with jax.named_scope("rotary_angles"):
        positions = (lengths[None, :] + jnp.arange(steps, dtype=jnp.int32)[:, None]).reshape(-1)
        half = head_dim // 2
        freqs = rope_base ** (-(jnp.arange(half, dtype=F32) * 2.0 / head_dim))
        angles = positions.astype(F32)[:, None] * freqs
        cosine = jnp.concatenate([jnp.cos(angles), jnp.cos(angles)], axis=1)
        sine = jnp.concatenate([-jnp.sin(angles), jnp.sin(angles)], axis=1)

    gathered = lax.all_gather(hidden_in.reshape(steps * block_rows, depth), "wide", axis=0, tiled=True)
    partial = pl.pallas_call(
        functools.partial(project_kernel, steps, narrow, rows),
        out_shape=jax.ShapeDtypeStruct((sources, per, LANES + width), BF16),
        in_specs=[whole()] * 3,
        out_specs=whole(),
        scratch_shapes=[pltpu.VMEM((tokens, depth), BF16)],
        compiler_params=pltpu.CompilerParams(vmem_limit_bytes=12 * MIB),
        cost_estimate=pl.CostEstimate(
            flops=2 * tokens * depth * width, bytes_accessed=2 * depth * width, transcendentals=0
        ),
        name="project",
    )(gathered, norm_gain.reshape(1, -1), resident(qkv_weight))
    parts = lax.all_to_all(partial, ("wide", "narrow"), 0, 0, tiled=True)
    attended = pl.pallas_call(
        functools.partial(attend_kernel, wide, narrow, steps, depth * narrow, slice_width),
        out_shape=jax.ShapeDtypeStruct((sources, per, slice_width), BF16),
        in_specs=[pl.BlockSpec(memory_space=pltpu.SMEM)] + [whole()] * 5,
        out_specs=whole(),
        scratch_shapes=[
            pltpu.VMEM((per, width * wide), F32),
            pltpu.VMEM((kv_heads, rows, steps * heads // kv_heads, head_dim), F32),
            pltpu.VMEM((wide, per, slice_width), F32),
        ],
        compiler_params=pltpu.CompilerParams(vmem_limit_bytes=12 * MIB),
        cost_estimate=pl.CostEstimate(
            flops=4 * per * heads * slots * head_dim,
            bytes_accessed=4 * rows * kv_heads * slots * head_dim,
            transcendentals=per * heads * slots,
        ),
        name="attend",
    )(lengths, parts, cosine, sine, resident(key_cache), resident(cache_of_values))
    spread = lax.all_to_all(attended, ("wide", "narrow"), 0, 0, tiled=True)
    products = pl.pallas_call(
        functools.partial(output_kernel, steps, narrow, rows),
        out_shape=jax.ShapeDtypeStruct((tokens, out_width), BF16),
        in_specs=[whole()] * 2,
        out_specs=whole(),
        scratch_shapes=[pltpu.VMEM((tokens, slice_width), F32), pltpu.VMEM((tokens, slice_width), BF16)],
        compiler_params=pltpu.CompilerParams(vmem_limit_bytes=12 * MIB),
        cost_estimate=pl.CostEstimate(
            flops=2 * tokens * slice_width * out_width, bytes_accessed=2 * slice_width * out_width, transcendentals=0
        ),
        name="output",
    )(spread, resident(out_weight))
    sums = lax.all_to_all(products.reshape(wide, steps * block_rows, out_width), "wide", 0, 0, tiled=True)
    total = jnp.sum(sums.astype(F32), axis=0).astype(BF16)
    return total.reshape(steps, block_rows, out_width)


def solution(mesh):
    in_specs = (
        P(None, ("groups", "wide"), "narrow"),
        P("narrow"),
        P("narrow", "wide"),
        P("wide", "narrow"),
        P(("groups", "wide", "narrow")),
        P(("groups", "wide", "narrow"), None, None, None),
        P(("groups", "wide", "narrow"), None, None, None),
    )
    out_specs = P(None, ("groups", "wide"), "narrow")
    return jax.shard_map(body, mesh=mesh, in_specs=in_specs, out_specs=out_specs, check_vma=False)
```

time: 336 us -> 80.4 us (0.24)
  other arithmetic: 99.3 us -> 0.95 us
  matrix products: 65 us -> 0 us
  local copies, waits for them, and re-layouts: 52.1 us -> 17.3 us
  waiting for transfers between devices: 37.7 us -> 10.8 us
  blocking collectives: 51.9 us -> 33.3 us
  between operations: 14.2 us -> 0.05 us
  Pallas kernels: 0 us -> 12 us
  starting transfers between devices: 13.7 us -> 5.52 us
    unnamed x4 -> x0, other arithmetic: 90.5 us -> none
    dot_general x23 -> x0, matrix products: 65 us -> none  [the longest x2 20.8 us: project(): jnp.dot(flat_rows, qkv_weight, preferred_element_type=jnp.float32)]
    reduce_scatter x4 -> x0, waiting for transfers between devices: 33.7 us -> none  [the longest x2 18 us: finish(): lax.psum_scatter(jnp.dot(flat_rows, out_weight, preferred_element_type=jn...]
    all_gather x4 -> x1, blocking collectives: 38.4 us -> 8.83 us  [body(): lax.all_gather(hidden_in.reshape(steps * block_rows, depth), 'wide', axis...]
    all_to_all x0 -> x2, blocking collectives: none -> 24.5 us  [the longest x1 13.2 us: body(): spread = lax.all_to_all(attended, ('wide', 'narrow'), 0, 0, tiled=True)]
    all_to_all x4 -> x0, local copies, waits for them, and re-layouts: 16.2 us -> none  [finish(): lax.all_to_all(attended[None], 'wide', split_axis=3, concat_axis=0, tiled...]
    another operation x9 -> x0, local copies, waits for them, and re-layouts: 13.9 us -> none  [the longest x4 13.6 us: finish(): attended[None]]
    psum x1 -> x0, blocking collectives: 13.4 us -> none  [project(): squares = lax.psum(jnp.sum(hidden * hidden, axis=-1), 'narrow')]
  transfers between devices with their start and end apart: 8 -> 1, of which waited for: 4 -> 1; matrix products, arithmetic and copies ran while one was open for 35% -> 0% of each run, Pallas kernels for 0% -> 0%
where the time goes in v1:
time: 80.4 us; the launch traced here: 80 us
  blocking collectives  33.3 us (41%)
  local copies, waits for them, and re-layouts  17.3 us (22%)
  Pallas kernels  12 us (15%)
  waiting for transfers between devices  10.8 us (13%)
  starting transfers between devices  5.52 us (7%)
  other arithmetic  0.95 us (1%)
    unnamed x10, local copies, waits for them, and re-layouts  16.5 us
    all_to_all x1, blocking collectives, body(): spread = lax.all_to_all(attended, ('wide', 'narrow'), 0, 0, tiled=True)  13.2 us
    all_to_all x1, blocking collectives, body(): lax.all_to_all(products.reshape(wide, steps * block_rows, out_width), 'wi...  11.2 us
    all_to_all x1, waiting for transfers between devices, body(): parts = lax.all_to_all(partial, ('wide', 'narrow'), 0, 0, tiled=True)  10.8 us
    all_gather x1, blocking collectives, body(): lax.all_gather(hidden_in.reshape(steps * block_rows, depth), 'wide', axis...  8.83 us
    all_to_all x1, starting transfers between devices, body(): parts = lax.all_to_all(partial, ('wide', 'narrow'), 0, 0, tiled=True)  5.52 us
    pallas_call x1, Pallas kernels, body(): pl.pallas_call(functools.partial(attend_kernel, wide, narrow, steps, dept...  4.53 us
    pallas_call x1, Pallas kernels, body(): pl.pallas_call(functools.partial(project_kernel, steps, narrow, rows), ou...  4.3 us
  transfers between devices with their start and end apart: 1, of which 1 were waited for; matrix products, arithmetic and copies ran while one was open for 0% of the time, Pallas kernels for 0%

profile of v1, /device:TPU:0, one launch (start us, length us, event | category | flops | bytes accessed | tf_op | source)
XLA Modules:
  0.0 80.0 jit_solution(3808377656427754604)
XLA Ops:
  0.0 0.0 copy-start.4
  0.0 0.7 reshape.35.gain_ref
  0.7 8.8 %all_gather.3.x_ref = bf16[64,4096]{1,0:T(8,128)(2,1)S(1)} all-gather(bf16[16,4096]{1,0:T(8,128)(2,1)} %bitcast.4), channel_id=1, replica_groups=mesh['groups'=2,'wide'=4,'narrow'=4] {'wide'}, dimensions={0}, use_global_device_ids=true | all-gather | bytes 655360 | tf_op jit(solution)/shard_map/all_gather | solution.py:182
  9.6 0.0 copy-start
  9.6 6.4 %copy-done = bf16[4096,2304]{1,0:T(8,128)(2,1)S(1)} copy-done((bf16[4096,2304]{1,0:T(8,128)(2,1)S(1)}, bf16[4096,2304]{1,0:T(8,128)(2,1)}, u32[]{:S(2)}) %copy-start) | copy-done | bytes 18874392
  15.9 4.3 %project.1 = bf16[16,4,2432]{2,1,0:T(4,128)(2,1)} custom-call(bf16[64,4096]{1,0:T(8,128)(2,1)S(1)} %all_gather.3.x_ref, bf16[1,4096]{1,0:T(2,128)(2,1)S(1)} %reshape.35.gain_ref, bf16[4096,2304]{1,0:T(8,128)(2,1)S(1)} %copy-done), custom_call_target="tpu_custom_call" | custom-call | flops 1207959552 | bytes 18874368 | tf_op jit(solution)/shard_map/project/pallas_call | solution.py:183
  20.2 5.5 %all-to-all-start = ((bf16[16,4,2432]{2,1,0:T(4,128)(2,1)}), bf16[16,4,2432]{2,1,0:T(4,128)(2,1)S(1)}, u32[]{:S(2)}, u32[]{:S(2)}) async-start(bf16[16,4,2432]{2,1,0:T(4,128)(2,1)} %project.1), calls=%async_computation | async-start | bytes 622592 | tf_op jit(solution)/shard_map/all_to_all | solution.py:195
  25.8 0.0 copy-done.4
  25.8 0.1 convert_element_type.13
  25.9 0.1 fusion
  26.0 0.1 pad_maximum_fusion
  26.1 10.8 %all-to-all-done.part_ref = bf16[16,4,2432]{2,1,0:T(4,128)(2,1)S(1)} async-done(((bf16[16,4,2432]{2,1,0:T(4,128)(2,1)}), bf16[16,4,2432]{2,1,0:T(4,128)(2,1)S(1)}, u32[]{:S(2)}, u32[]{:S(2)}) %all-to-all-start) | async-done | bytes 311328 | tf_op jit(solution)/shard_map/all_to_all | solution.py:195
  36.9 0.0 copy-start.2
  36.9 2.2 %copy-done.2 = bf16[2,4,2048,128]{3,2,1,0:T(8,128)(2,1)S(1)} copy-done((bf16[2,4,2048,128]{3,2,1,0:T(8,128)(2,1)S(1)}, bf16[2,4,2048,128]{3,2,1,0:T(8,128)(2,1)}, u32[]{:S(2)}) %copy-start.2) | copy-done | bytes 4194328
  39.1 0.0 copy-start.3
  39.1 2.2 %copy-done.3 = bf16[2,4,2048,128]{3,2,1,0:T(8,128)(2,1)S(1)} copy-done((bf16[2,4,2048,128]{3,2,1,0:T(8,128)(2,1)S(1)}, bf16[2,4,2048,128]{3,2,1,0:T(8,128)(2,1)}, u32[]{:S(2)}) %copy-start.3) | copy-done | bytes 4194328
  41.3 4.5 %attend.1 = bf16[16,4,2048]{2,1,0:T(4,128)(2,1)S(1)} custom-call(s32[2]{0:T(128)S(1)} %copy-done.4, bf16[16,4,2432]{2,1,0:T(4,128)(2,1)S(1)} %all-to-all-done.part_ref, f32[4,128]{1,0:T(4,128)S(1)} %get-tuple-element.8.cos_ref, f32[4,128]{1,0:T(4,128)S(1)} %get-tuple-element.9.sin_ref, bf16[2,4,2048,128]{3,2,1,0:T(8,128)(2,1)S(1)} %copy-done.2, ...), custom_call_target="tpu_custom_call" | custom-call | flops 268435456 | bytes 8388608 | tf_op jit(solution)/shard_map/attend/pallas_call | solution.py:196
  45.8 13.2 %all_to_all.15.x_ref = bf16[16,4,2048]{2,1,0:T(4,128)(2,1)S(1)} all-to-all(bf16[16,4,2048]{2,1,0:T(4,128)(2,1)S(1)} %attend.1), channel_id=1, replica_groups=mesh['groups'=2,'wide'=4,'narrow'=4] {'wide','narrow'}, dimensions={0} | all-to-all | bytes 524288 | tf_op jit(solution)/shard_map/all_to_all | solution.py:214
  59.0 0.0 copy-start.1
  59.0 5.8 %copy-done.1 = bf16[2048,4096]{1,0:T(8,128)(2,1)S(1)} copy-done((bf16[2048,4096]{1,0:T(8,128)(2,1)S(1)}, bf16[2048,4096]{1,0:T(8,128)(2,1)}, u32[]{:S(2)}) %copy-start.1) | copy-done | bytes 16777240
  64.8 3.2 %output.1 = bf16[64,4096]{1,0:T(8,128)(2,1)S(1)} custom-call(bf16[16,4,2048]{2,1,0:T(4,128)(2,1)S(1)} %all_to_all.15.x_ref, bf16[2048,4096]{1,0:T(8,128)(2,1)S(1)} %copy-done.1), custom_call_target="tpu_custom_call" | custom-call | flops 1073741824 | bytes 16777216 | tf_op jit(solution)/shard_map/output/pallas_call | solution.py:215
  68.0 11.2 %all_to_all.16 = bf16[4,16,4096]{2,1,0:T(8,128)(2,1)S(1)} all-to-all(bf16[4,16,4096]{2,1,0:T(8,128)(2,1)S(1)} %bitcast.3), channel_id=1, replica_groups=mesh['groups'=2,'wide'=4,'narrow'=4] {'wide'}, dimensions={0} | all-to-all | bytes 1048576 | tf_op jit(solution)/shard_map/all_to_all | solution.py:227
  79.2 0.7 reduce_sum.12
  (2 shorter events, 0.0 us)
Async XLA Ops:
  0.0 25.8 %copy-start.4 = (s32[2]{0:T(128)S(1)}, s32[2]{0:T(128)}, u32[]{:S(2)}) copy-start(s32[2]{0:T(128)} %lengths_ref.1) | copy-start | bytes 28
  9.6 6.4 %copy-start = (bf16[4096,2304]{1,0:T(8,128)(2,1)S(1)}, bf16[4096,2304]{1,0:T(8,128)(2,1)}, u32[]{:S(2)}) copy-start(bf16[4096,2304]{1,0:T(8,128)(2,1)} %w_ref.2) | copy-start | bytes 56623108
  20.2 16.7 %all-to-all-start = ((bf16[16,4,2432]{2,1,0:T(4,128)(2,1)}), bf16[16,4,2432]{2,1,0:T(4,128)(2,1)S(1)}, u32[]{:S(2)}, u32[]{:S(2)}) async-start(bf16[16,4,2432]{2,1,0:T(4,128)(2,1)} %project.1), calls=%async_computation | async-start | bytes 622592 | tf_op jit(solution)/shard_map/all_to_all | solution.py:195
  36.9 2.2 %copy-start.2 = (bf16[2,4,2048,128]{3,2,1,0:T(8,128)(2,1)S(1)}, bf16[2,4,2048,128]{3,2,1,0:T(8,128)(2,1)}, u32[]{:S(2)}) copy-start(bf16[2,4,2048,128]{3,2,1,0:T(8,128)(2,1)} %key_ref.1) | copy-start | bytes 12582916
  39.1 2.2 %copy-start.3 = (bf16[2,4,2048,128]{3,2,1,0:T(8,128)(2,1)S(1)}, bf16[2,4,2048,128]{3,2,1,0:T(8,128)(2,1)}, u32[]{:S(2)}) copy-start(bf16[2,4,2048,128]{3,2,1,0:T(8,128)(2,1)} %value_ref.1) | copy-start | bytes 12582916
  59.0 5.8 %copy-start.1 = (bf16[2048,4096]{1,0:T(8,128)(2,1)S(1)}, bf16[2048,4096]{1,0:T(8,128)(2,1)}, u32[]{:S(2)}) copy-start(bf16[2048,4096]{1,0:T(8,128)(2,1)} %w_ref.3) | copy-start | bytes 50331652

commit v2 on v1

v2 whole, which is shorter than its diff:
```python
import functools

import jax
import jax.numpy as jnp
import numpy as np
from jax import lax
from jax.experimental import pallas as pl
from jax.experimental.pallas import tpu as pltpu
from jax.sharding import PartitionSpec as P

F32 = jnp.float32
BF16 = jnp.bfloat16
LANES = 128
MIB = 1 << 20
norm_epsilon = 1e-05
rope_base = 500000.0


def chunks(total, size):
    return [(at, min(size, total - at)) for at in range(0, total, size)]


def iotas(tokens):
    out = lax.broadcasted_iota(jnp.int32, (tokens, tokens), 0)
    src = lax.broadcasted_iota(jnp.int32, (tokens, tokens), 1)
    return out, src


def whole():
    return pl.BlockSpec(memory_space=pltpu.VMEM)


def hbm():
    return pl.BlockSpec(memory_space=pl.ANY)


def params():
    return pltpu.CompilerParams(vmem_limit_bytes=16 * MIB)


def swap(array, axis, distance):
    size = lax.axis_size(axis)
    return lax.ppermute(array, axis, [(i, i ^ distance) for i in range(size)])


def resident(array):
    return pltpu.with_memory_space_constraint(array, pltpu.VMEM)


def fetch_kernel(spans, turns, *refs):
    count = len(spans)
    sources, sem = refs[:count], refs[-1]
    outs = refs[len(refs) - 1 - count - 2 * bool(turns) : -1]
    copies = []
    for i, (at, size) in enumerate(spans):
        copies.append(pltpu.make_async_copy(sources[i].at[pl.ds(at, size)], outs[i], sem.at[i]))
    for copy in copies:
        copy.start()
    if turns:
        steps, rows = turns
        lengths_ref, freqs_ref = refs[count : count + 2]
        cos_ref, sin_ref = outs[-2:]
        for s in range(steps):
            for r in range(rows):
                i = s * rows + r
                angle = (lengths_ref[r] + s).astype(F32) * freqs_ref[...]
                lane = lax.broadcasted_iota(jnp.int32, angle.shape, 1)
                cos_ref[i : i + 1] = jnp.cos(angle)
                sin_ref[i : i + 1] = jnp.where(lane < angle.shape[1] // 2, -1.0, 1.0) * jnp.sin(angle)
    for copy in copies:
        copy.wait()


def fetch(spans, after, turns=()):
    arrays = [pltpu.with_memory_space_constraint(a, pltpu.HBM) for a, _, _ in spans]
    outs = [pltpu.VMEM((n,) + a.shape[1:], a.dtype) for a, _, n in spans]
    size = sum(2 * n * a.size // a.shape[0] * a.dtype.itemsize for a, _, n in spans)
    extra, extra_specs = [], []
    if turns:
        steps, lengths, freqs = turns
        turns = (steps, lengths.shape[0])
        extra, extra_specs = [lengths, freqs], [pl.BlockSpec(memory_space=pltpu.SMEM), whole()]
        outs += [jax.ShapeDtypeStruct((steps * lengths.shape[0], freqs.shape[1]), F32)] * 2
    return pl.pallas_call(
        functools.partial(fetch_kernel, [(at, n) for _, at, n in spans], turns),
        out_shape=outs,
        in_specs=[pl.BlockSpec(memory_space=pltpu.HBM)] * len(arrays) + extra_specs + [hbm()] * len(after),
        out_specs=[whole()] * len(outs),
        scratch_shapes=[pltpu.SemaphoreType.DMA((len(arrays),))],
        compiler_params=params(),
        cost_estimate=pl.CostEstimate(flops=0, bytes_accessed=size, transcendentals=0),
        name="fetch",
    )(*arrays, *extra, *after)


def project_kernel(wide, narrow, steps, rows, *refs):
    blocks, (gain_ref, near_ref, w_ref) = refs[:wide], refs[wide : wide + 3]
    outs, (scaled, acc, far, sem) = refs[wide + 3 : -4], refs[-4:]
    block, depth = blocks[0].shape
    tokens = block * wide
    split, width = near_ref.shape
    rest = []
    for i, (at, size) in enumerate(chunks(depth - split, 512)):
        rest.append(
            pltpu.make_async_copy(w_ref.at[pl.ds(split + at, size)], far.at[pl.ds(at, size)], sem.at[i])
        )
        rest[-1].start()
    per = steps * rows
    here = lax.axis_index("narrow")
    out, src = iotas(tokens)
    row = lax.rem(out, rows)
    step = lax.rem(lax.div(out, rows), steps)
    d = lax.rem(lax.div(out, per), wide)
    owner = lax.bitwise_xor(lax.div(out, per * wide), here)
    order = (src == ((d * steps + step) * narrow + owner) * rows + row).astype(BF16)
    squares = jnp.zeros((tokens, 1), F32)
    for at, size in chunks(depth, 512):
        x = jnp.concatenate([b[:, at : at + size] for b in blocks], axis=0)
        part = jnp.dot(order, x, preferred_element_type=F32)
        squares = squares + jnp.sum(part * part, axis=1, keepdims=True)
        scaled[:, at : at + size] = (part * gain_ref[:, at : at + size].astype(F32)).astype(BF16)
    high = squares.astype(BF16).astype(F32)
    lane = lax.broadcasted_iota(jnp.int32, (tokens, LANES), 1)
    head = jnp.where(lane == 0, high, jnp.where(lane == 1, squares - high, 0.0)).astype(BF16)
    span = per * wide
    for e in range(narrow):
        outs[e][:, :LANES] = head[e * span : (e + 1) * span]
    for at, size in chunks(width, 768):
        acc[:, at : at + size] = jnp.dot(
            scaled[:, :split], near_ref[:, at : at + size], preferred_element_type=F32
        )
    for i, (low, deep) in enumerate(chunks(depth - split, 512)):
        rest[i].wait()
        for at, size in chunks(width, 768):
            y = acc[:, at : at + size] + jnp.dot(
                scaled[:, split + low : split + low + deep],
                far[low : low + deep, at : at + size],
                preferred_element_type=F32,
            )
            if i < len(rest) - 1:
                acc[:, at : at + size] = y
                continue
            y = y.astype(BF16)
            for e in range(narrow):
                outs[e][:, LANES + at : LANES + at + size] = y[e * span : (e + 1) * span]


def normalize_kernel(wide, narrow, model, *refs):
    parts, outs = refs[:narrow], refs[-wide:]
    per = outs[0].shape[0]
    head = sum(p[:, :LANES].astype(F32) for p in parts)
    factor = lax.rsqrt((head[:, 0:1] + head[:, 1:2]) / model + norm_epsilon)
    total = sum(p[:, LANES:].astype(F32) for p in parts) * factor
    for d in range(wide):
        outs[d][...] = total[d * per : (d + 1) * per].astype(BF16)


def attend_kernel(wide, steps, slice_width, *refs):
    lengths_ref, parts = refs[0], refs[1 : 1 + wide]
    cos_ref, sin_ref, key_ref, value_ref = refs[1 + wide : 5 + wide]
    outs = refs[5 + wide : 5 + 2 * wide]
    stack, proj, query, total = refs[5 + 2 * wide :]
    rows, kv_heads, slots, head_dim = key_ref.shape
    width = parts[0].shape[1]
    width_query = slice_width * wide
    heads = width_query // head_dim
    group = heads // kv_heads
    scale = head_dim ** (-0.5)
    here = lax.axis_index("wide")

    for d in range(wide):
        stack[d] = parts[d][...].astype(F32)
    for w in range(wide):
        proj[:, w * width : (w + 1) * width] = stack[lax.bitwise_xor(here, w)]

    cosine = cos_ref[...]
    sine = sin_ref[...]

    def turned(at):
        x = proj[:, at : at + head_dim]
        return (x * cosine + pltpu.roll(x, head_dim // 2, 1) * sine).astype(BF16).astype(F32)

    for h in range(heads):
        q = turned(h * head_dim)
        for s in range(steps):
            for r in range(rows):
                i = s * rows + r
                at = s * group + h % group
                query[h // group, r, at : at + 1, :] = q[i : i + 1]
    lane = lax.broadcasted_iota(jnp.int32, (steps * group, slots), 1)
    step_of = lax.div(lax.broadcasted_iota(jnp.int32, (steps * group, 1), 0), group)
    for k in range(kv_heads):
        fresh_key = turned(width_query + k * head_dim)
        at = width_query + (kv_heads + k) * head_dim
        fresh_value = proj[:, at : at + head_dim]
        for r in range(rows):
            q = query[k, r]
            scores = lax.dot_general(
                q.astype(BF16), key_ref[r, k], (((1,), (1,)), ((), ())), preferred_element_type=F32
            ) * scale
            scores = jnp.where(lane < lengths_ref[r], scores, -jnp.inf)
            highest = jnp.max(scores, axis=1, keepdims=True)
            newest = []
            for j in range(steps):
                i = j * rows + r
                dot = jnp.sum(q * fresh_key[i : i + 1], axis=1, keepdims=True) * scale
                dot = jnp.where(step_of >= j, dot, -jnp.inf)
                newest.append(dot)
                highest = jnp.maximum(highest, dot)
            weights = jnp.exp(scores - highest)
            denominator = jnp.sum(weights, axis=1, keepdims=True)
            out = jnp.dot(weights.astype(BF16), value_ref[r, k], preferred_element_type=F32)
            for j in range(steps):
                i = j * rows + r
                weight = jnp.exp(newest[j] - highest)
                denominator = denominator + weight
                out = out + weight.astype(BF16).astype(F32) * fresh_value[i : i + 1]
            out = out / denominator
            for s in range(steps):
                for g in range(group):
                    at = (k * group + g) * head_dim
                    w, col = at // slice_width, at % slice_width
                    i = s * rows + r
                    total[w, i : i + 1, col : col + head_dim] = out[s * group + g : s * group + g + 1]
    for d in range(wide):
        outs[d][...] = total[lax.bitwise_xor(here, d)].astype(BF16)


def join_kernel(*refs):
    per = refs[0].shape[0]
    scratch = refs[-1]
    for d, ref in enumerate(refs[:-2]):
        scratch[d * per : (d + 1) * per] = ref[...].astype(F32)
    refs[-2][...] = scratch[...].astype(BF16)


def output_kernel(wide, narrow, steps, rows, *refs):
    blocks, w_refs, (keep_ref, send_ref, ordered) = refs[:narrow], refs[narrow:-3], refs[-3:]
    split = w_refs[0].shape[0]
    block, depth = blocks[0].shape
    tokens = block * narrow
    per = steps * rows
    here = lax.axis_index("narrow")
    out, src = iotas(tokens)
    row = lax.rem(out, rows)
    owner = lax.rem(lax.div(out, rows), narrow)
    step = lax.rem(lax.div(out, rows * narrow), steps)
    d = lax.div(out, per * narrow)
    d = lax.rem(d, wide // 2) * 2 + lax.div(d, wide // 2)
    e = lax.bitwise_xor(owner, here)
    order = (src == ((e * wide + d) * steps + step) * rows + row).astype(BF16)
    for at, size in chunks(depth, 512):
        x = jnp.concatenate([b[:, at : at + size] for b in blocks], axis=0)
        ordered[:, at : at + size] = jnp.dot(order, x, preferred_element_type=F32).astype(BF16)
    half = tokens // 2
    for at, size in chunks(w_refs[0].shape[1], 512):
        y = jnp.dot(ordered[:, :split], w_refs[0][:, at : at + size], preferred_element_type=F32)
        y = y + jnp.dot(ordered[:, split:], w_refs[1][:, at : at + size], preferred_element_type=F32)
        keep_ref[:, at : at + size] = y[:half]
        send_ref[:, at : at + size] = y[half:].astype(BF16)


def pair_kernel(keep_ref, other_ref, *outs):
    block = outs[0].shape[0]
    for x, out in enumerate(outs):
        span = pl.ds(x * block, block)
        out[...] = (keep_ref[span] + other_ref[span].astype(F32)).astype(out.dtype)


def total_kernel(*refs):
    refs[-1][...] = sum(ref[...].astype(F32) for ref in refs[:-1]).astype(BF16)


def call(kernel, name, outs, inputs, scratch=(), specs=None, flops=0, size=0, exps=0):
    return pl.pallas_call(
        kernel,
        out_shape=outs,
        in_specs=specs or [whole()] * len(inputs),
        out_specs=jax.tree.map(lambda _: whole(), outs),
        scratch_shapes=list(scratch),
        compiler_params=params(),
        cost_estimate=pl.CostEstimate(flops=flops, bytes_accessed=size, transcendentals=exps),
        name=name,
    )(*inputs)


def body(hidden_in, norm_gain, qkv_weight, out_weight, lengths, key_cache, cache_of_values):
    wide = lax.axis_size("wide")
    narrow = lax.axis_size("narrow")
    steps, block_rows, depth = hidden_in.shape
    rows, kv_heads, slots, head_dim = key_cache.shape
    width = qkv_weight.shape[1]
    slice_width, out_width = out_weight.shape
    block = steps * block_rows
    tokens = block * wide
    per = steps * rows
    heads = slice_width * wide // head_dim
    shape = jax.ShapeDtypeStruct

    half = np.arange(head_dim) % (head_dim // 2)
    freqs = np.asarray(rope_base ** (-2.0 * half / head_dim), np.float32)[None]
    qkv_split = depth // 2
    out_split = slice_width // 2

    (qkv_near,) = fetch([(qkv_weight, 0, qkv_split)], [])
    with jax.named_scope("gather_tokens"):
        own = hidden_in.reshape(block, depth)
        blocks = []
        for x in range(wide // 2):
            near = swap(own, "wide", 2 * x) if x else own
            if x:
                near, qkv_near = lax.optimization_barrier((near, qkv_near))
            blocks += [near, swap(near, "wide", 1)]
    partial = call(
        functools.partial(project_kernel, wide, narrow, steps, rows), "project",
        [shape((per * wide, LANES + width), BF16)] * narrow,
        blocks
        + [norm_gain.reshape(1, -1), resident(qkv_near), pltpu.with_memory_space_constraint(qkv_weight, pltpu.HBM)],
        [
            pltpu.VMEM((tokens, depth), BF16),
            pltpu.VMEM((tokens, width), F32),
            pltpu.VMEM((depth - qkv_split, width), BF16),
            pltpu.SemaphoreType.DMA((-(-(depth - qkv_split) // 512),)),
        ],
        [whole()] * (wide + 2) + [pl.BlockSpec(memory_space=pltpu.HBM)],
        flops=2 * tokens * depth * width, size=2 * depth * width,
    )
    keys, values, out_near, cosine, sine = fetch(
        [(key_cache, 0, rows), (cache_of_values, 0, rows), (out_weight, 0, out_split)],
        [partial[0]],
        (steps, lengths, jnp.asarray(freqs)),
    )
    with jax.named_scope("sum_over_narrow"):
        parts = [swap(p, "narrow", e) if e else p for e, p in enumerate(partial)]
    normed = call(
        functools.partial(normalize_kernel, wide, narrow, depth * narrow), "normalize",
        [shape((per, width), BF16)] * wide,
        parts + [cosine],
        specs=[whole()] * narrow + [hbm()],
        size=4 * tokens * width,
    )
    with jax.named_scope("columns_to_owner"):
        mine = [swap(p, "wide", d) if d else p for d, p in enumerate(normed)]
    attended = call(
        functools.partial(attend_kernel, wide, steps, slice_width), "attend",
        [shape((per, slice_width), BF16)] * wide,
        [lengths] + mine + [cosine, sine, resident(keys), resident(values)],
        [
            pltpu.VMEM((wide, per, width), F32),
            pltpu.VMEM((per, width * wide), F32),
            pltpu.VMEM((kv_heads, rows, steps * heads // kv_heads, head_dim), F32),
            pltpu.VMEM((wide, per, slice_width), F32),
        ],
        [pl.BlockSpec(memory_space=pltpu.SMEM)] + [whole()] * (wide + 4),
        flops=4 * per * heads * slots * head_dim,
        size=4 * rows * kv_heads * slots * head_dim,
        exps=per * heads * slots,
    )
    with jax.named_scope("heads_to_weights"):
        arrived = [swap(p, "wide", d) if d else p for d, p in enumerate(attended)]
    joined = call(
        join_kernel, "join", shape((per * wide, slice_width), BF16), arrived,
        [pltpu.VMEM((per * wide, slice_width), F32)], size=4 * per * wide * slice_width,
    )
    (out_far,) = fetch([(out_weight, out_split, slice_width - out_split)], [joined])
    with jax.named_scope("gather_over_narrow"):
        spread = [swap(joined, "narrow", e) if e else joined for e in range(narrow)]
    keep, send = call(
        functools.partial(output_kernel, wide, narrow, steps, rows), "output",
        [shape((tokens // 2, out_width), F32), shape((tokens // 2, out_width), BF16)],
        spread + [resident(out_near), resident(out_far)],
        [pltpu.VMEM((tokens, slice_width), BF16)],
        flops=2 * tokens * slice_width * out_width, size=2 * slice_width * out_width,
    )
    with jax.named_scope("sum_over_wide"):
        other = swap(send, "wide", 1)
        chip = call(
            pair_kernel, "pair",
            [shape((block, out_width), BF16 if x else F32) for x in range(wide // 2)],
            [keep, other], size=6 * tokens * out_width // 2,
        )
        sums = [swap(c, "wide", 2 * x) if x else c for x, c in enumerate(chip)]
    total = call(
        total_kernel, "total", shape((block, out_width), BF16), sums, size=8 * block * out_width
    )
    return total.reshape(steps, block_rows, out_width)


def solution(mesh):
    in_specs = (
        P(None, ("groups", "wide"), "narrow"),
        P("narrow"),
        P("narrow", "wide"),
        P("wide", "narrow"),
        P(("groups", "wide", "narrow")),
        P(("groups", "wide", "narrow"), None, None, None),
        P(("groups", "wide", "narrow"), None, None, None),
    )
    out_specs = P(None, ("groups", "wide"), "narrow")
    return jax.shard_map(body, mesh=mesh, in_specs=in_specs, out_specs=out_specs, check_vma=False)
```

time: 80.4 us -> 57.9 us (0.72)
  blocking collectives: 33.3 us -> 0 us
  local copies, waits for them, and re-layouts: 17.3 us -> 0.03 us
  Pallas kernels: 12 us -> 26.4 us
  starting transfers between devices: 5.52 us -> 17.7 us
  waiting for transfers between devices: 10.8 us -> 13.4 us
  other arithmetic: 0.95 us -> 0 us
    all_to_all x2 -> x0, blocking collectives: 24.5 us -> none  [the longest x1 13.2 us: body(): spread = lax.all_to_all(attended, ('wide', 'narrow'), 0, 0, tiled=True)]
    ppermute x0 -> x17, starting transfers between devices: none -> 17.7 us  [swap(): return lax.ppermute(array, axis, [(i, i ^ distance) for i in range(size)])]
    unnamed x10 -> x8, local copies, waits for them, and re-layouts: 16.5 us -> 0.02 us
    pallas_call x3 -> x10, Pallas kernels: 12 us -> 26.4 us  [the longest x3 13.5 us: fetch(): pl.pallas_call(functools.partial(fetch_kernel, [(at, n) for _, at, n in s...]
    ppermute x0 -> x17, waiting for transfers between devices: none -> 13.4 us  [swap(): return lax.ppermute(array, axis, [(i, i ^ distance) for i in range(size)])]
    all_to_all x1 -> x0, waiting for transfers between devices: 10.8 us -> none  [body(): parts = lax.all_to_all(partial, ('wide', 'narrow'), 0, 0, tiled=True)]
    all_gather x1 -> x0, blocking collectives: 8.83 us -> none  [body(): lax.all_gather(hidden_in.reshape(steps * block_rows, depth), 'wide', axis...]
    all_to_all x1 -> x0, starting transfers between devices: 5.52 us -> none  [body(): parts = lax.all_to_all(partial, ('wide', 'narrow'), 0, 0, tiled=True)]
  transfers between devices with their start and end apart: 1 -> 17, of which waited for: 1 -> 8; matrix products, arithmetic and copies ran while one was open for 0% -> 0% of each run, Pallas kernels for 0% -> 23%
where the time goes in v2:
time: 57.9 us; the launch traced here: 57.7 us
  Pallas kernels  26.4 us (46%)
  starting transfers between devices  17.7 us (31%)
  waiting for transfers between devices  13.4 us (23%)
    ppermute x17, starting transfers between devices, swap(): return lax.ppermute(array, axis, [(i, i ^ distance) for i in range(size)])  17.7 us
    pallas_call x3, Pallas kernels, fetch(): pl.pallas_call(functools.partial(fetch_kernel, [(at, n) for _, at, n in s...  13.5 us
    ppermute x17, waiting for transfers between devices, swap(): return lax.ppermute(array, axis, [(i, i ^ distance) for i in range(size)])  13.4 us
    pallas_call x7, Pallas kernels, call(): pl.pallas_call(kernel, out_shape=outs, in_specs=specs or [whole()] * len(...  12.9 us
  transfers between devices with their start and end apart: 17, of which 8 were waited for; matrix products, arithmetic and copies ran while one was open for 0% of the time, Pallas kernels for 23%

profile of v2, /device:TPU:0, one launch (start us, length us, event | category | flops | bytes accessed | tf_op | source)
XLA Modules:
  0.0 57.7 jit_solution(9606959038334658762)
XLA Ops:
  0.0 2.9 %collective-permute-start.1 = (bf16[16,4096]{1,0:T(8,128)(2,1)}, bf16[16,4096]{1,0:T(8,128)(2,1)S(1)}, u32[]{:S(2)}, u32[]{:S(2)}) collective-permute-start(bf16[16,4096]{1,0:T(8,128)(2,1)} %bitcast.2), channel_id=1, source_target_pairs={{0,8},{4,12},{8,0},{12,4},{1,9},{5,13},{9,1},{13,5},{2,10},{6,14},... | collective-permute-start | bytes 393224 | tf_op jit(solution)/shard_map/gather_tokens/ppermute | solution.py:43
  2.9 0.0 collective-permute-start
  2.9 3.7 %fetch.3.refs_5_ = bf16[2048,2304]{1,0:T(8,128)(2,1)S(1)} custom-call(bf16[4096,2304]{1,0:T(8,128)(2,1)} %refs_6_.1), custom_call_target="tpu_custom_call" | custom-call | bytes 18874368 | tf_op jit(solution)/shard_map/fetch/pallas_call | solution.py:84
  6.6 0.0 collective-permute-done.1.refs_2_
  6.7 0.5 collective-permute-start.2
  7.2 0.0 copy-done.3
  7.2 0.0 copy-start.1
  7.3 0.0 copy-start.2
  7.3 0.0 collective-permute-done.refs_1_
  7.3 0.9 %collective-permute-done.2.refs_3_ = bf16[16,4096]{1,0:T(8,128)(2,1)S(1)} collective-permute-done((bf16[16,4096]{1,0:T(8,128)(2,1)S(1)}, bf16[16,4096]{1,0:T(8,128)(2,1)S(1)}, u32[]{:S(2)}, u32[]{:S(2)}) %collective-permute-start.2) | collective-permute-done | bytes 131104 | tf_op jit(solution)/shard_map/gather_tokens/ppermute | solution.py:43
  8.2 0.0 copy-done
  8.2 4.5 %project.1 = (bf16[16,2432]{1,0:T(8,128)(2,1)S(1)}, bf16[16,2432]{1,0:T(8,128)(2,1)S(1)}, bf16[16,2432]{1,0:T(8,128)(2,1)S(1)}, bf16[16,2432]{1,0:T(8,128)(2,1)S(1)}) custom-call(bf16[16,4096]{1,0:T(8,128)(2,1)S(1)} %bitcast.4, bf16[16,4096]{1,0:T(8,128)(2,1)S(1)} %collective-permute-done.refs_1_, bf16[16,4096]{1,0:T(8,128)(2,1)S(1)} %collective-permute-done.1.refs_2_, ...), custom_call_target="tpu_custom_call" | custom-call | flops 1207959552 | bytes 18874368 | tf_op jit(solution)/shard_map/project/pallas_call | solution.py:275
  12.7 1.7 %collective-permute-start.3 = (bf16[16,2432]{1,0:T(8,128)(2,1)S(1)}, bf16[16,2432]{1,0:T(8,128)(2,1)S(1)}, u32[]{:S(2)}, u32[]{:S(2)}) collective-permute-start(bf16[16,2432]{1,0:T(8,128)(2,1)S(1)} %get-tuple-element.31), channel_id=1, source_target_pairs={{0,1},{1,0},{2,3},{3,2},{4,5},{5,4},{6,7},{7,6},{8,9},{9,8},{10,11... | collective-permute-start | bytes 233480 | tf_op jit(solution)/shard_map/sum_over_narrow/ppermute | solution.py:43
  14.4 2.6 %collective-permute-start.4 = (bf16[16,2432]{1,0:T(8,128)(2,1)S(1)}, bf16[16,2432]{1,0:T(8,128)(2,1)S(1)}, u32[]{:S(2)}, u32[]{:S(2)}) collective-permute-start(bf16[16,2432]{1,0:T(8,128)(2,1)S(1)} %get-tuple-element.32), channel_id=1, source_target_pairs={{0,2},{1,3},{2,0},{3,1},{4,6},{5,7},{6,4},{7,5},{8,10},{9,11},{10,... | collective-permute-start | bytes 233480 | tf_op jit(solution)/shard_map/sum_over_narrow/ppermute | solution.py:43
  17.0 0.2 collective-permute-start.5
  17.2 0.0 copy-done.1
  17.2 0.0 copy-done.2
  17.2 6.4 %fetch.4 = (bf16[2,4,2048,128]{3,2,1,0:T(8,128)(2,1)S(1)}, bf16[2,4,2048,128]{3,2,1,0:T(8,128)(2,1)S(1)}, bf16[1024,4096]{1,0:T(8,128)(2,1)S(1)}, f32[4,128]{1,0:T(4,128)S(1)}, f32[4,128]{1,0:T(4,128)S(1)}) custom-call(bf16[2,4,2048,128]{3,2,1,0:T(8,128)(2,1)} %refs_0_.5, bf16[2,4,2048,128]{3,2,1,0:T(8,128)(2,1)} %refs_1_.1, bf16[2048,4096]{1,0:T(8,128)(2,1)} %refs_0_.7, ...), custom_call_target="tpu_custom_call" | custom-call | bytes 33554432 | tf_op jit(solution)/shard_map/fetch/pallas_call | solution.py:84
  23.6 0.0 collective-permute-done.3.refs_1_
  23.6 0.0 collective-permute-done.4.refs_2_
  23.6 0.0 collective-permute-done.5.refs_3_
  23.6 0.2 normalize.1
  23.8 0.1 collective-permute-start.6
  23.9 1.6 %collective-permute-start.7 = (bf16[4,2304]{1,0:T(4,128)(2,1)S(1)}, bf16[4,2304]{1,0:T(4,128)(2,1)S(1)}, u32[]{:S(2)}, u32[]{:S(2)}) collective-permute-start(bf16[4,2304]{1,0:T(4,128)(2,1)S(1)} %get-tuple-element.37), channel_id=1, source_target_pairs={{0,8},{4,12},{8,0},{12,4},{1,9},{5,13},{9,1},{13,5},{2,10},{6,14},... | collective-permute-start | bytes 55304 | tf_op jit(solution)/shard_map/columns_to_owner/ppermute | solution.py:43
  25.5 0.3 collective-permute-start.8
  25.8 0.0 collective-permute-done.6.refs_2_
  25.8 2.0 %collective-permute-done.7.refs_3_ = bf16[4,2304]{1,0:T(4,128)(2,1)S(1)} collective-permute-done((bf16[4,2304]{1,0:T(4,128)(2,1)S(1)}, bf16[4,2304]{1,0:T(4,128)(2,1)S(1)}, u32[]{:S(2)}, u32[]{:S(2)}) %collective-permute-start.7) | collective-permute-done | bytes 18464 | tf_op jit(solution)/shard_map/columns_to_owner/ppermute | solution.py:43
  27.7 0.9 %collective-permute-done.8.refs_4_ = bf16[4,2304]{1,0:T(4,128)(2,1)S(1)} collective-permute-done((bf16[4,2304]{1,0:T(4,128)(2,1)S(1)}, bf16[4,2304]{1,0:T(4,128)(2,1)S(1)}, u32[]{:S(2)}, u32[]{:S(2)}) %collective-permute-start.8) | collective-permute-done | bytes 18464 | tf_op jit(solution)/shard_map/columns_to_owner/ppermute | solution.py:43
  28.6 4.3 %attend.1 = (bf16[4,2048]{1,0:T(4,128)(2,1)S(1)}, bf16[4,2048]{1,0:T(4,128)(2,1)S(1)}, bf16[4,2048]{1,0:T(4,128)(2,1)S(1)}, bf16[4,2048]{1,0:T(4,128)(2,1)S(1)}) custom-call(s32[2]{0:T(128)S(1)} %copy-done.1, bf16[4,2304]{1,0:T(4,128)(2,1)S(1)} %get-tuple-element.35.refs_1_, bf16[4,2304]{1,0:T(4,128)(2,1)S(1)} %collective-permute-done.6.refs_2_, ...), custom_call_target="tpu_custom_call" | custom-call | flops 268435456 | bytes 8388608 | tf_op jit(solution)/shard_map/attend/pallas_call | solution.py:275
  33.0 0.2 collective-permute-start.9
  33.2 0.7 %collective-permute-start.10 = (bf16[4,2048]{1,0:T(4,128)(2,1)S(1)}, bf16[4,2048]{1,0:T(4,128)(2,1)S(1)}, u32[]{:S(2)}, u32[]{:S(2)}) collective-permute-start(bf16[4,2048]{1,0:T(4,128)(2,1)S(1)} %get-tuple-element.44), channel_id=1, source_target_pairs={{0,8},{4,12},{8,0},{12,4},{1,9},{5,13},{9,1},{13,5},{2,10},{6,14},... | collective-permute-start | bytes 49160 | tf_op jit(solution)/shard_map/heads_to_weights/ppermute | solution.py:43
  33.9 1.0 %collective-permute-start.11 = (bf16[4,2048]{1,0:T(4,128)(2,1)S(1)}, bf16[4,2048]{1,0:T(4,128)(2,1)S(1)}, u32[]{:S(2)}, u32[]{:S(2)}) collective-permute-start(bf16[4,2048]{1,0:T(4,128)(2,1)S(1)} %get-tuple-element.45), channel_id=1, source_target_pairs={{0,12},{4,8},{8,4},{12,0},{1,13},{5,9},{9,5},{13,1},{2,14},{6,10},... | collective-permute-start | bytes 49160 | tf_op jit(solution)/shard_map/heads_to_weights/ppermute | solution.py:43
  34.9 0.0 collective-permute-done.9.refs_1_
  34.9 2.1 %collective-permute-done.10.refs_2_ = bf16[4,2048]{1,0:T(4,128)(2,1)S(1)} collective-permute-done((bf16[4,2048]{1,0:T(4,128)(2,1)S(1)}, bf16[4,2048]{1,0:T(4,128)(2,1)S(1)}, u32[]{:S(2)}, u32[]{:S(2)}) %collective-permute-start.10) | collective-permute-done | bytes 16416 | tf_op jit(solution)/shard_map/heads_to_weights/ppermute | solution.py:43
  37.0 0.1 collective-permute-done.11.refs_3_
  37.2 3.7 %collective-permute-start.14 = (bf16[16,2048]{1,0:T(8,128)(2,1)S(1)}, bf16[16,2048]{1,0:T(8,128)(2,1)S(1)}, u32[]{:S(2)}, u32[]{:S(2)}) collective-permute-start(bf16[16,2048]{1,0:T(8,128)(2,1)S(1)} %join.1.refs_1_.refs_0_), channel_id=1, source_target_pairs={{0,3},{1,2},{2,1},{3,0},{4,7},{5,6},{6,5},{7,4},{8,11},{9,10},{10,... | collective-permute-start | bytes 196616 | tf_op jit(solution)/shard_map/gather_over_narrow/ppermute | solution.py:43
  40.9 0.0 collective-permute-start.13
  40.9 0.8 %collective-permute-start.12 = (bf16[16,2048]{1,0:T(8,128)(2,1)S(1)}, bf16[16,2048]{1,0:T(8,128)(2,1)S(1)}, u32[]{:S(2)}, u32[]{:S(2)}) collective-permute-start(bf16[16,2048]{1,0:T(8,128)(2,1)S(1)} %join.1.refs_1_.refs_0_), channel_id=1, source_target_pairs={{0,1},{1,0},{2,3},{3,2},{4,5},{5,4},{6,7},{7,6},{8,9},{9,8},{10,11... | collective-permute-start | bytes 196616 | tf_op jit(solution)/shard_map/gather_over_narrow/ppermute | solution.py:43
  41.6 3.4 %fetch.5.refs_5_ = bf16[1024,4096]{1,0:T(8,128)(2,1)S(1)} custom-call(bf16[2048,4096]{1,0:T(8,128)(2,1)} %refs_0_.7, bf16[16,2048]{1,0:T(8,128)(2,1)S(1)} %join.1.refs_1_.refs_0_), custom_call_target="tpu_custom_call" | custom-call | bytes 16777216 | tf_op jit(solution)/shard_map/fetch/pallas_call | solution.py:84
  45.0 0.0 collective-permute-done.14.refs_3_
  45.0 1.5 %collective-permute-done.13.refs_2_ = bf16[16,2048]{1,0:T(8,128)(2,1)S(1)} collective-permute-done((bf16[16,2048]{1,0:T(8,128)(2,1)S(1)}, bf16[16,2048]{1,0:T(8,128)(2,1)S(1)}, u32[]{:S(2)}, u32[]{:S(2)}) %collective-permute-start.13) | collective-permute-done | bytes 65568 | tf_op jit(solution)/shard_map/gather_over_narrow/ppermute | solution.py:43
  46.5 0.0 collective-permute-done.12.refs_1_
  46.6 3.2 %output.1 = (f32[32,4096]{1,0:T(8,128)S(1)}, bf16[32,4096]{1,0:T(8,128)(2,1)S(1)}) custom-call(bf16[16,2048]{1,0:T(8,128)(2,1)S(1)} %join.1.refs_1_.refs_0_, bf16[16,2048]{1,0:T(8,128)(2,1)S(1)} %collective-permute-done.12.refs_1_, bf16[16,2048]{1,0:T(8,128)(2,1)S(1)} %collective-permute-done.13.refs_2_, ...), custom_call_target="tpu_custom_call" | custom-call | flops 1073741824 | bytes 16777216 | tf_op jit(solution)/shard_map/output/pallas_call | solution.py:275
  49.8 0.1 collective-permute-start.15
  49.8 1.5 %collective-permute-done.15.other_ref = bf16[32,4096]{1,0:T(8,128)(2,1)S(1)} collective-permute-done((bf16[32,4096]{1,0:T(8,128)(2,1)S(1)}, bf16[32,4096]{1,0:T(8,128)(2,1)S(1)}, u32[]{:S(2)}, u32[]{:S(2)}) %collective-permute-start.15) | collective-permute-done | bytes 262176 | tf_op jit(solution)/shard_map/sum_over_wide/ppermute | solution.py:43
  51.4 1.3 %collective-permute-start.16 = (bf16[16,4096]{1,0:T(8,128)(2,1)S(1)}, bf16[16,4096]{1,0:T(8,128)(2,1)S(1)}, u32[]{:S(2)}, u32[]{:S(2)}) collective-permute-start(bf16[16,4096]{1,0:T(8,128)(2,1)S(1)} %get-tuple-element.50), channel_id=1, source_target_pairs={{0,8},{4,12},{8,0},{12,4},{1,9},{5,13},{9,1},{13,5},{2,10},{6,14},... | collective-permute-start | bytes 393224 | tf_op jit(solution)/shard_map/sum_over_wide/ppermute | solution.py:43
  52.7 4.3 %collective-permute-done.16.refs_1_ = bf16[16,4096]{1,0:T(8,128)(2,1)S(1)} collective-permute-done((bf16[16,4096]{1,0:T(8,128)(2,1)S(1)}, bf16[16,4096]{1,0:T(8,128)(2,1)S(1)}, u32[]{:S(2)}, u32[]{:S(2)}) %collective-permute-start.16) | collective-permute-done | bytes 131104 | tf_op jit(solution)/shard_map/sum_over_wide/ppermute | solution.py:43
  57.0 0.7 %total.1 = bf16[16,4096]{1,0:T(8,128)(2,1)} custom-call(f32[16,4096]{1,0:T(8,128)S(1)} %get-tuple-element.49.refs_0_, bf16[16,4096]{1,0:T(8,128)(2,1)S(1)} %collective-permute-done.16.refs_1_), custom_call_target="tpu_custom_call" | custom-call | bytes 524288 | tf_op jit(solution)/shard_map/total/pallas_call | solution.py:275
  (5 shorter events, 0.1 us)
Async XLA Ops:
  0.0 7.2 %copy-start.3 = (bf16[4096]{0:T(1024)(128)(2,1)S(1)}, bf16[4096]{0:T(1024)(128)(2,1)}, u32[]{:S(2)}) copy-start(bf16[4096]{0:T(1024)(128)(2,1)} %param.9) | copy-start | bytes 24580
  0.0 8.2 %copy-start = (bf16[2,8,4096]{2,1,0:T(8,128)(2,1)S(1)}, bf16[2,8,4096]{2,1,0:T(8,128)(2,1)}, u32[]{:S(2)}) copy-start(bf16[2,8,4096]{2,1,0:T(8,128)(2,1)} %param.8) | copy-start | bytes 393220
  0.0 6.7 %collective-permute-start.1 = (bf16[16,4096]{1,0:T(8,128)(2,1)}, bf16[16,4096]{1,0:T(8,128)(2,1)S(1)}, u32[]{:S(2)}, u32[]{:S(2)}) collective-permute-start(bf16[16,4096]{1,0:T(8,128)(2,1)} %bitcast.2), channel_id=1, source_target_pairs={{0,8},{4,12},{8,0},{12,4},{1,9},{5,13},{9,1},{13,5},{2,10},{6,14},... | collective-permute-start | bytes 393224 | tf_op jit(solution)/shard_map/gather_tokens/ppermute | solution.py:43
  2.9 4.3 %collective-permute-start = (bf16[16,4096]{1,0:T(8,128)(2,1)}, bf16[16,4096]{1,0:T(8,128)(2,1)S(1)}, u32[]{:S(2)}, u32[]{:S(2)}) collective-permute-start(bf16[16,4096]{1,0:T(8,128)(2,1)} %bitcast.3), channel_id=1, source_target_pairs={{0,4},{4,0},{8,12},{12,8},{1,5},{5,1},{9,13},{13,9},{2,6},{6,2},{1... | collective-permute-start | bytes 393224 | tf_op jit(solution)/shard_map/gather_tokens/ppermute | solution.py:43
  6.7 1.5 %collective-permute-start.2 = (bf16[16,4096]{1,0:T(8,128)(2,1)S(1)}, bf16[16,4096]{1,0:T(8,128)(2,1)S(1)}, u32[]{:S(2)}, u32[]{:S(2)}) collective-permute-start(bf16[16,4096]{1,0:T(8,128)(2,1)S(1)} %collective-permute-done.1.refs_2_), channel_id=1, source_target_pairs={{0,4},{4,0},{8,12},{12,8},{1,5},{5,1},{9,13},{13,9},{2,6},{6,2},{1... | collective-permute-start | bytes 393224 | tf_op jit(solution)/shard_map/gather_tokens/ppermute | solution.py:43
  7.2 9.9 %copy-start.1 = (s32[2]{0:T(128)S(1)}, s32[2]{0:T(128)}, u32[]{:S(2)}) copy-start(s32[2]{0:T(128)} %refs_0_.6) | copy-start | bytes 28
  7.3 9.9 %copy-start.2 = (f32[1,128]{1,0:T(1,128)S(1)}, f32[1,128]{1,0:T(1,128)}, u32[]{:S(2)}) copy-start(f32[1,128]{1,0:T(1,128)} %constant.2.clone.refs_4_) | copy-start | bytes 1540
  12.7 10.9 %collective-permute-start.3 = (bf16[16,2432]{1,0:T(8,128)(2,1)S(1)}, bf16[16,2432]{1,0:T(8,128)(2,1)S(1)}, u32[]{:S(2)}, u32[]{:S(2)}) collective-permute-start(bf16[16,2432]{1,0:T(8,128)(2,1)S(1)} %get-tuple-element.31), channel_id=1, source_target_pairs={{0,1},{1,0},{2,3},{3,2},{4,5},{5,4},{6,7},{7,6},{8,9},{9,8},{10,11... | collective-permute-start | bytes 233480 | tf_op jit(solution)/shard_map/sum_over_narrow/ppermute | solution.py:43
  14.4 9.3 %collective-permute-start.4 = (bf16[16,2432]{1,0:T(8,128)(2,1)S(1)}, bf16[16,2432]{1,0:T(8,128)(2,1)S(1)}, u32[]{:S(2)}, u32[]{:S(2)}) collective-permute-start(bf16[16,2432]{1,0:T(8,128)(2,1)S(1)} %get-tuple-element.32), channel_id=1, source_target_pairs={{0,2},{1,3},{2,0},{3,1},{4,6},{5,7},{6,4},{7,5},{8,10},{9,11},{10,... | collective-permute-start | bytes 233480 | tf_op jit(solution)/shard_map/sum_over_narrow/ppermute | solution.py:43
  17.0 6.7 %collective-permute-start.5 = (bf16[16,2432]{1,0:T(8,128)(2,1)S(1)}, bf16[16,2432]{1,0:T(8,128)(2,1)S(1)}, u32[]{:S(2)}, u32[]{:S(2)}) collective-permute-start(bf16[16,2432]{1,0:T(8,128)(2,1)S(1)} %get-tuple-element.33), channel_id=1, source_target_pairs={{0,3},{1,2},{2,1},{3,0},{4,7},{5,6},{6,5},{7,4},{8,11},{9,10},{10,... | collective-permute-start | bytes 233480 | tf_op jit(solution)/shard_map/sum_over_narrow/ppermute | solution.py:43
  23.8 1.9 %collective-permute-start.6 = (bf16[4,2304]{1,0:T(4,128)(2,1)S(1)}, bf16[4,2304]{1,0:T(4,128)(2,1)S(1)}, u32[]{:S(2)}, u32[]{:S(2)}) collective-permute-start(bf16[4,2304]{1,0:T(4,128)(2,1)S(1)} %get-tuple-element.36), channel_id=1, source_target_pairs={{0,4},{4,0},{8,12},{12,8},{1,5},{5,1},{9,13},{13,9},{2,6},{6,2},{1... | collective-permute-start | bytes 55304 | tf_op jit(solution)/shard_map/columns_to_owner/ppermute | solution.py:43
  23.9 3.8 %collective-permute-start.7 = (bf16[4,2304]{1,0:T(4,128)(2,1)S(1)}, bf16[4,2304]{1,0:T(4,128)(2,1)S(1)}, u32[]{:S(2)}, u32[]{:S(2)}) collective-permute-start(bf16[4,2304]{1,0:T(4,128)(2,1)S(1)} %get-tuple-element.37), channel_id=1, source_target_pairs={{0,8},{4,12},{8,0},{12,4},{1,9},{5,13},{9,1},{13,5},{2,10},{6,14},... | collective-permute-start | bytes 55304 | tf_op jit(solution)/shard_map/columns_to_owner/ppermute | solution.py:43
  25.5 3.2 %collective-permute-start.8 = (bf16[4,2304]{1,0:T(4,128)(2,1)S(1)}, bf16[4,2304]{1,0:T(4,128)(2,1)S(1)}, u32[]{:S(2)}, u32[]{:S(2)}) collective-permute-start(bf16[4,2304]{1,0:T(4,128)(2,1)S(1)} %get-tuple-element.38), channel_id=1, source_target_pairs={{0,12},{4,8},{8,4},{12,0},{1,13},{5,9},{9,5},{13,1},{2,14},{6,10},... | collective-permute-start | bytes 55304 | tf_op jit(solution)/shard_map/columns_to_owner/ppermute | solution.py:43
  33.0 1.9 %collective-permute-start.9 = (bf16[4,2048]{1,0:T(4,128)(2,1)S(1)}, bf16[4,2048]{1,0:T(4,128)(2,1)S(1)}, u32[]{:S(2)}, u32[]{:S(2)}) collective-permute-start(bf16[4,2048]{1,0:T(4,128)(2,1)S(1)} %get-tuple-element.43), channel_id=1, source_target_pairs={{0,4},{4,0},{8,12},{12,8},{1,5},{5,1},{9,13},{13,9},{2,6},{6,2},{1... | collective-permute-start | bytes 49160 | tf_op jit(solution)/shard_map/heads_to_weights/ppermute | solution.py:43
  33.2 3.8 %collective-permute-start.10 = (bf16[4,2048]{1,0:T(4,128)(2,1)S(1)}, bf16[4,2048]{1,0:T(4,128)(2,1)S(1)}, u32[]{:S(2)}, u32[]{:S(2)}) collective-permute-start(bf16[4,2048]{1,0:T(4,128)(2,1)S(1)} %get-tuple-element.44), channel_id=1, source_target_pairs={{0,8},{4,12},{8,0},{12,4},{1,9},{5,13},{9,1},{13,5},{2,10},{6,14},... | collective-permute-start | bytes 49160 | tf_op jit(solution)/shard_map/heads_to_weights/ppermute | solution.py:43
  33.9 3.2 %collective-permute-start.11 = (bf16[4,2048]{1,0:T(4,128)(2,1)S(1)}, bf16[4,2048]{1,0:T(4,128)(2,1)S(1)}, u32[]{:S(2)}, u32[]{:S(2)}) collective-permute-start(bf16[4,2048]{1,0:T(4,128)(2,1)S(1)} %get-tuple-element.45), channel_id=1, source_target_pairs={{0,12},{4,8},{8,4},{12,0},{1,13},{5,9},{9,5},{13,1},{2,14},{6,10},... | collective-permute-start | bytes 49160 | tf_op jit(solution)/shard_map/heads_to_weights/ppermute | solution.py:43
  37.2 7.9 %collective-permute-start.14 = (bf16[16,2048]{1,0:T(8,128)(2,1)S(1)}, bf16[16,2048]{1,0:T(8,128)(2,1)S(1)}, u32[]{:S(2)}, u32[]{:S(2)}) collective-permute-start(bf16[16,2048]{1,0:T(8,128)(2,1)S(1)} %join.1.refs_1_.refs_0_), channel_id=1, source_target_pairs={{0,3},{1,2},{2,1},{3,0},{4,7},{5,6},{6,5},{7,4},{8,11},{9,10},{10,... | collective-permute-start | bytes 196616 | tf_op jit(solution)/shard_map/gather_over_narrow/ppermute | solution.py:43
  40.9 5.7 %collective-permute-start.13 = (bf16[16,2048]{1,0:T(8,128)(2,1)S(1)}, bf16[16,2048]{1,0:T(8,128)(2,1)S(1)}, u32[]{:S(2)}, u32[]{:S(2)}) collective-permute-start(bf16[16,2048]{1,0:T(8,128)(2,1)S(1)} %join.1.refs_1_.refs_0_), channel_id=1, source_target_pairs={{0,2},{1,3},{2,0},{3,1},{4,6},{5,7},{6,4},{7,5},{8,10},{9,11},{10,... | collective-permute-start | bytes 196616 | tf_op jit(solution)/shard_map/gather_over_narrow/ppermute | solution.py:43
  40.9 5.7 %collective-permute-start.12 = (bf16[16,2048]{1,0:T(8,128)(2,1)S(1)}, bf16[16,2048]{1,0:T(8,128)(2,1)S(1)}, u32[]{:S(2)}, u32[]{:S(2)}) collective-permute-start(bf16[16,2048]{1,0:T(8,128)(2,1)S(1)} %join.1.refs_1_.refs_0_), channel_id=1, source_target_pairs={{0,1},{1,0},{2,3},{3,2},{4,5},{5,4},{6,7},{7,6},{8,9},{9,8},{10,11... | collective-permute-start | bytes 196616 | tf_op jit(solution)/shard_map/gather_over_narrow/ppermute | solution.py:43
  49.8 1.6 %collective-permute-start.15 = (bf16[32,4096]{1,0:T(8,128)(2,1)S(1)}, bf16[32,4096]{1,0:T(8,128)(2,1)S(1)}, u32[]{:S(2)}, u32[]{:S(2)}) collective-permute-start(bf16[32,4096]{1,0:T(8,128)(2,1)S(1)} %get-tuple-element.48), channel_id=1, source_target_pairs={{0,4},{4,0},{8,12},{12,8},{1,5},{5,1},{9,13},{13,9},{2,6},{6,2},{1... | collective-permute-start | bytes 786440 | tf_op jit(solution)/shard_map/sum_over_wide/ppermute | solution.py:43
  51.4 5.6 %collective-permute-start.16 = (bf16[16,4096]{1,0:T(8,128)(2,1)S(1)}, bf16[16,4096]{1,0:T(8,128)(2,1)S(1)}, u32[]{:S(2)}, u32[]{:S(2)}) collective-permute-start(bf16[16,4096]{1,0:T(8,128)(2,1)S(1)} %get-tuple-element.50), channel_id=1, source_target_pairs={{0,8},{4,12},{8,0},{12,4},{1,9},{5,13},{9,1},{13,5},{2,10},{6,14},... | collective-permute-start | bytes 393224 | tf_op jit(solution)/shard_map/sum_over_wide/ppermute | solution.py:43

commit v3 on v2

--- a/solution.py
+++ b/solution.py
@@ -1,4 +1,5 @@
 import functools
+import math
 
 import jax
 import jax.numpy as jnp
@@ -50,7 +51,7 @@
 def fetch_kernel(spans, turns, *refs):
     count = len(spans)
     sources, sem = refs[:count], refs[-1]
-    outs = refs[len(refs) - 1 - count - 2 * bool(turns) : -1]
+    outs = refs[len(refs) - 1 - count - 3 * bool(turns) : -1]
     copies = []
     for i, (at, size) in enumerate(spans):
         copies.append(pltpu.make_async_copy(sources[i].at[pl.ds(at, size)], outs[i], sem.at[i]))
@@ -59,7 +60,7 @@
     if turns:
         steps, rows = turns
         lengths_ref, freqs_ref = refs[count : count + 2]
-        cos_ref, sin_ref = outs[-2:]
+        cos_ref, sin_ref, mask_ref = outs[-3:]
         for s in range(steps):
             for r in range(rows):
                 i = s * rows + r
@@ -67,6 +68,9 @@
                 lane = lax.broadcasted_iota(jnp.int32, angle.shape, 1)
                 cos_ref[i : i + 1] = jnp.cos(angle)
                 sin_ref[i : i + 1] = jnp.where(lane < angle.shape[1] // 2, -1.0, 1.0) * jnp.sin(angle)
+        slot = lax.broadcasted_iota(jnp.int32, (1, mask_ref.shape[1]), 1)
+        for r in range(rows):
+            mask_ref[r : r + 1] = jnp.where(slot < lengths_ref[r], 0.0, -jnp.inf)
     for copy in copies:
         copy.wait()
 
@@ -81,6 +85,7 @@
         turns = (steps, lengths.shape[0])
         extra, extra_specs = [lengths, freqs], [pl.BlockSpec(memory_space=pltpu.SMEM), whole()]
         outs += [jax.ShapeDtypeStruct((steps * lengths.shape[0], freqs.shape[1]), F32)] * 2
+        outs += [jax.ShapeDtypeStruct((lengths.shape[0], arrays[0].shape[2]), F32)]
     return pl.pallas_call(
         functools.partial(fetch_kernel, [(at, n) for _, at, n in spans], turns),
         out_shape=outs,
@@ -156,16 +161,15 @@
 
 
 def attend_kernel(wide, steps, slice_width, *refs):
-    lengths_ref, parts = refs[0], refs[1 : 1 + wide]
+    mask_ref, parts = refs[0], refs[1 : 1 + wide]
     cos_ref, sin_ref, key_ref, value_ref = refs[1 + wide : 5 + wide]
-    outs = refs[5 + wide : 5 + 2 * wide]
-    stack, proj, query, total = refs[5 + 2 * wide :]
+    outs, (stack, proj, query, total) = refs[-4 - wide : -4], refs[-4:]
     rows, kv_heads, slots, head_dim = key_ref.shape
     width = parts[0].shape[1]
     width_query = slice_width * wide
     heads = width_query // head_dim
     group = heads // kv_heads
-    scale = head_dim ** (-0.5)
+    scale = head_dim ** (-0.5) * math.log2(math.e)
     here = lax.axis_index("wide")
 
     for d in range(wide):
@@ -187,33 +191,43 @@
                 i = s * rows + r
                 at = s * group + h % group
                 query[h // group, r, at : at + 1, :] = q[i : i + 1]
-    lane = lax.broadcasted_iota(jnp.int32, (steps * group, slots), 1)
     step_of = lax.div(lax.broadcasted_iota(jnp.int32, (steps * group, 1), 0), group)
-    for k in range(kv_heads):
+
+    def compare(k):
+        return [
+            lax.dot_general(
+                query[k, r].astype(BF16), key_ref[r, k], (((1,), (1,)), ((), ())), preferred_element_type=F32
+            )
+            for r in range(rows)
+        ]
+
+    def weigh(k, scores):
         fresh_key = turned(width_query + k * head_dim)
-        at = width_query + (kv_heads + k) * head_dim
-        fresh_value = proj[:, at : at + head_dim]
+        made = []
         for r in range(rows):
-            q = query[k, r]
-            scores = lax.dot_general(
-                q.astype(BF16), key_ref[r, k], (((1,), (1,)), ((), ())), preferred_element_type=F32
-            ) * scale
-            scores = jnp.where(lane < lengths_ref[r], scores, -jnp.inf)
-            highest = jnp.max(scores, axis=1, keepdims=True)
+            cached = scores[r] + mask_ref[r : r + 1]
+            highest = jnp.max(cached, axis=1, keepdims=True)
             newest = []
             for j in range(steps):
                 i = j * rows + r
-                dot = jnp.sum(q * fresh_key[i : i + 1], axis=1, keepdims=True) * scale
-                dot = jnp.where(step_of >= j, dot, -jnp.inf)
-                newest.append(dot)
-                highest = jnp.maximum(highest, dot)
-            weights = jnp.exp(scores - highest)
+                dot = jnp.sum(query[k, r] * fresh_key[i : i + 1], axis=1, keepdims=True)
+                newest.append(jnp.where(step_of >= j, dot, -jnp.inf))
+                highest = jnp.maximum(highest, newest[-1])
+            weights = jnp.exp2((cached - highest) * scale)
             denominator = jnp.sum(weights, axis=1, keepdims=True)
-            out = jnp.dot(weights.astype(BF16), value_ref[r, k], preferred_element_type=F32)
-            for j in range(steps):
+            fresh = [jnp.exp2((dot - highest) * scale) for dot in newest]
+            for weight in fresh:
+                denominator = denominator + weight
+            made.append((weights.astype(BF16), fresh, denominator))
+        return made
+
+    def combine(k, made):
+        at = width_query + (kv_heads + k) * head_dim
+        fresh_value = proj[:, at : at + head_dim]
+        for r, (weights, fresh, denominator) in enumerate(made):
+            out = jnp.dot(weights, value_ref[r, k], preferred_element_type=F32)
+            for j, weight in enumerate(fresh):
                 i = j * rows + r
-                weight = jnp.exp(newest[j] - highest)
-                denominator = denominator + weight
                 out = out + weight.astype(BF16).astype(F32) * fresh_value[i : i + 1]
             out = out / denominator
             for s in range(steps):
@@ -222,6 +236,15 @@
                     w, col = at // slice_width, at % slice_width
                     i = s * rows + r
                     total[w, i : i + 1, col : col + head_dim] = out[s * group + g : s * group + g + 1]
+
+    scores, ready = compare(0), None
+    for k in range(kv_heads):
+        following = compare(k + 1) if k + 1 < kv_heads else None
+        made = weigh(k, scores)
+        if ready:
+            combine(*ready)
+        ready, scores = (k, made), following
+    combine(*ready)
     for d in range(wide):
         outs[d][...] = total[lax.bitwise_xor(here, d)].astype(BF16)
 
@@ -235,8 +258,11 @@
 
 
 def output_kernel(wide, narrow, steps, rows, *refs):
-    blocks, w_refs, (keep_ref, send_ref, ordered) = refs[:narrow], refs[narrow:-3], refs[-3:]
-    split = w_refs[0].shape[0]
+    blocks, (early_ref, late_ref, w_ref) = refs[:narrow], refs[narrow : narrow + 3]
+    keep_ref, send_ref, ordered, acc, last, sem = refs[narrow + 3 :]
+    ends = [early_ref.shape[0], early_ref.shape[0] + late_ref.shape[0], w_ref.shape[0]]
+    rest = pltpu.make_async_copy(w_ref.at[pl.ds(ends[1], ends[2] - ends[1])], last, sem)
+    rest.start()
     block, depth = blocks[0].shape
     tokens = block * narrow
     per = steps * rows
@@ -253,11 +279,18 @@
         x = jnp.concatenate([b[:, at : at + size] for b in blocks], axis=0)
         ordered[:, at : at + size] = jnp.dot(order, x, preferred_element_type=F32).astype(BF16)
     half = tokens // 2
-    for at, size in chunks(w_refs[0].shape[1], 512):
-        y = jnp.dot(ordered[:, :split], w_refs[0][:, at : at + size], preferred_element_type=F32)
-        y = y + jnp.dot(ordered[:, split:], w_refs[1][:, at : at + size], preferred_element_type=F32)
-        keep_ref[:, at : at + size] = y[:half]
-        send_ref[:, at : at + size] = y[half:].astype(BF16)
+    for i, (piece, begin, end) in enumerate(zip((early_ref, late_ref, last), [0] + ends, ends)):
+        if i == 2:
+            rest.wait()
+        for at, size in chunks(w_ref.shape[1], 512):
+            y = jnp.dot(ordered[:, begin:end], piece[:, at : at + size], preferred_element_type=F32)
+            if i:
+                y = y + acc[:, at : at + size]
+            if i < 2:
+                acc[:, at : at + size] = y
+                continue
+            keep_ref[:, at : at + size] = y[:half]
+            send_ref[:, at : at + size] = y[half:].astype(BF16)
 
 
 def pair_kernel(keep_ref, other_ref, *outs):
@@ -300,7 +333,7 @@
     half = np.arange(head_dim) % (head_dim // 2)
     freqs = np.asarray(rope_base ** (-2.0 * half / head_dim), np.float32)[None]
     qkv_split = depth // 2
-    out_split = slice_width // 2
+    early, late = slice_width // 4, slice_width // 2
 
     (qkv_near,) = fetch([(qkv_weight, 0, qkv_split)], [])
     with jax.named_scope("gather_tokens"):
@@ -325,13 +358,13 @@
         [whole()] * (wide + 2) + [pl.BlockSpec(memory_space=pltpu.HBM)],
         flops=2 * tokens * depth * width, size=2 * depth * width,
     )
-    keys, values, out_near, cosine, sine = fetch(
-        [(key_cache, 0, rows), (cache_of_values, 0, rows), (out_weight, 0, out_split)],
+    keys, values, cosine, sine, mask = fetch(
+        [(key_cache, 0, rows), (cache_of_values, 0, rows)],
         [partial[0]],
         (steps, lengths, jnp.asarray(freqs)),
     )
     with jax.named_scope("sum_over_narrow"):
-        parts = [swap(p, "narrow", e) if e else p for e, p in enumerate(partial)]
+        parts = [swap(partial[e], "narrow", e) if e else partial[e] for e in reversed(range(narrow))]
     normed = call(
         functools.partial(normalize_kernel, wide, narrow, depth * narrow), "normalize",
         [shape((per, width), BF16)] * wide,
@@ -339,19 +372,20 @@
         specs=[whole()] * narrow + [hbm()],
         size=4 * tokens * width,
     )
+    (out_early,) = fetch([(out_weight, 0, early)], [normed[0]])
     with jax.named_scope("columns_to_owner"):
         mine = [swap(p, "wide", d) if d else p for d, p in enumerate(normed)]
     attended = call(
         functools.partial(attend_kernel, wide, steps, slice_width), "attend",
         [shape((per, slice_width), BF16)] * wide,
-        [lengths] + mine + [cosine, sine, resident(keys), resident(values)],
+        [mask] + mine + [cosine, sine, resident(keys), resident(values), out_early],
         [
             pltpu.VMEM((wide, per, width), F32),
             pltpu.VMEM((per, width * wide), F32),
             pltpu.VMEM((kv_heads, rows, steps * heads // kv_heads, head_dim), F32),
             pltpu.VMEM((wide, per, slice_width), F32),
         ],
-        [pl.BlockSpec(memory_space=pltpu.SMEM)] + [whole()] * (wide + 4),
+        [whole()] * (wide + 5) + [hbm()],
         flops=4 * per * heads * slots * head_dim,
         size=4 * rows * kv_heads * slots * head_dim,
         exps=per * heads * slots,
@@ -362,14 +396,21 @@
         join_kernel, "join", shape((per * wide, slice_width), BF16), arrived,
         [pltpu.VMEM((per * wide, slice_width), F32)], size=4 * per * wide * slice_width,
     )
-    (out_far,) = fetch([(out_weight, out_split, slice_width - out_split)], [joined])
+    (out_late,) = fetch([(out_weight, early, late)], [joined])
     with jax.named_scope("gather_over_narrow"):
         spread = [swap(joined, "narrow", e) if e else joined for e in range(narrow)]
     keep, send = call(
         functools.partial(output_kernel, wide, narrow, steps, rows), "output",
         [shape((tokens // 2, out_width), F32), shape((tokens // 2, out_width), BF16)],
-        spread + [resident(out_near), resident(out_far)],
-        [pltpu.VMEM((tokens, slice_width), BF16)],
+        spread
+        + [resident(out_early), resident(out_late), pltpu.with_memory_space_constraint(out_weight, pltpu.HBM)],
+        [
+            pltpu.VMEM((tokens, slice_width), BF16),
+            pltpu.VMEM((tokens, out_width), F32),
+            pltpu.VMEM((slice_width - early - late, out_width), BF16),
+            pltpu.SemaphoreType.DMA,
+        ],
+        [whole()] * (narrow + 2) + [pl.BlockSpec(memory_space=pltpu.HBM)],
         flops=2 * tokens * slice_width * out_width, size=2 * slice_width * out_width,
     )
     with jax.named_scope("sum_over_wide"):

time: 57.9 us -> 55.5 us (0.959)
  Pallas kernels: 26.4 us -> 24.3 us
    pallas_call x7, Pallas kernels: 12.9 us -> 11 us  [call(): pl.pallas_call(kernel, out_shape=outs, in_specs=specs or [whole()] * len(...]
    pallas_call x3 -> x4, Pallas kernels: 13.5 us -> 13.3 us  [fetch(): pl.pallas_call(functools.partial(fetch_kernel, [(at, n) for _, at, n in s...]
  transfers between devices with their start and end apart: 17 -> 17, of which waited for: 8 -> 8; matrix products, arithmetic and copies ran while one was open for 0% -> 0% of each run, Pallas kernels for 23% -> 24%
where the time goes in v3:
time: 55.5 us; the launch traced here: 55.3 us
  Pallas kernels  24.3 us (44%)
  starting transfers between devices  17.3 us (31%)
  waiting for transfers between devices  13.5 us (24%)
    ppermute x17, starting transfers between devices, swap(): return lax.ppermute(array, axis, [(i, i ^ distance) for i in range(size)])  17.3 us
    ppermute x17, waiting for transfers between devices, swap(): return lax.ppermute(array, axis, [(i, i ^ distance) for i in range(size)])  13.5 us
    pallas_call x4, Pallas kernels, fetch(): pl.pallas_call(functools.partial(fetch_kernel, [(at, n) for _, at, n in s...  13.3 us
    pallas_call x7, Pallas kernels, call(): pl.pallas_call(kernel, out_shape=outs, in_specs=specs or [whole()] * len(...  11 us
  transfers between devices with their start and end apart: 17, of which 8 were waited for; matrix products, arithmetic and copies ran while one was open for 0% of the time, Pallas kernels for 24%

profile of v3, /device:TPU:0, one launch (start us, length us, event | category | flops | bytes accessed | tf_op | source)
XLA Modules:
  0.0 55.3 jit_solution(17072001355366389331)
XLA Ops:
  0.0 2.9 %collective-permute-start.1 = (bf16[16,4096]{1,0:T(8,128)(2,1)}, bf16[16,4096]{1,0:T(8,128)(2,1)S(1)}, u32[]{:S(2)}, u32[]{:S(2)}) collective-permute-start(bf16[16,4096]{1,0:T(8,128)(2,1)} %bitcast.2), channel_id=1, source_target_pairs={{0,8},{4,12},{8,0},{12,4},{1,9},{5,13},{9,1},{13,5},{2,10},{6,14},... | collective-permute-start | bytes 393224 | tf_op jit(solution)/shard_map/gather_tokens/ppermute | solution.py:44
  2.9 0.0 collective-permute-start
  2.9 3.7 %fetch.4.refs_5_ = bf16[2048,2304]{1,0:T(8,128)(2,1)S(1)} custom-call(bf16[4096,2304]{1,0:T(8,128)(2,1)} %refs_6_.2), custom_call_target="tpu_custom_call" | custom-call | bytes 18874368 | tf_op jit(solution)/shard_map/fetch/pallas_call | solution.py:89
  6.6 0.0 collective-permute-done.1.refs_2_
  6.7 0.5 collective-permute-start.2
  7.2 0.0 copy-done.3
  7.2 0.0 copy-start.1
  7.3 0.0 copy-start.2
  7.3 0.0 collective-permute-done.refs_1_
  7.3 0.9 %collective-permute-done.2.refs_3_ = bf16[16,4096]{1,0:T(8,128)(2,1)S(1)} collective-permute-done((bf16[16,4096]{1,0:T(8,128)(2,1)S(1)}, bf16[16,4096]{1,0:T(8,128)(2,1)S(1)}, u32[]{:S(2)}, u32[]{:S(2)}) %collective-permute-start.2) | collective-permute-done | bytes 131104 | tf_op jit(solution)/shard_map/gather_tokens/ppermute | solution.py:44
  8.2 0.0 copy-done
  8.2 4.5 %project.1 = (bf16[16,2432]{1,0:T(8,128)(2,1)S(1)}, bf16[16,2432]{1,0:T(8,128)(2,1)S(1)}, bf16[16,2432]{1,0:T(8,128)(2,1)S(1)}, bf16[16,2432]{1,0:T(8,128)(2,1)S(1)}) custom-call(bf16[16,4096]{1,0:T(8,128)(2,1)S(1)} %bitcast.4, bf16[16,4096]{1,0:T(8,128)(2,1)S(1)} %collective-permute-done.refs_1_, bf16[16,4096]{1,0:T(8,128)(2,1)S(1)} %collective-permute-done.1.refs_2_, ...), custom_call_target="tpu_custom_call" | custom-call | flops 1207959552 | bytes 18874368 | tf_op jit(solution)/shard_map/project/pallas_call | solution.py:308
  12.7 3.7 %collective-permute-start.3 = (bf16[16,2432]{1,0:T(8,128)(2,1)S(1)}, bf16[16,2432]{1,0:T(8,128)(2,1)S(1)}, u32[]{:S(2)}, u32[]{:S(2)}) collective-permute-start(bf16[16,2432]{1,0:T(8,128)(2,1)S(1)} %get-tuple-element.32), channel_id=1, source_target_pairs={{0,3},{1,2},{2,1},{3,0},{4,7},{5,6},{6,5},{7,4},{8,11},{9,10},{10,... | collective-permute-start | bytes 233480 | tf_op jit(solution)/shard_map/sum_over_narrow/ppermute | solution.py:44
  16.4 0.0 collective-permute-start.4
  16.4 0.8 %collective-permute-start.5 = (bf16[16,2432]{1,0:T(8,128)(2,1)S(1)}, bf16[16,2432]{1,0:T(8,128)(2,1)S(1)}, u32[]{:S(2)}, u32[]{:S(2)}) collective-permute-start(bf16[16,2432]{1,0:T(8,128)(2,1)S(1)} %get-tuple-element.34), channel_id=1, source_target_pairs={{0,1},{1,0},{2,3},{3,2},{4,5},{5,4},{6,7},{7,6},{8,9},{9,8},{10,11... | collective-permute-start | bytes 233480 | tf_op jit(solution)/shard_map/sum_over_narrow/ppermute | solution.py:44
  17.2 0.0 copy-done.1
  17.2 4.0 %fetch.5 = (bf16[2,4,2048,128]{3,2,1,0:T(8,128)(2,1)S(1)}, bf16[2,4,2048,128]{3,2,1,0:T(8,128)(2,1)S(1)}, f32[4,128]{1,0:T(4,128)S(1)}, f32[4,128]{1,0:T(4,128)S(1)}, f32[2,2048]{1,0:T(2,128)S(1)}) custom-call(bf16[2,4,2048,128]{3,2,1,0:T(8,128)(2,1)} %refs_0_.5, bf16[2,4,2048,128]{3,2,1,0:T(8,128)(2,1)} %refs_1_.1, s32[2]{0:T(128)S(1)} %copy-done.1, ...), custom_call_target="tpu_custom_call" | custom-call | bytes 16777216 | tf_op jit(solution)/shard_map/fetch/pallas_call | solution.py:89
  21.2 0.0 collective-permute-done.3.refs_0_
  21.2 2.2 %collective-permute-done.4.refs_1_ = bf16[16,2432]{1,0:T(8,128)(2,1)S(1)} collective-permute-done((bf16[16,2432]{1,0:T(8,128)(2,1)S(1)}, bf16[16,2432]{1,0:T(8,128)(2,1)S(1)}, u32[]{:S(2)}, u32[]{:S(2)}) %collective-permute-start.4) | collective-permute-done | bytes 77856 | tf_op jit(solution)/shard_map/sum_over_narrow/ppermute | solution.py:44
  23.4 0.0 collective-permute-done.5.refs_2_
  23.4 0.2 normalize.1
  23.6 0.1 collective-permute-start.6
  23.7 1.4 %collective-permute-start.7 = (bf16[4,2304]{1,0:T(4,128)(2,1)S(1)}, bf16[4,2304]{1,0:T(4,128)(2,1)S(1)}, u32[]{:S(2)}, u32[]{:S(2)}) collective-permute-start(bf16[4,2304]{1,0:T(4,128)(2,1)S(1)} %get-tuple-element.38), channel_id=1, source_target_pairs={{0,8},{4,12},{8,0},{12,4},{1,9},{5,13},{9,1},{13,5},{2,10},{6,14},... | collective-permute-start | bytes 55304 | tf_op jit(solution)/shard_map/columns_to_owner/ppermute | solution.py:44
  25.0 0.5 collective-permute-start.8
  25.5 2.2 %fetch.6.refs_9_.refs_4_ = bf16[512,4096]{1,0:T(8,128)(2,1)S(1)} custom-call(bf16[2048,4096]{1,0:T(8,128)(2,1)} %refs_6_.3, bf16[4,2304]{1,0:T(4,128)(2,1)S(1)} %get-tuple-element.36.refs_1_), custom_call_target="tpu_custom_call" | custom-call | bytes 8388608 | tf_op jit(solution)/shard_map/fetch/pallas_call | solution.py:89
  27.7 0.0 collective-permute-done.6.refs_2_
  27.7 0.0 collective-permute-done.7.refs_3_
  27.7 0.5 collective-permute-done.8.refs_4_
  28.2 2.4 %attend.1 = (bf16[4,2048]{1,0:T(4,128)(2,1)S(1)}, bf16[4,2048]{1,0:T(4,128)(2,1)S(1)}, bf16[4,2048]{1,0:T(4,128)(2,1)S(1)}, bf16[4,2048]{1,0:T(4,128)(2,1)S(1)}) custom-call(f32[2,2048]{1,0:T(2,128)S(1)} %get-tuple-element.31.refs_0_, bf16[4,2304]{1,0:T(4,128)(2,1)S(1)} %get-tuple-element.36.refs_1_, bf16[4,2304]{1,0:T(4,128)(2,1)S(1)} %collective-permute-done.6.refs_2_, ...), custom_call_target="tpu_custom_call" | custom-call | flops 268435456 | bytes 8388608 | tf_op jit(solution)/shard_map/attend/pallas_call | solution.py:308
  30.6 0.2 collective-permute-start.9
  30.9 1.0 %collective-permute-start.10 = (bf16[4,2048]{1,0:T(4,128)(2,1)S(1)}, bf16[4,2048]{1,0:T(4,128)(2,1)S(1)}, u32[]{:S(2)}, u32[]{:S(2)}) collective-permute-start(bf16[4,2048]{1,0:T(4,128)(2,1)S(1)} %get-tuple-element.45), channel_id=1, source_target_pairs={{0,8},{4,12},{8,0},{12,4},{1,9},{5,13},{9,1},{13,5},{2,10},{6,14},... | collective-permute-start | bytes 49160 | tf_op jit(solution)/shard_map/heads_to_weights/ppermute | solution.py:44
  31.9 0.7 %collective-permute-start.11 = (bf16[4,2048]{1,0:T(4,128)(2,1)S(1)}, bf16[4,2048]{1,0:T(4,128)(2,1)S(1)}, u32[]{:S(2)}, u32[]{:S(2)}) collective-permute-start(bf16[4,2048]{1,0:T(4,128)(2,1)S(1)} %get-tuple-element.46), channel_id=1, source_target_pairs={{0,12},{4,8},{8,4},{12,0},{1,13},{5,9},{9,5},{13,1},{2,14},{6,10},... | collective-permute-start | bytes 49160 | tf_op jit(solution)/shard_map/heads_to_weights/ppermute | solution.py:44
  32.6 0.0 collective-permute-done.9.refs_1_
  32.6 2.0 %collective-permute-done.10.refs_2_ = bf16[4,2048]{1,0:T(4,128)(2,1)S(1)} collective-permute-done((bf16[4,2048]{1,0:T(4,128)(2,1)S(1)}, bf16[4,2048]{1,0:T(4,128)(2,1)S(1)}, u32[]{:S(2)}, u32[]{:S(2)}) %collective-permute-start.10) | collective-permute-done | bytes 16416 | tf_op jit(solution)/shard_map/heads_to_weights/ppermute | solution.py:44
  34.6 0.6 %collective-permute-done.11.refs_3_ = bf16[4,2048]{1,0:T(4,128)(2,1)S(1)} collective-permute-done((bf16[4,2048]{1,0:T(4,128)(2,1)S(1)}, bf16[4,2048]{1,0:T(4,128)(2,1)S(1)}, u32[]{:S(2)}, u32[]{:S(2)}) %collective-permute-start.11) | collective-permute-done | bytes 16416 | tf_op jit(solution)/shard_map/heads_to_weights/ppermute | solution.py:44
  35.2 2.6 %collective-permute-start.14 = (bf16[16,2048]{1,0:T(8,128)(2,1)S(1)}, bf16[16,2048]{1,0:T(8,128)(2,1)S(1)}, u32[]{:S(2)}, u32[]{:S(2)}) collective-permute-start(bf16[16,2048]{1,0:T(8,128)(2,1)S(1)} %join.1.refs_1_.refs_0_), channel_id=1, source_target_pairs={{0,3},{1,2},{2,1},{3,0},{4,7},{5,6},{6,5},{7,4},{8,11},{9,10},{10,... | collective-permute-start | bytes 196616 | tf_op jit(solution)/shard_map/gather_over_narrow/ppermute | solution.py:44
  37.8 0.0 collective-permute-start.13
  37.8 1.9 %collective-permute-start.12 = (bf16[16,2048]{1,0:T(8,128)(2,1)S(1)}, bf16[16,2048]{1,0:T(8,128)(2,1)S(1)}, u32[]{:S(2)}, u32[]{:S(2)}) collective-permute-start(bf16[16,2048]{1,0:T(8,128)(2,1)S(1)} %join.1.refs_1_.refs_0_), channel_id=1, source_target_pairs={{0,1},{1,0},{2,3},{3,2},{4,5},{5,4},{6,7},{7,6},{8,9},{9,8},{10,11... | collective-permute-start | bytes 196616 | tf_op jit(solution)/shard_map/gather_over_narrow/ppermute | solution.py:44
  39.7 3.4 %fetch.7.refs_5_ = bf16[1024,4096]{1,0:T(8,128)(2,1)S(1)} custom-call(bf16[2048,4096]{1,0:T(8,128)(2,1)} %refs_6_.3, bf16[16,2048]{1,0:T(8,128)(2,1)S(1)} %join.1.refs_1_.refs_0_), custom_call_target="tpu_custom_call" | custom-call | bytes 16777216 | tf_op jit(solution)/shard_map/fetch/pallas_call | solution.py:89
  43.1 0.0 collective-permute-done.14.refs_3_
  43.1 1.1 %collective-permute-done.13.refs_2_ = bf16[16,2048]{1,0:T(8,128)(2,1)S(1)} collective-permute-done((bf16[16,2048]{1,0:T(8,128)(2,1)S(1)}, bf16[16,2048]{1,0:T(8,128)(2,1)S(1)}, u32[]{:S(2)}, u32[]{:S(2)}) %collective-permute-start.13) | collective-permute-done | bytes 65568 | tf_op jit(solution)/shard_map/gather_over_narrow/ppermute | solution.py:44
  44.2 0.0 collective-permute-done.12.refs_1_
  44.2 3.2 %output.1 = (f32[32,4096]{1,0:T(8,128)S(1)}, bf16[32,4096]{1,0:T(8,128)(2,1)S(1)}) custom-call(bf16[16,2048]{1,0:T(8,128)(2,1)S(1)} %join.1.refs_1_.refs_0_, bf16[16,2048]{1,0:T(8,128)(2,1)S(1)} %collective-permute-done.12.refs_1_, bf16[16,2048]{1,0:T(8,128)(2,1)S(1)} %collective-permute-done.13.refs_2_, ...), custom_call_target="tpu_custom_call" | custom-call | flops 1073741824 | bytes 16777216 | tf_op jit(solution)/shard_map/output/pallas_call | solution.py:308
  47.4 0.2 collective-permute-start.15
  47.5 1.4 %collective-permute-done.15.other_ref = bf16[32,4096]{1,0:T(8,128)(2,1)S(1)} collective-permute-done((bf16[32,4096]{1,0:T(8,128)(2,1)S(1)}, bf16[32,4096]{1,0:T(8,128)(2,1)S(1)}, u32[]{:S(2)}, u32[]{:S(2)}) %collective-permute-start.15) | collective-permute-done | bytes 262176 | tf_op jit(solution)/shard_map/sum_over_wide/ppermute | solution.py:44
  49.0 0.9 %collective-permute-start.16 = (bf16[16,4096]{1,0:T(8,128)(2,1)S(1)}, bf16[16,4096]{1,0:T(8,128)(2,1)S(1)}, u32[]{:S(2)}, u32[]{:S(2)}) collective-permute-start(bf16[16,4096]{1,0:T(8,128)(2,1)S(1)} %get-tuple-element.50), channel_id=1, source_target_pairs={{0,8},{4,12},{8,0},{12,4},{1,9},{5,13},{9,1},{13,5},{2,10},{6,14},... | collective-permute-start | bytes 393224 | tf_op jit(solution)/shard_map/sum_over_wide/ppermute | solution.py:44
  49.9 4.7 %collective-permute-done.16.refs_1_ = bf16[16,4096]{1,0:T(8,128)(2,1)S(1)} collective-permute-done((bf16[16,4096]{1,0:T(8,128)(2,1)S(1)}, bf16[16,4096]{1,0:T(8,128)(2,1)S(1)}, u32[]{:S(2)}, u32[]{:S(2)}) %collective-permute-start.16) | collective-permute-done | bytes 131104 | tf_op jit(solution)/shard_map/sum_over_wide/ppermute | solution.py:44
  54.6 0.7 %total.1 = bf16[16,4096]{1,0:T(8,128)(2,1)} custom-call(f32[16,4096]{1,0:T(8,128)S(1)} %get-tuple-element.49.refs_0_, bf16[16,4096]{1,0:T(8,128)(2,1)S(1)} %collective-permute-done.16.refs_1_), custom_call_target="tpu_custom_call" | custom-call | bytes 524288 | tf_op jit(solution)/shard_map/total/pallas_call | solution.py:308
  (6 shorter events, 0.1 us)
Async XLA Ops:
  0.0 7.2 %copy-start.3 = (bf16[4096]{0:T(1024)(128)(2,1)S(1)}, bf16[4096]{0:T(1024)(128)(2,1)}, u32[]{:S(2)}) copy-start(bf16[4096]{0:T(1024)(128)(2,1)} %param.9) | copy-start | bytes 24580
  0.0 8.2 %copy-start = (bf16[2,8,4096]{2,1,0:T(8,128)(2,1)S(1)}, bf16[2,8,4096]{2,1,0:T(8,128)(2,1)}, u32[]{:S(2)}) copy-start(bf16[2,8,4096]{2,1,0:T(8,128)(2,1)} %param.8) | copy-start | bytes 393220
  0.0 6.7 %collective-permute-start.1 = (bf16[16,4096]{1,0:T(8,128)(2,1)}, bf16[16,4096]{1,0:T(8,128)(2,1)S(1)}, u32[]{:S(2)}, u32[]{:S(2)}) collective-permute-start(bf16[16,4096]{1,0:T(8,128)(2,1)} %bitcast.2), channel_id=1, source_target_pairs={{0,8},{4,12},{8,0},{12,4},{1,9},{5,13},{9,1},{13,5},{2,10},{6,14},... | collective-permute-start | bytes 393224 | tf_op jit(solution)/shard_map/gather_tokens/ppermute | solution.py:44
  2.9 4.3 %collective-permute-start = (bf16[16,4096]{1,0:T(8,128)(2,1)}, bf16[16,4096]{1,0:T(8,128)(2,1)S(1)}, u32[]{:S(2)}, u32[]{:S(2)}) collective-permute-start(bf16[16,4096]{1,0:T(8,128)(2,1)} %bitcast.3), channel_id=1, source_target_pairs={{0,4},{4,0},{8,12},{12,8},{1,5},{5,1},{9,13},{13,9},{2,6},{6,2},{1... | collective-permute-start | bytes 393224 | tf_op jit(solution)/shard_map/gather_tokens/ppermute | solution.py:44
  6.7 1.5 %collective-permute-start.2 = (bf16[16,4096]{1,0:T(8,128)(2,1)S(1)}, bf16[16,4096]{1,0:T(8,128)(2,1)S(1)}, u32[]{:S(2)}, u32[]{:S(2)}) collective-permute-start(bf16[16,4096]{1,0:T(8,128)(2,1)S(1)} %collective-permute-done.1.refs_2_), channel_id=1, source_target_pairs={{0,4},{4,0},{8,12},{12,8},{1,5},{5,1},{9,13},{13,9},{2,6},{6,2},{1... | collective-permute-start | bytes 393224 | tf_op jit(solution)/shard_map/gather_tokens/ppermute | solution.py:44
  7.2 9.9 %copy-start.1 = (s32[2]{0:T(128)S(1)}, s32[2]{0:T(128)}, u32[]{:S(2)}) copy-start(s32[2]{0:T(128)} %refs_2_.1) | copy-start | bytes 28
  7.3 9.9 %copy-start.2 = (f32[1,128]{1,0:T(1,128)S(1)}, f32[1,128]{1,0:T(1,128)}, u32[]{:S(2)}) copy-start(f32[1,128]{1,0:T(1,128)} %constant.2.clone.refs_3_) | copy-start | bytes 1540
  12.7 8.5 %collective-permute-start.3 = (bf16[16,2432]{1,0:T(8,128)(2,1)S(1)}, bf16[16,2432]{1,0:T(8,128)(2,1)S(1)}, u32[]{:S(2)}, u32[]{:S(2)}) collective-permute-start(bf16[16,2432]{1,0:T(8,128)(2,1)S(1)} %get-tuple-element.32), channel_id=1, source_target_pairs={{0,3},{1,2},{2,1},{3,0},{4,7},{5,6},{6,5},{7,4},{8,11},{9,10},{10,... | collective-permute-start | bytes 233480 | tf_op jit(solution)/shard_map/sum_over_narrow/ppermute | solution.py:44
  16.4 7.0 %collective-permute-start.4 = (bf16[16,2432]{1,0:T(8,128)(2,1)S(1)}, bf16[16,2432]{1,0:T(8,128)(2,1)S(1)}, u32[]{:S(2)}, u32[]{:S(2)}) collective-permute-start(bf16[16,2432]{1,0:T(8,128)(2,1)S(1)} %get-tuple-element.33), channel_id=1, source_target_pairs={{0,2},{1,3},{2,0},{3,1},{4,6},{5,7},{6,4},{7,5},{8,10},{9,11},{10,... | collective-permute-start | bytes 233480 | tf_op jit(solution)/shard_map/sum_over_narrow/ppermute | solution.py:44
  16.4 7.0 %collective-permute-start.5 = (bf16[16,2432]{1,0:T(8,128)(2,1)S(1)}, bf16[16,2432]{1,0:T(8,128)(2,1)S(1)}, u32[]{:S(2)}, u32[]{:S(2)}) collective-permute-start(bf16[16,2432]{1,0:T(8,128)(2,1)S(1)} %get-tuple-element.34), channel_id=1, source_target_pairs={{0,1},{1,0},{2,3},{3,2},{4,5},{5,4},{6,7},{7,6},{8,9},{9,8},{10,11... | collective-permute-start | bytes 233480 | tf_op jit(solution)/shard_map/sum_over_narrow/ppermute | solution.py:44
  23.6 4.1 %collective-permute-start.6 = (bf16[4,2304]{1,0:T(4,128)(2,1)S(1)}, bf16[4,2304]{1,0:T(4,128)(2,1)S(1)}, u32[]{:S(2)}, u32[]{:S(2)}) collective-permute-start(bf16[4,2304]{1,0:T(4,128)(2,1)S(1)} %get-tuple-element.37), channel_id=1, source_target_pairs={{0,4},{4,0},{8,12},{12,8},{1,5},{5,1},{9,13},{13,9},{2,6},{6,2},{1... | collective-permute-start | bytes 55304 | tf_op jit(solution)/shard_map/columns_to_owner/ppermute | solution.py:44
  23.7 4.1 %collective-permute-start.7 = (bf16[4,2304]{1,0:T(4,128)(2,1)S(1)}, bf16[4,2304]{1,0:T(4,128)(2,1)S(1)}, u32[]{:S(2)}, u32[]{:S(2)}) collective-permute-start(bf16[4,2304]{1,0:T(4,128)(2,1)S(1)} %get-tuple-element.38), channel_id=1, source_target_pairs={{0,8},{4,12},{8,0},{12,4},{1,9},{5,13},{9,1},{13,5},{2,10},{6,14},... | collective-permute-start | bytes 55304 | tf_op jit(solution)/shard_map/columns_to_owner/ppermute | solution.py:44
  25.0 3.2 %collective-permute-start.8 = (bf16[4,2304]{1,0:T(4,128)(2,1)S(1)}, bf16[4,2304]{1,0:T(4,128)(2,1)S(1)}, u32[]{:S(2)}, u32[]{:S(2)}) collective-permute-start(bf16[4,2304]{1,0:T(4,128)(2,1)S(1)} %get-tuple-element.39), channel_id=1, source_target_pairs={{0,12},{4,8},{8,4},{12,0},{1,13},{5,9},{9,5},{13,1},{2,14},{6,10},... | collective-permute-start | bytes 55304 | tf_op jit(solution)/shard_map/columns_to_owner/ppermute | solution.py:44
  30.6 1.9 %collective-permute-start.9 = (bf16[4,2048]{1,0:T(4,128)(2,1)S(1)}, bf16[4,2048]{1,0:T(4,128)(2,1)S(1)}, u32[]{:S(2)}, u32[]{:S(2)}) collective-permute-start(bf16[4,2048]{1,0:T(4,128)(2,1)S(1)} %get-tuple-element.44), channel_id=1, source_target_pairs={{0,4},{4,0},{8,12},{12,8},{1,5},{5,1},{9,13},{13,9},{2,6},{6,2},{1... | collective-permute-start | bytes 49160 | tf_op jit(solution)/shard_map/heads_to_weights/ppermute | solution.py:44
  30.9 3.7 %collective-permute-start.10 = (bf16[4,2048]{1,0:T(4,128)(2,1)S(1)}, bf16[4,2048]{1,0:T(4,128)(2,1)S(1)}, u32[]{:S(2)}, u32[]{:S(2)}) collective-permute-start(bf16[4,2048]{1,0:T(4,128)(2,1)S(1)} %get-tuple-element.45), channel_id=1, source_target_pairs={{0,8},{4,12},{8,0},{12,4},{1,9},{5,13},{9,1},{13,5},{2,10},{6,14},... | collective-permute-start | bytes 49160 | tf_op jit(solution)/shard_map/heads_to_weights/ppermute | solution.py:44
  31.9 3.3 %collective-permute-start.11 = (bf16[4,2048]{1,0:T(4,128)(2,1)S(1)}, bf16[4,2048]{1,0:T(4,128)(2,1)S(1)}, u32[]{:S(2)}, u32[]{:S(2)}) collective-permute-start(bf16[4,2048]{1,0:T(4,128)(2,1)S(1)} %get-tuple-element.46), channel_id=1, source_target_pairs={{0,12},{4,8},{8,4},{12,0},{1,13},{5,9},{9,5},{13,1},{2,14},{6,10},... | collective-permute-start | bytes 49160 | tf_op jit(solution)/shard_map/heads_to_weights/ppermute | solution.py:44
  35.2 7.9 %collective-permute-start.14 = (bf16[16,2048]{1,0:T(8,128)(2,1)S(1)}, bf16[16,2048]{1,0:T(8,128)(2,1)S(1)}, u32[]{:S(2)}, u32[]{:S(2)}) collective-permute-start(bf16[16,2048]{1,0:T(8,128)(2,1)S(1)} %join.1.refs_1_.refs_0_), channel_id=1, source_target_pairs={{0,3},{1,2},{2,1},{3,0},{4,7},{5,6},{6,5},{7,4},{8,11},{9,10},{10,... | collective-permute-start | bytes 196616 | tf_op jit(solution)/shard_map/gather_over_narrow/ppermute | solution.py:44
  37.8 6.4 %collective-permute-start.13 = (bf16[16,2048]{1,0:T(8,128)(2,1)S(1)}, bf16[16,2048]{1,0:T(8,128)(2,1)S(1)}, u32[]{:S(2)}, u32[]{:S(2)}) collective-permute-start(bf16[16,2048]{1,0:T(8,128)(2,1)S(1)} %join.1.refs_1_.refs_0_), channel_id=1, source_target_pairs={{0,2},{1,3},{2,0},{3,1},{4,6},{5,7},{6,4},{7,5},{8,10},{9,11},{10,... | collective-permute-start | bytes 196616 | tf_op jit(solution)/shard_map/gather_over_narrow/ppermute | solution.py:44
  37.8 6.4 %collective-permute-start.12 = (bf16[16,2048]{1,0:T(8,128)(2,1)S(1)}, bf16[16,2048]{1,0:T(8,128)(2,1)S(1)}, u32[]{:S(2)}, u32[]{:S(2)}) collective-permute-start(bf16[16,2048]{1,0:T(8,128)(2,1)S(1)} %join.1.refs_1_.refs_0_), channel_id=1, source_target_pairs={{0,1},{1,0},{2,3},{3,2},{4,5},{5,4},{6,7},{7,6},{8,9},{9,8},{10,11... | collective-permute-start | bytes 196616 | tf_op jit(solution)/shard_map/gather_over_narrow/ppermute | solution.py:44
  47.4 1.6 %collective-permute-start.15 = (bf16[32,4096]{1,0:T(8,128)(2,1)S(1)}, bf16[32,4096]{1,0:T(8,128)(2,1)S(1)}, u32[]{:S(2)}, u32[]{:S(2)}) collective-permute-start(bf16[32,4096]{1,0:T(8,128)(2,1)S(1)} %get-tuple-element.48), channel_id=1, source_target_pairs={{0,4},{4,0},{8,12},{12,8},{1,5},{5,1},{9,13},{13,9},{2,6},{6,2},{1... | collective-permute-start | bytes 786440 | tf_op jit(solution)/shard_map/sum_over_wide/ppermute | solution.py:44
  49.0 5.6 %collective-permute-start.16 = (bf16[16,4096]{1,0:T(8,128)(2,1)S(1)}, bf16[16,4096]{1,0:T(8,128)(2,1)S(1)}, u32[]{:S(2)}, u32[]{:S(2)}) collective-permute-start(bf16[16,4096]{1,0:T(8,128)(2,1)S(1)} %get-tuple-element.50), channel_id=1, source_target_pairs={{0,8},{4,12},{8,0},{12,4},{1,9},{5,13},{9,1},{13,5},{2,10},{6,14},... | collective-permute-start | bytes 393224 | tf_op jit(solution)/shard_map/sum_over_wide/ppermute | solution.py:44

commit v4 on v3

--- a/solution.py
+++ b/solution.py
@@ -160,32 +160,46 @@
         outs[d][...] = total[d * per : (d + 1) * per].astype(BF16)
 
 
-def attend_kernel(wide, steps, slice_width, *refs):
-    mask_ref, parts = refs[0], refs[1 : 1 + wide]
-    cos_ref, sin_ref, key_ref, value_ref = refs[1 + wide : 5 + wide]
-    outs, (stack, proj, query, total) = refs[-4 - wide : -4], refs[-4:]
+def assemble(parts, proj, stack):
+    wide, width = len(parts), parts[0].shape[1]
+    here = lax.axis_index("wide")
+    for d in range(wide):
+        stack[d] = parts[d][...].astype(F32)
+    for w in range(wide):
+        proj[:, w * width : (w + 1) * width] = stack[lax.bitwise_xor(here, w)]
+
+
+def attend_kernel(wide, steps, slice_width, far, *refs):
+    count = wide if far else 1
+    parts, (mask_ref, cos_ref, sin_ref, key_ref, value_ref) = refs[:count], refs[count : count + 5]
+    near = wide // 2
+    if far:
+        outs, (proj, stack, query, total) = refs[-4 - near : -4], refs[-4:]
+        assemble(parts, proj, stack)
+    else:
+        outs, proj, (query, total) = refs[-2 - near : -2], parts[0], refs[-2:]
     rows, kv_heads, slots, head_dim = key_ref.shape
-    width = parts[0].shape[1]
     width_query = slice_width * wide
     heads = width_query // head_dim
     group = heads // kv_heads
     scale = head_dim ** (-0.5) * math.log2(math.e)
     here = lax.axis_index("wide")
-
-    for d in range(wide):
-        stack[d] = parts[d][...].astype(F32)
-    for w in range(wide):
-        proj[:, w * width : (w + 1) * width] = stack[lax.bitwise_xor(here, w)]
+    half = lax.div(here, near)
+    half = 1 - half if far else half
+    first = half * (kv_heads // 2)
 
     cosine = cos_ref[...]
     sine = sin_ref[...]
 
+    def columns(at):
+        return proj[:, pl.ds(pl.multiple_of(at, LANES), head_dim)]
+
     def turned(at):
-        x = proj[:, at : at + head_dim]
+        x = columns(at)
         return (x * cosine + pltpu.roll(x, head_dim // 2, 1) * sine).astype(BF16).astype(F32)
 
-    for h in range(heads):
-        q = turned(h * head_dim)
+    for h in range(heads // 2):
+        q = turned((first * group + h) * head_dim)
         for s in range(steps):
             for r in range(rows):
                 i = s * rows + r
@@ -196,13 +210,16 @@
     def compare(k):
         return [
             lax.dot_general(
-                query[k, r].astype(BF16), key_ref[r, k], (((1,), (1,)), ((), ())), preferred_element_type=F32
+                query[k, r].astype(BF16),
+                key_ref[r, first + k],
+                (((1,), (1,)), ((), ())),
+                preferred_element_type=F32,
             )
             for r in range(rows)
         ]
 
     def weigh(k, scores):
-        fresh_key = turned(width_query + k * head_dim)
+        fresh_key = turned(width_query + (first + k) * head_dim)
         made = []
         for r in range(rows):
             cached = scores[r] + mask_ref[r : r + 1]
@@ -222,10 +239,9 @@
         return made
 
     def combine(k, made):
-        at = width_query + (kv_heads + k) * head_dim
-        fresh_value = proj[:, at : at + head_dim]
+        fresh_value = columns(width_query + (kv_heads + first + k) * head_dim)
         for r, (weights, fresh, denominator) in enumerate(made):
-            out = jnp.dot(weights, value_ref[r, k], preferred_element_type=F32)
+            out = jnp.dot(weights, value_ref[r, first + k], preferred_element_type=F32)
             for j, weight in enumerate(fresh):
                 i = j * rows + r
                 out = out + weight.astype(BF16).astype(F32) * fresh_value[i : i + 1]
@@ -238,31 +254,27 @@
                     total[w, i : i + 1, col : col + head_dim] = out[s * group + g : s * group + g + 1]
 
     scores, ready = compare(0), None
-    for k in range(kv_heads):
-        following = compare(k + 1) if k + 1 < kv_heads else None
+    for k in range(kv_heads // 2):
+        following = compare(k + 1) if k + 1 < kv_heads // 2 else None
         made = weigh(k, scores)
         if ready:
             combine(*ready)
         ready, scores = (k, made), following
     combine(*ready)
-    for d in range(wide):
-        outs[d][...] = total[lax.bitwise_xor(here, d)].astype(BF16)
-
-
-def join_kernel(*refs):
+    for d in range(near):
+        outs[d][...] = total[lax.bitwise_xor(lax.rem(here, near), d)].astype(BF16)
+
+
+def join_kernel(order, *refs):
     per = refs[0].shape[0]
     scratch = refs[-1]
-    for d, ref in enumerate(refs[:-2]):
+    for d, ref in zip(order, refs):
         scratch[d * per : (d + 1) * per] = ref[...].astype(F32)
     refs[-2][...] = scratch[...].astype(BF16)
 
 
-def output_kernel(wide, narrow, steps, rows, *refs):
-    blocks, (early_ref, late_ref, w_ref) = refs[:narrow], refs[narrow : narrow + 3]
-    keep_ref, send_ref, ordered, acc, last, sem = refs[narrow + 3 :]
-    ends = [early_ref.shape[0], early_ref.shape[0] + late_ref.shape[0], w_ref.shape[0]]
-    rest = pltpu.make_async_copy(w_ref.at[pl.ds(ends[1], ends[2] - ends[1])], last, sem)
-    rest.start()
+def arrange_kernel(wide, narrow, steps, rows, *refs):
+    blocks, ordered = refs[:narrow], refs[-1]
     block, depth = blocks[0].shape
     tokens = block * narrow
     per = steps * rows
@@ -273,24 +285,32 @@
     step = lax.rem(lax.div(out, rows * narrow), steps)
     d = lax.div(out, per * narrow)
     d = lax.rem(d, wide // 2) * 2 + lax.div(d, wide // 2)
-    e = lax.bitwise_xor(owner, here)
-    order = (src == ((e * wide + d) * steps + step) * rows + row).astype(BF16)
+    place = narrow - 1 - lax.bitwise_xor(owner, here)
+    order = (src == ((place * wide + d) * steps + step) * rows + row).astype(BF16)
     for at, size in chunks(depth, 512):
         x = jnp.concatenate([b[:, at : at + size] for b in blocks], axis=0)
         ordered[:, at : at + size] = jnp.dot(order, x, preferred_element_type=F32).astype(BF16)
-    half = tokens // 2
-    for i, (piece, begin, end) in enumerate(zip((early_ref, late_ref, last), [0] + ends, ends)):
-        if i == 2:
-            rest.wait()
-        for at, size in chunks(w_ref.shape[1], 512):
-            y = jnp.dot(ordered[:, begin:end], piece[:, at : at + size], preferred_element_type=F32)
-            if i:
-                y = y + acc[:, at : at + size]
-            if i < 2:
-                acc[:, at : at + size] = y
-                continue
-            keep_ref[:, at : at + size] = y[:half]
-            send_ref[:, at : at + size] = y[half:].astype(BF16)
+
+
+def output_kernel(first, arrange, *refs):
+    inputs, (keep_ref, send_ref) = refs[: -2 - bool(arrange)], refs[-2:]
+    blocks, pieces = inputs[:-3], inputs[-3:]
+    half, span = keep_ref.shape
+    if arrange:
+        ordered = refs[-3]
+        arrange(*blocks, ordered)
+    else:
+        ordered = blocks[0]
+    for at, size in chunks(span, 512):
+        y, begin = 0.0, 0
+        for piece in pieces:
+            end = begin + piece.shape[0]
+            y = y + jnp.dot(
+                ordered[:, begin:end], piece[:, first + at : first + at + size], preferred_element_type=F32
+            )
+            begin = end
+        keep_ref[:, at : at + size] = y[:half]
+        send_ref[:, at : at + size] = y[half:].astype(BF16)
 
 
 def pair_kernel(keep_ref, other_ref, *outs):
@@ -301,7 +321,12 @@
 
 
 def total_kernel(*refs):
-    refs[-1][...] = sum(ref[...].astype(F32) for ref in refs[:-1]).astype(BF16)
+    count = refs[-1].shape[1] // refs[0].shape[1]
+    each = (len(refs) - 1) // count
+    span = refs[0].shape[1]
+    for i in range(count):
+        part = refs[i * each : (i + 1) * each]
+        refs[-1][:, i * span : (i + 1) * span] = sum(ref[...].astype(F32) for ref in part).astype(BF16)
 
 
 def call(kernel, name, outs, inputs, scratch=(), specs=None, flops=0, size=0, exps=0):
@@ -333,7 +358,7 @@
     half = np.arange(head_dim) % (head_dim // 2)
     freqs = np.asarray(rope_base ** (-2.0 * half / head_dim), np.float32)[None]
     qkv_split = depth // 2
-    early, late = slice_width // 4, slice_width // 2
+    quarter = slice_width // 4
 
     (qkv_near,) = fetch([(qkv_weight, 0, qkv_split)], [])
     with jax.named_scope("gather_tokens"):
@@ -358,8 +383,8 @@
         [whole()] * (wide + 2) + [pl.BlockSpec(memory_space=pltpu.HBM)],
         flops=2 * tokens * depth * width, size=2 * depth * width,
     )
-    keys, values, cosine, sine, mask = fetch(
-        [(key_cache, 0, rows), (cache_of_values, 0, rows)],
+    keys, values, out_first, cosine, sine, mask = fetch(
+        [(key_cache, 0, rows), (cache_of_values, 0, rows), (out_weight, 0, quarter)],
         [partial[0]],
         (steps, lengths, jnp.asarray(freqs)),
     )
@@ -372,55 +397,65 @@
         specs=[whole()] * narrow + [hbm()],
         size=4 * tokens * width,
     )
-    (out_early,) = fetch([(out_weight, 0, early)], [normed[0]])
+    (out_second,) = fetch([(out_weight, quarter, quarter)], [normed[0]])
     with jax.named_scope("columns_to_owner"):
         mine = [swap(p, "wide", d) if d else p for d, p in enumerate(normed)]
-    attended = call(
-        functools.partial(attend_kernel, wide, steps, slice_width), "attend",
-        [shape((per, slice_width), BF16)] * wide,
-        [mask] + mine + [cosine, sine, resident(keys), resident(values), out_early],
-        [
-            pltpu.VMEM((wide, per, width), F32),
-            pltpu.VMEM((per, width * wide), F32),
-            pltpu.VMEM((kv_heads, rows, steps * heads // kv_heads, head_dim), F32),
-            pltpu.VMEM((wide, per, slice_width), F32),
-        ],
-        [whole()] * (wide + 5) + [hbm()],
-        flops=4 * per * heads * slots * head_dim,
-        size=4 * rows * kv_heads * slots * head_dim,
-        exps=per * heads * slots,
-    )
-    with jax.named_scope("heads_to_weights"):
-        arrived = [swap(p, "wide", d) if d else p for d, p in enumerate(attended)]
+    common = [mask, cosine, sine, resident(keys), resident(values)]
+    scratch = [
+        pltpu.VMEM((kv_heads // 2, rows, steps * heads // kv_heads, head_dim), F32),
+        pltpu.VMEM((wide // 2, per, slice_width), F32),
+    ]
+    arrived, inputs, extra = {}, mine, [out_second]
+    for far in (True, False):
+        results = call(
+            functools.partial(attend_kernel, wide, steps, slice_width, far), "attend",
+            [shape((per, slice_width), BF16)] * (wide // 2) + ([shape((per, width * wide), F32)] if far else []),
+            inputs + common + extra,
+            ([pltpu.VMEM((wide, per, width), F32)] if far else []) + scratch,
+            [whole()] * (len(inputs) + 5) + [hbm()] * len(extra),
+            flops=2 * per * heads * slots * head_dim,
+            size=2 * rows * kv_heads * slots * head_dim,
+            exps=per * heads * slots // 2,
+        )
+        with jax.named_scope("heads_to_weights"):
+            outs = results[: wide // 2]
+            if not far:
+                outs, arrived = lax.optimization_barrier((outs, arrived))
+            for i in range(wide // 2):
+                d = i + wide // 2 * far
+                arrived[d] = swap(outs[i], "wide", d) if d else outs[i]
+        inputs, extra = [results[-1]], []
     joined = call(
-        join_kernel, "join", shape((per * wide, slice_width), BF16), arrived,
+        functools.partial(join_kernel, list(arrived)), "join", shape((per * wide, slice_width), BF16),
+        list(arrived.values()),
         [pltpu.VMEM((per * wide, slice_width), F32)], size=4 * per * wide * slice_width,
     )
-    (out_late,) = fetch([(out_weight, early, late)], [joined])
+    (out_last,) = fetch([(out_weight, 2 * quarter, 2 * quarter)], [joined])
     with jax.named_scope("gather_over_narrow"):
-        spread = [swap(joined, "narrow", e) if e else joined for e in range(narrow)]
-    keep, send = call(
-        functools.partial(output_kernel, wide, narrow, steps, rows), "output",
-        [shape((tokens // 2, out_width), F32), shape((tokens // 2, out_width), BF16)],
-        spread
-        + [resident(out_early), resident(out_late), pltpu.with_memory_space_constraint(out_weight, pltpu.HBM)],
-        [
-            pltpu.VMEM((tokens, slice_width), BF16),
-            pltpu.VMEM((tokens, out_width), F32),
-            pltpu.VMEM((slice_width - early - late, out_width), BF16),
-            pltpu.SemaphoreType.DMA,
-        ],
-        [whole()] * (narrow + 2) + [pl.BlockSpec(memory_space=pltpu.HBM)],
-        flops=2 * tokens * slice_width * out_width, size=2 * slice_width * out_width,
-    )
-    with jax.named_scope("sum_over_wide"):
-        other = swap(send, "wide", 1)
-        chip = call(
-            pair_kernel, "pair",
-            [shape((block, out_width), BF16 if x else F32) for x in range(wide // 2)],
-            [keep, other], size=6 * tokens * out_width // 2,
+        spread = [swap(joined, "narrow", e) if e else joined for e in reversed(range(narrow))]
+    weights = [resident(out_first), resident(out_second), resident(out_last)]
+    span = out_width // 2
+    made = [shape((tokens // 2, span), F32), shape((tokens // 2, span), BF16)]
+    arrange = functools.partial(arrange_kernel, wide, narrow, steps, rows)
+    inputs, sums = spread, []
+    for i in range(2):
+        results = call(
+            functools.partial(output_kernel, i * span, None if i else arrange), "output",
+            ([] if i else [shape((tokens, slice_width), BF16)]) + made,
+            inputs + weights,
+            flops=2 * tokens * slice_width * span, size=2 * slice_width * span,
         )
-        sums = [swap(c, "wide", 2 * x) if x else c for x, c in enumerate(chip)]
+        if not i:
+            inputs, results = list(results[:1]), results[1:]
+        keep, send = results
+        with jax.named_scope("sum_over_wide"):
+            other = swap(send, "wide", 1)
+            chip = call(
+                pair_kernel, "pair",
+                [shape((block, span), BF16 if x else F32) for x in range(wide // 2)],
+                [keep, other], size=6 * tokens * span // 2,
+            )
+            sums += [swap(c, "wide", 2 * x) if x else c for x, c in enumerate(chip)]
     total = call(
         total_kernel, "total", shape((block, out_width), BF16), sums, size=8 * block * out_width
     )

time: 55.5 us -> 54.4 us (0.980)
  waiting for transfers between devices: 13.5 us -> 9.12 us
  starting transfers between devices: 17.3 us -> 19 us
  Pallas kernels: 24.3 us -> 25.9 us
    ppermute x17 -> x19, waiting for transfers between devices: 13.5 us -> 9.12 us  [swap(): return lax.ppermute(array, axis, [(i, i ^ distance) for i in range(size)])]
    ppermute x17 -> x19, starting transfers between devices: 17.3 us -> 19 us  [swap(): return lax.ppermute(array, axis, [(i, i ^ distance) for i in range(size)])]
    pallas_call x4, Pallas kernels: 13.3 us -> 14.5 us  [fetch(): pl.pallas_call(functools.partial(fetch_kernel, [(at, n) for _, at, n in s...]
    pallas_call x7 -> x10, Pallas kernels: 11 us -> 11.4 us  [call(): pl.pallas_call(kernel, out_shape=outs, in_specs=specs or [whole()] * len(...]
  transfers between devices with their start and end apart: 17 -> 19, of which waited for: 8 -> 9; matrix products, arithmetic and copies ran while one was open for 0% -> 0% of each run, Pallas kernels for 24% -> 32%
where the time goes in v4:
time: 54.4 us; the launch traced here: 54.2 us
  Pallas kernels  25.9 us (48%)
  starting transfers between devices  19 us (35%)
  waiting for transfers between devices  9.12 us (17%)
    ppermute x19, starting transfers between devices, swap(): return lax.ppermute(array, axis, [(i, i ^ distance) for i in range(size)])  19 us
    pallas_call x4, Pallas kernels, fetch(): pl.pallas_call(functools.partial(fetch_kernel, [(at, n) for _, at, n in s...  14.5 us
    pallas_call x10, Pallas kernels, call(): pl.pallas_call(kernel, out_shape=outs, in_specs=specs or [whole()] * len(...  11.4 us
    ppermute x19, waiting for transfers between devices, swap(): return lax.ppermute(array, axis, [(i, i ^ distance) for i in range(size)])  9.12 us
  transfers between devices with their start and end apart: 19, of which 9 were waited for; matrix products, arithmetic and copies ran while one was open for 0% of the time, Pallas kernels for 32%

profile of v4, /device:TPU:0, one launch (start us, length us, event | category | flops | bytes accessed | tf_op | source)
XLA Modules:
  0.0 54.2 jit_solution(6584054615377518451)
XLA Ops:
  0.0 2.9 %collective-permute-start.1 = (bf16[16,4096]{1,0:T(8,128)(2,1)}, bf16[16,4096]{1,0:T(8,128)(2,1)S(1)}, u32[]{:S(2)}, u32[]{:S(2)}) collective-permute-start(bf16[16,4096]{1,0:T(8,128)(2,1)} %bitcast.2), channel_id=1, source_target_pairs={{0,8},{4,12},{8,0},{12,4},{1,9},{5,13},{9,1},{13,5},{2,10},{6,14},... | collective-permute-start | bytes 393224 | tf_op jit(solution)/shard_map/gather_tokens/ppermute | solution.py:44
  2.9 0.0 collective-permute-start
  2.9 3.7 %fetch.4.refs_5_ = bf16[2048,2304]{1,0:T(8,128)(2,1)S(1)} custom-call(bf16[4096,2304]{1,0:T(8,128)(2,1)} %refs_6_.1), custom_call_target="tpu_custom_call" | custom-call | bytes 18874368 | tf_op jit(solution)/shard_map/fetch/pallas_call | solution.py:89
  6.6 0.0 collective-permute-done.1.refs_2_
  6.7 0.5 %collective-permute-start.2 = (bf16[16,4096]{1,0:T(8,128)(2,1)S(1)}, bf16[16,4096]{1,0:T(8,128)(2,1)S(1)}, u32[]{:S(2)}, u32[]{:S(2)}) collective-permute-start(bf16[16,4096]{1,0:T(8,128)(2,1)S(1)} %collective-permute-done.1.refs_2_), channel_id=1, source_target_pairs={{0,4},{4,0},{8,12},{12,8},{1,5},{5,1},{9,13},{13,9},{2,6},{6,2},{1... | collective-permute-start | bytes 393224 | tf_op jit(solution)/shard_map/gather_tokens/ppermute | solution.py:44
  7.2 0.0 copy-start.1
  7.3 0.0 copy-start.2
  7.3 0.0 collective-permute-done.refs_1_
  7.3 0.9 %collective-permute-done.2.refs_3_ = bf16[16,4096]{1,0:T(8,128)(2,1)S(1)} collective-permute-done((bf16[16,4096]{1,0:T(8,128)(2,1)S(1)}, bf16[16,4096]{1,0:T(8,128)(2,1)S(1)}, u32[]{:S(2)}, u32[]{:S(2)}) %collective-permute-start.2) | collective-permute-done | bytes 131104 | tf_op jit(solution)/shard_map/gather_tokens/ppermute | solution.py:44
  8.2 4.5 %project.1 = (bf16[16,2432]{1,0:T(8,128)(2,1)S(1)}, bf16[16,2432]{1,0:T(8,128)(2,1)S(1)}, bf16[16,2432]{1,0:T(8,128)(2,1)S(1)}, bf16[16,2432]{1,0:T(8,128)(2,1)S(1)}) custom-call(bf16[16,4096]{1,0:T(8,128)(2,1)S(1)} %bitcast.4, bf16[16,4096]{1,0:T(8,128)(2,1)S(1)} %collective-permute-done.refs_1_, bf16[16,4096]{1,0:T(8,128)(2,1)S(1)} %collective-permute-done.1.refs_2_, ...), custom_call_target="tpu_custom_call" | custom-call | flops 1207959552 | bytes 18874368 | tf_op jit(solution)/shard_map/project/pallas_call | solution.py:333
  12.7 3.7 %collective-permute-start.3 = (bf16[16,2432]{1,0:T(8,128)(2,1)S(1)}, bf16[16,2432]{1,0:T(8,128)(2,1)S(1)}, u32[]{:S(2)}, u32[]{:S(2)}) collective-permute-start(bf16[16,2432]{1,0:T(8,128)(2,1)S(1)} %get-tuple-element.41), channel_id=1, source_target_pairs={{0,3},{1,2},{2,1},{3,0},{4,7},{5,6},{6,5},{7,4},{8,11},{9,10},{10,... | collective-permute-start | bytes 233480 | tf_op jit(solution)/shard_map/sum_over_narrow/ppermute | solution.py:44
  16.4 0.0 collective-permute-start.4
  16.4 0.8 %collective-permute-start.5 = (bf16[16,2432]{1,0:T(8,128)(2,1)S(1)}, bf16[16,2432]{1,0:T(8,128)(2,1)S(1)}, u32[]{:S(2)}, u32[]{:S(2)}) collective-permute-start(bf16[16,2432]{1,0:T(8,128)(2,1)S(1)} %get-tuple-element.43), channel_id=1, source_target_pairs={{0,1},{1,0},{2,3},{3,2},{4,5},{5,4},{6,7},{7,6},{8,9},{9,8},{10,11... | collective-permute-start | bytes 233480 | tf_op jit(solution)/shard_map/sum_over_narrow/ppermute | solution.py:44
  17.2 5.2 %fetch.5 = (bf16[2,4,2048,128]{3,2,1,0:T(8,128)(2,1)S(1)}, bf16[2,4,2048,128]{3,2,1,0:T(8,128)(2,1)S(1)}, bf16[512,4096]{1,0:T(8,128)(2,1)S(1)}, f32[4,128]{1,0:...) custom-call(bf16[2,4,2048,128]{3,2,1,0:T(8,128)(2,1)} %refs_0_.5, bf16[2,4,2048,128]{3,2,1,0:T(8,128)(2,1)} %refs_1_.1, ...), custom_call_target="tpu_custom_call" | custom-call | bytes 25165824 | tf_op jit(solution)/shard_map/fetch/pallas_call | solution.py:89
  22.4 0.0 collective-permute-done.3.refs_0_
  22.4 1.0 %collective-permute-done.4.refs_1_ = bf16[16,2432]{1,0:T(8,128)(2,1)S(1)} collective-permute-done((bf16[16,2432]{1,0:T(8,128)(2,1)S(1)}, bf16[16,2432]{1,0:T(8,128)(2,1)S(1)}, u32[]{:S(2)}, u32[]{:S(2)}) %collective-permute-start.4) | collective-permute-done | bytes 77856 | tf_op jit(solution)/shard_map/sum_over_narrow/ppermute | solution.py:44
  23.4 0.0 collective-permute-done.5.refs_2_
  23.4 0.2 normalize.1
  23.6 0.1 collective-permute-start.6
  23.7 1.4 %collective-permute-start.7 = (bf16[4,2304]{1,0:T(4,128)(2,1)S(1)}, bf16[4,2304]{1,0:T(4,128)(2,1)S(1)}, u32[]{:S(2)}, u32[]{:S(2)}) collective-permute-start(bf16[4,2304]{1,0:T(4,128)(2,1)S(1)} %get-tuple-element.48), channel_id=1, source_target_pairs={{0,8},{4,12},{8,0},{12,4},{1,9},{5,13},{9,1},{13,5},{2,10},{6,14},... | collective-permute-start | bytes 55304 | tf_op jit(solution)/shard_map/columns_to_owner/ppermute | solution.py:44
  25.0 0.5 collective-permute-start.8
  25.5 2.2 %fetch.6.refs_9_.refs_5_.refs_2_ = bf16[512,4096]{1,0:T(8,128)(2,1)S(1)} custom-call(bf16[2048,4096]{1,0:T(8,128)(2,1)} %refs_0_.7, bf16[4,2304]{1,0:T(4,128)(2,1)S(1)} %get-tuple-element.46.refs_1_.refs_0_), custom_call_target="tpu_custom_call" | custom-call | bytes 8388608 | tf_op jit(solution)/shard_map/fetch/pallas_call | solution.py:89
  27.7 0.0 collective-permute-done.6.refs_1_
  27.7 0.5 collective-permute-done.8.refs_3_
  28.2 1.4 %attend.2 = (bf16[4,2048]{1,0:T(4,128)(2,1)S(1)}, bf16[4,2048]{1,0:T(4,128)(2,1)S(1)}, f32[4,9216]{1,0:T(4,128)S(1)}) custom-call(bf16[4,2304]{1,0:T(4,128)(2,1)S(1)} %get-tuple-element.46.refs_1_.refs_0_, bf16[4,2304]{1,0:T(4,128)(2,1)S(1)} %collective-permute-done.6.refs_1_, bf16[4,2304]{1,0:T(4,128)(2,1)S(1)} %collective-permute-done.7.refs_2_, ...), custom_call_target="tpu_custom_call" | custom-call | flops 134217728 | bytes 4194304 | tf_op jit(solution)/shard_map/attend/pallas_call | solution.py:333
  29.6 0.9 %collective-permute-start.9 = (bf16[4,2048]{1,0:T(4,128)(2,1)S(1)}, bf16[4,2048]{1,0:T(4,128)(2,1)S(1)}, u32[]{:S(2)}, u32[]{:S(2)}) collective-permute-start(bf16[4,2048]{1,0:T(4,128)(2,1)S(1)} %get-tuple-element.57), channel_id=1, source_target_pairs={{0,8},{4,12},{8,0},{12,4},{1,9},{5,13},{9,1},{13,5},{2,10},{6,14},... | collective-permute-start | bytes 49160 | tf_op jit(solution)/shard_map/heads_to_weights/ppermute | solution.py:44
  30.5 0.7 %collective-permute-start.10 = (bf16[4,2048]{1,0:T(4,128)(2,1)S(1)}, bf16[4,2048]{1,0:T(4,128)(2,1)S(1)}, u32[]{:S(2)}, u32[]{:S(2)}) collective-permute-start(bf16[4,2048]{1,0:T(4,128)(2,1)S(1)} %get-tuple-element.58), channel_id=1, source_target_pairs={{0,12},{4,8},{8,4},{12,0},{1,13},{5,9},{9,5},{13,1},{2,14},{6,10},... | collective-permute-start | bytes 49160 | tf_op jit(solution)/shard_map/heads_to_weights/ppermute | solution.py:44
  31.2 1.3 %attend.3 = (bf16[4,2048]{1,0:T(4,128)(2,1)S(1)}, bf16[4,2048]{1,0:T(4,128)(2,1)S(1)}) custom-call(f32[4,9216]{1,0:T(4,128)S(1)} %get-tuple-element.54.refs_0_, f32[2,2048]{1,0:T(2,128)S(1)} %get-tuple-element.50.refs_4_.refs_1_, f32[4,128]{1,0:T(4,128)S(1)} %get-tuple-element.45.refs_4_.refs_5_.refs_2_, f32[4,128]{1,0:T(4,128)S(1)} %get-tuple-element.51.refs_6_.refs_3_, ...), custom_call_target="tpu_custom_call" | custom-call | flops 134217728 | bytes 4194304 | tf_op jit(solution)/shard_map/attend/pallas_call | solution.py:333
  32.5 0.9 %collective-permute-done.9.refs_0_ = bf16[4,2048]{1,0:T(4,128)(2,1)S(1)} collective-permute-done((bf16[4,2048]{1,0:T(4,128)(2,1)S(1)}, bf16[4,2048]{1,0:T(4,128)(2,1)S(1)}, u32[]{:S(2)}, u32[]{:S(2)}) %collective-permute-start.9) | collective-permute-done | bytes 16416 | tf_op jit(solution)/shard_map/heads_to_weights/ppermute | solution.py:44
  33.4 0.3 collective-permute-done.10.refs_1_
  33.7 0.1 collective-permute-start.11
  33.8 1.1 %collective-permute-done.11.refs_3_ = bf16[4,2048]{1,0:T(4,128)(2,1)S(1)} collective-permute-done((bf16[4,2048]{1,0:T(4,128)(2,1)S(1)}, bf16[4,2048]{1,0:T(4,128)(2,1)S(1)}, u32[]{:S(2)}, u32[]{:S(2)}) %collective-permute-start.11) | collective-permute-done | bytes 16416 | tf_op jit(solution)/shard_map/heads_to_weights/ppermute | solution.py:44
  34.9 2.9 %collective-permute-start.12 = (bf16[16,2048]{1,0:T(8,128)(2,1)S(1)}, bf16[16,2048]{1,0:T(8,128)(2,1)S(1)}, u32[]{:S(2)}, u32[]{:S(2)}) collective-permute-start(bf16[16,2048]{1,0:T(8,128)(2,1)S(1)} %join.1.refs_1_.refs_3_), channel_id=1, source_target_pairs={{0,3},{1,2},{2,1},{3,0},{4,7},{5,6},{6,5},{7,4},{8,11},{9,10},{10,... | collective-permute-start | bytes 196616 | tf_op jit(solution)/shard_map/gather_over_narrow/ppermute | solution.py:44
  37.8 0.0 collective-permute-start.13
  37.8 1.6 %collective-permute-start.14 = (bf16[16,2048]{1,0:T(8,128)(2,1)S(1)}, bf16[16,2048]{1,0:T(8,128)(2,1)S(1)}, u32[]{:S(2)}, u32[]{:S(2)}) collective-permute-start(bf16[16,2048]{1,0:T(8,128)(2,1)S(1)} %join.1.refs_1_.refs_3_), channel_id=1, source_target_pairs={{0,1},{1,0},{2,3},{3,2},{4,5},{5,4},{6,7},{7,6},{8,9},{9,8},{10,11... | collective-permute-start | bytes 196616 | tf_op jit(solution)/shard_map/gather_over_narrow/ppermute | solution.py:44
  39.3 3.4 %fetch.7.refs_6_.refs_3_ = bf16[1024,4096]{1,0:T(8,128)(2,1)S(1)} custom-call(bf16[2048,4096]{1,0:T(8,128)(2,1)} %refs_0_.7, bf16[16,2048]{1,0:T(8,128)(2,1)S(1)} %join.1.refs_1_.refs_3_), custom_call_target="tpu_custom_call" | custom-call | bytes 16777216 | tf_op jit(solution)/shard_map/fetch/pallas_call | solution.py:89
  42.7 1.0 %collective-permute-done.13.refs_1_ = bf16[16,2048]{1,0:T(8,128)(2,1)S(1)} collective-permute-done((bf16[16,2048]{1,0:T(8,128)(2,1)S(1)}, bf16[16,2048]{1,0:T(8,128)(2,1)S(1)}, u32[]{:S(2)}, u32[]{:S(2)}) %collective-permute-start.13) | collective-permute-done | bytes 65568 | tf_op jit(solution)/shard_map/gather_over_narrow/ppermute | solution.py:44
  43.8 1.7 %output.2 = (bf16[64,2048]{1,0:T(8,128)(2,1)S(1)}, f32[32,2048]{1,0:T(8,128)S(1)}, bf16[32,2048]{1,0:T(8,128)(2,1)S(1)}) custom-call(bf16[16,2048]{1,0:T(8,128)(2,1)S(1)} %collective-permute-done.12.refs_0_, bf16[16,2048]{1,0:T(8,128)(2,1)S(1)} %collective-permute-done.13.refs_1_, bf16[16,2048]{1,0:T(8,128)(2,1)S(1)} %collective-permute-done.14.refs_2_, ...), custom_call_target="tpu_custom_call" | custom-call | flops 536870912 | bytes 8388608 | tf_op jit(solution)/shard_map/output/pallas_call | solution.py:333
  45.5 0.2 collective-permute-start.15
  45.7 1.6 %output.3 = (f32[32,2048]{1,0:T(8,128)S(1)}, bf16[32,2048]{1,0:T(8,128)(2,1)S(1)}) custom-call(bf16[64,2048]{1,0:T(8,128)(2,1)S(1)} %get-tuple-element.68.refs_0_, bf16[512,4096]{1,0:T(8,128)(2,1)S(1)} %get-tuple-element.63.refs_4_.refs_1_, bf16[512,4096]{1,0:T(8,128)(2,1)S(1)} %fetch.6.refs_9_.refs_5_.refs_2_, bf16[1024,4096]{1,0:T(8,128)(2,1)S(1)} %fetch.7.refs_6_.refs_3_), custom_call_target="tpu_custom_call" | custom-call | flops 536870912 | bytes 8388608 | tf_op jit(solution)/shard_map/output/pallas_call | solution.py:333
  47.3 0.5 collective-permute-start.17
  47.7 0.0 collective-permute-done.15.other_ref
  47.8 1.3 %collective-permute-start.16 = (bf16[16,2048]{1,0:T(8,128)(2,1)S(1)}, bf16[16,2048]{1,0:T(8,128)(2,1)S(1)}, u32[]{:S(2)}, u32[]{:S(2)}) collective-permute-start(bf16[16,2048]{1,0:T(8,128)(2,1)S(1)} %get-tuple-element.67), channel_id=1, source_target_pairs={{0,8},{4,12},{8,0},{12,4},{1,9},{5,13},{9,1},{13,5},{2,10},{6,14},... | collective-permute-start | bytes 196616 | tf_op jit(solution)/shard_map/sum_over_wide/ppermute | solution.py:44
  49.1 0.0 collective-permute-done.17.other_ref
  49.1 1.0 %collective-permute-start.18 = (bf16[16,2048]{1,0:T(8,128)(2,1)S(1)}, bf16[16,2048]{1,0:T(8,128)(2,1)S(1)}, u32[]{:S(2)}, u32[]{:S(2)}) collective-permute-start(bf16[16,2048]{1,0:T(8,128)(2,1)S(1)} %get-tuple-element.72), channel_id=1, source_target_pairs={{0,8},{4,12},{8,0},{12,4},{1,9},{5,13},{9,1},{13,5},{2,10},{6,14},... | collective-permute-start | bytes 196616 | tf_op jit(solution)/shard_map/sum_over_wide/ppermute | solution.py:44
  50.1 2.4 %collective-permute-done.16.refs_1_ = bf16[16,2048]{1,0:T(8,128)(2,1)S(1)} collective-permute-done((bf16[16,2048]{1,0:T(8,128)(2,1)S(1)}, bf16[16,2048]{1,0:T(8,128)(2,1)S(1)}, u32[]{:S(2)}, u32[]{:S(2)}) %collective-permute-start.16) | collective-permute-done | bytes 65568 | tf_op jit(solution)/shard_map/sum_over_wide/ppermute | solution.py:44
  52.5 1.0 %collective-permute-done.18.refs_3_ = bf16[16,2048]{1,0:T(8,128)(2,1)S(1)} collective-permute-done((bf16[16,2048]{1,0:T(8,128)(2,1)S(1)}, bf16[16,2048]{1,0:T(8,128)(2,1)S(1)}, u32[]{:S(2)}, u32[]{:S(2)}) %collective-permute-start.18) | collective-permute-done | bytes 65568 | tf_op jit(solution)/shard_map/sum_over_wide/ppermute | solution.py:44
  53.5 0.7 %total.1 = bf16[16,4096]{1,0:T(8,128)(2,1)} custom-call(f32[16,2048]{1,0:T(8,128)S(1)} %get-tuple-element.66.refs_0_, bf16[16,2048]{1,0:T(8,128)(2,1)S(1)} %collective-permute-done.16.refs_1_, f32[16,2048]{1,0:T(8,128)S(1)} %get-tuple-element.71.refs_2_, bf16[16,2048]{1,0:T(8,128)(2,1)S(1)} %collective-permute-done.18.refs_3_), custom_call_target="tpu_custom_call" | custom-call | bytes 524288 | tf_op jit(solution)/shard_map/total/pallas_call | solution.py:333
  (13 shorter events, 0.1 us)
Async XLA Ops:
  0.0 7.2 %copy-start.3 = (bf16[4096]{0:T(1024)(128)(2,1)S(1)}, bf16[4096]{0:T(1024)(128)(2,1)}, u32[]{:S(2)}) copy-start(bf16[4096]{0:T(1024)(128)(2,1)} %param.9) | copy-start | bytes 24580
  0.0 8.2 %copy-start = (bf16[2,8,4096]{2,1,0:T(8,128)(2,1)S(1)}, bf16[2,8,4096]{2,1,0:T(8,128)(2,1)}, u32[]{:S(2)}) copy-start(bf16[2,8,4096]{2,1,0:T(8,128)(2,1)} %param.8) | copy-start | bytes 393220
  0.0 6.7 %collective-permute-start.1 = (bf16[16,4096]{1,0:T(8,128)(2,1)}, bf16[16,4096]{1,0:T(8,128)(2,1)S(1)}, u32[]{:S(2)}, u32[]{:S(2)}) collective-permute-start(bf16[16,4096]{1,0:T(8,128)(2,1)} %bitcast.2), channel_id=1, source_target_pairs={{0,8},{4,12},{8,0},{12,4},{1,9},{5,13},{9,1},{13,5},{2,10},{6,14},... | collective-permute-start | bytes 393224 | tf_op jit(solution)/shard_map/gather_tokens/ppermute | solution.py:44
  2.9 4.3 %collective-permute-start = (bf16[16,4096]{1,0:T(8,128)(2,1)}, bf16[16,4096]{1,0:T(8,128)(2,1)S(1)}, u32[]{:S(2)}, u32[]{:S(2)}) collective-permute-start(bf16[16,4096]{1,0:T(8,128)(2,1)} %bitcast.3), channel_id=1, source_target_pairs={{0,4},{4,0},{8,12},{12,8},{1,5},{5,1},{9,13},{13,9},{2,6},{6,2},{1... | collective-permute-start | bytes 393224 | tf_op jit(solution)/shard_map/gather_tokens/ppermute | solution.py:44
  6.7 1.5 %collective-permute-start.2 = (bf16[16,4096]{1,0:T(8,128)(2,1)S(1)}, bf16[16,4096]{1,0:T(8,128)(2,1)S(1)}, u32[]{:S(2)}, u32[]{:S(2)}) collective-permute-start(bf16[16,4096]{1,0:T(8,128)(2,1)S(1)} %collective-permute-done.1.refs_2_), channel_id=1, source_target_pairs={{0,4},{4,0},{8,12},{12,8},{1,5},{5,1},{9,13},{13,9},{2,6},{6,2},{1... | collective-permute-start | bytes 393224 | tf_op jit(solution)/shard_map/gather_tokens/ppermute | solution.py:44
  7.2 9.9 %copy-start.1 = (s32[2]{0:T(128)S(1)}, s32[2]{0:T(128)}, u32[]{:S(2)}) copy-start(s32[2]{0:T(128)} %refs_3_.1) | copy-start | bytes 28
  7.3 9.9 %copy-start.2 = (f32[1,128]{1,0:T(1,128)S(1)}, f32[1,128]{1,0:T(1,128)}, u32[]{:S(2)}) copy-start(f32[1,128]{1,0:T(1,128)} %constant.2.clone.refs_4_) | copy-start | bytes 1540
  12.7 9.7 %collective-permute-start.3 = (bf16[16,2432]{1,0:T(8,128)(2,1)S(1)}, bf16[16,2432]{1,0:T(8,128)(2,1)S(1)}, u32[]{:S(2)}, u32[]{:S(2)}) collective-permute-start(bf16[16,2432]{1,0:T(8,128)(2,1)S(1)} %get-tuple-element.41), channel_id=1, source_target_pairs={{0,3},{1,2},{2,1},{3,0},{4,7},{5,6},{6,5},{7,4},{8,11},{9,10},{10,... | collective-permute-start | bytes 233480 | tf_op jit(solution)/shard_map/sum_over_narrow/ppermute | solution.py:44
  16.4 7.0 %collective-permute-start.4 = (bf16[16,2432]{1,0:T(8,128)(2,1)S(1)}, bf16[16,2432]{1,0:T(8,128)(2,1)S(1)}, u32[]{:S(2)}, u32[]{:S(2)}) collective-permute-start(bf16[16,2432]{1,0:T(8,128)(2,1)S(1)} %get-tuple-element.42), channel_id=1, source_target_pairs={{0,2},{1,3},{2,0},{3,1},{4,6},{5,7},{6,4},{7,5},{8,10},{9,11},{10,... | collective-permute-start | bytes 233480 | tf_op jit(solution)/shard_map/sum_over_narrow/ppermute | solution.py:44
  16.4 7.0 %collective-permute-start.5 = (bf16[16,2432]{1,0:T(8,128)(2,1)S(1)}, bf16[16,2432]{1,0:T(8,128)(2,1)S(1)}, u32[]{:S(2)}, u32[]{:S(2)}) collective-permute-start(bf16[16,2432]{1,0:T(8,128)(2,1)S(1)} %get-tuple-element.43), channel_id=1, source_target_pairs={{0,1},{1,0},{2,3},{3,2},{4,5},{5,4},{6,7},{7,6},{8,9},{9,8},{10,11... | collective-permute-start | bytes 233480 | tf_op jit(solution)/shard_map/sum_over_narrow/ppermute | solution.py:44
  23.6 4.1 %collective-permute-start.6 = (bf16[4,2304]{1,0:T(4,128)(2,1)S(1)}, bf16[4,2304]{1,0:T(4,128)(2,1)S(1)}, u32[]{:S(2)}, u32[]{:S(2)}) collective-permute-start(bf16[4,2304]{1,0:T(4,128)(2,1)S(1)} %get-tuple-element.47), channel_id=1, source_target_pairs={{0,4},{4,0},{8,12},{12,8},{1,5},{5,1},{9,13},{13,9},{2,6},{6,2},{1... | collective-permute-start | bytes 55304 | tf_op jit(solution)/shard_map/columns_to_owner/ppermute | solution.py:44
  23.7 4.1 %collective-permute-start.7 = (bf16[4,2304]{1,0:T(4,128)(2,1)S(1)}, bf16[4,2304]{1,0:T(4,128)(2,1)S(1)}, u32[]{:S(2)}, u32[]{:S(2)}) collective-permute-start(bf16[4,2304]{1,0:T(4,128)(2,1)S(1)} %get-tuple-element.48), channel_id=1, source_target_pairs={{0,8},{4,12},{8,0},{12,4},{1,9},{5,13},{9,1},{13,5},{2,10},{6,14},... | collective-permute-start | bytes 55304 | tf_op jit(solution)/shard_map/columns_to_owner/ppermute | solution.py:44
  25.0 3.2 %collective-permute-start.8 = (bf16[4,2304]{1,0:T(4,128)(2,1)S(1)}, bf16[4,2304]{1,0:T(4,128)(2,1)S(1)}, u32[]{:S(2)}, u32[]{:S(2)}) collective-permute-start(bf16[4,2304]{1,0:T(4,128)(2,1)S(1)} %get-tuple-element.49), channel_id=1, source_target_pairs={{0,12},{4,8},{8,4},{12,0},{1,13},{5,9},{9,5},{13,1},{2,14},{6,10},... | collective-permute-start | bytes 55304 | tf_op jit(solution)/shard_map/columns_to_owner/ppermute | solution.py:44
  29.6 3.8 %collective-permute-start.9 = (bf16[4,2048]{1,0:T(4,128)(2,1)S(1)}, bf16[4,2048]{1,0:T(4,128)(2,1)S(1)}, u32[]{:S(2)}, u32[]{:S(2)}) collective-permute-start(bf16[4,2048]{1,0:T(4,128)(2,1)S(1)} %get-tuple-element.57), channel_id=1, source_target_pairs={{0,8},{4,12},{8,0},{12,4},{1,9},{5,13},{9,1},{13,5},{2,10},{6,14},... | collective-permute-start | bytes 49160 | tf_op jit(solution)/shard_map/heads_to_weights/ppermute | solution.py:44
  30.5 3.2 %collective-permute-start.10 = (bf16[4,2048]{1,0:T(4,128)(2,1)S(1)}, bf16[4,2048]{1,0:T(4,128)(2,1)S(1)}, u32[]{:S(2)}, u32[]{:S(2)}) collective-permute-start(bf16[4,2048]{1,0:T(4,128)(2,1)S(1)} %get-tuple-element.58), channel_id=1, source_target_pairs={{0,12},{4,8},{8,4},{12,0},{1,13},{5,9},{9,5},{13,1},{2,14},{6,10},... | collective-permute-start | bytes 49160 | tf_op jit(solution)/shard_map/heads_to_weights/ppermute | solution.py:44
  33.7 1.2 %collective-permute-start.11 = (bf16[4,2048]{1,0:T(4,128)(2,1)S(1)}, bf16[4,2048]{1,0:T(4,128)(2,1)S(1)}, u32[]{:S(2)}, u32[]{:S(2)}) collective-permute-start(bf16[4,2048]{1,0:T(4,128)(2,1)S(1)} %get-tuple-element.62), channel_id=1, source_target_pairs={{0,4},{4,0},{8,12},{12,8},{1,5},{5,1},{9,13},{13,9},{2,6},{6,2},{1... | collective-permute-start | bytes 49160 | tf_op jit(solution)/shard_map/heads_to_weights/ppermute | solution.py:44
  34.9 7.9 %collective-permute-start.12 = (bf16[16,2048]{1,0:T(8,128)(2,1)S(1)}, bf16[16,2048]{1,0:T(8,128)(2,1)S(1)}, u32[]{:S(2)}, u32[]{:S(2)}) collective-permute-start(bf16[16,2048]{1,0:T(8,128)(2,1)S(1)} %join.1.refs_1_.refs_3_), channel_id=1, source_target_pairs={{0,3},{1,2},{2,1},{3,0},{4,7},{5,6},{6,5},{7,4},{8,11},{9,10},{10,... | collective-permute-start | bytes 196616 | tf_op jit(solution)/shard_map/gather_over_narrow/ppermute | solution.py:44
  37.8 6.0 %collective-permute-start.13 = (bf16[16,2048]{1,0:T(8,128)(2,1)S(1)}, bf16[16,2048]{1,0:T(8,128)(2,1)S(1)}, u32[]{:S(2)}, u32[]{:S(2)}) collective-permute-start(bf16[16,2048]{1,0:T(8,128)(2,1)S(1)} %join.1.refs_1_.refs_3_), channel_id=1, source_target_pairs={{0,2},{1,3},{2,0},{3,1},{4,6},{5,7},{6,4},{7,5},{8,10},{9,11},{10,... | collective-permute-start | bytes 196616 | tf_op jit(solution)/shard_map/gather_over_narrow/ppermute | solution.py:44
  37.8 6.0 %collective-permute-start.14 = (bf16[16,2048]{1,0:T(8,128)(2,1)S(1)}, bf16[16,2048]{1,0:T(8,128)(2,1)S(1)}, u32[]{:S(2)}, u32[]{:S(2)}) collective-permute-start(bf16[16,2048]{1,0:T(8,128)(2,1)S(1)} %join.1.refs_1_.refs_3_), channel_id=1, source_target_pairs={{0,1},{1,0},{2,3},{3,2},{4,5},{5,4},{6,7},{7,6},{8,9},{9,8},{10,11... | collective-permute-start | bytes 196616 | tf_op jit(solution)/shard_map/gather_over_narrow/ppermute | solution.py:44
  45.5 2.2 %collective-permute-start.15 = (bf16[32,2048]{1,0:T(8,128)(2,1)S(1)}, bf16[32,2048]{1,0:T(8,128)(2,1)S(1)}, u32[]{:S(2)}, u32[]{:S(2)}) collective-permute-start(bf16[32,2048]{1,0:T(8,128)(2,1)S(1)} %get-tuple-element.65), channel_id=1, source_target_pairs={{0,4},{4,0},{8,12},{12,8},{1,5},{5,1},{9,13},{13,9},{2,6},{6,2},{1... | collective-permute-start | bytes 393224 | tf_op jit(solution)/shard_map/sum_over_wide/ppermute | solution.py:44
  47.3 1.8 %collective-permute-start.17 = (bf16[32,2048]{1,0:T(8,128)(2,1)S(1)}, bf16[32,2048]{1,0:T(8,128)(2,1)S(1)}, u32[]{:S(2)}, u32[]{:S(2)}) collective-permute-start(bf16[32,2048]{1,0:T(8,128)(2,1)S(1)} %get-tuple-element.70), channel_id=1, source_target_pairs={{0,4},{4,0},{8,12},{12,8},{1,5},{5,1},{9,13},{13,9},{2,6},{6,2},{1... | collective-permute-start | bytes 393224 | tf_op jit(solution)/shard_map/sum_over_wide/ppermute | solution.py:44
  47.8 4.7 %collective-permute-start.16 = (bf16[16,2048]{1,0:T(8,128)(2,1)S(1)}, bf16[16,2048]{1,0:T(8,128)(2,1)S(1)}, u32[]{:S(2)}, u32[]{:S(2)}) collective-permute-start(bf16[16,2048]{1,0:T(8,128)(2,1)S(1)} %get-tuple-element.67), channel_id=1, source_target_pairs={{0,8},{4,12},{8,0},{12,4},{1,9},{5,13},{9,1},{13,5},{2,10},{6,14},... | collective-permute-start | bytes 196616 | tf_op jit(solution)/shard_map/sum_over_wide/ppermute | solution.py:44
  49.1 4.4 %collective-permute-start.18 = (bf16[16,2048]{1,0:T(8,128)(2,1)S(1)}, bf16[16,2048]{1,0:T(8,128)(2,1)S(1)}, u32[]{:S(2)}, u32[]{:S(2)}) collective-permute-start(bf16[16,2048]{1,0:T(8,128)(2,1)S(1)} %get-tuple-element.72), channel_id=1, source_target_pairs={{0,8},{4,12},{8,0},{12,4},{1,9},{5,13},{9,1},{13,5},{2,10},{6,14},... | collective-permute-start | bytes 196616 | tf_op jit(solution)/shard_map/sum_over_wide/ppermute | solution.py:44

commit v5 on v4

--- a/solution.py
+++ b/solution.py
@@ -64,13 +64,13 @@
         for s in range(steps):
             for r in range(rows):
                 i = s * rows + r
-                angle = (lengths_ref[r] + s).astype(F32) * freqs_ref[...]
+                angle = (lengths_ref[:, r : r + 1] + s).astype(F32) * freqs_ref[...]
                 lane = lax.broadcasted_iota(jnp.int32, angle.shape, 1)
                 cos_ref[i : i + 1] = jnp.cos(angle)
                 sin_ref[i : i + 1] = jnp.where(lane < angle.shape[1] // 2, -1.0, 1.0) * jnp.sin(angle)
         slot = lax.broadcasted_iota(jnp.int32, (1, mask_ref.shape[1]), 1)
         for r in range(rows):
-            mask_ref[r : r + 1] = jnp.where(slot < lengths_ref[r], 0.0, -jnp.inf)
+            mask_ref[r : r + 1] = jnp.where(slot < lengths_ref[:, r : r + 1], 0.0, -jnp.inf)
     for copy in copies:
         copy.wait()
 
@@ -83,7 +83,7 @@
     if turns:
         steps, lengths, freqs = turns
         turns = (steps, lengths.shape[0])
-        extra, extra_specs = [lengths, freqs], [pl.BlockSpec(memory_space=pltpu.SMEM), whole()]
+        extra, extra_specs = [lengths.reshape(1, -1), freqs], [whole()] * 2
         outs += [jax.ShapeDtypeStruct((steps * lengths.shape[0], freqs.shape[1]), F32)] * 2
         outs += [jax.ShapeDtypeStruct((lengths.shape[0], arrays[0].shape[2]), F32)]
     return pl.pallas_call(
@@ -169,24 +169,23 @@
         proj[:, w * width : (w + 1) * width] = stack[lax.bitwise_xor(here, w)]
 
 
-def attend_kernel(wide, steps, slice_width, far, *refs):
+def attend_kernel(wide, steps, slice_width, low, span, *refs):
+    far = 2 * low == wide
     count = wide if far else 1
     parts, (mask_ref, cos_ref, sin_ref, key_ref, value_ref) = refs[:count], refs[count : count + 5]
-    near = wide // 2
     if far:
-        outs, (proj, stack, query, total) = refs[-4 - near : -4], refs[-4:]
+        outs, (proj, stack, query, total) = refs[-4 - span : -4], refs[-4:]
         assemble(parts, proj, stack)
     else:
-        outs, proj, (query, total) = refs[-2 - near : -2], parts[0], refs[-2:]
+        outs, proj, (query, total) = refs[-2 - span : -2], parts[0], refs[-2:]
     rows, kv_heads, slots, head_dim = key_ref.shape
     width_query = slice_width * wide
     heads = width_query // head_dim
     group = heads // kv_heads
     scale = head_dim ** (-0.5) * math.log2(math.e)
     here = lax.axis_index("wide")
-    half = lax.div(here, near)
-    half = 1 - half if far else half
-    first = half * (kv_heads // 2)
+    taken = kv_heads * span // wide
+    first = lax.div(lax.bitwise_xor(here, low), span) * taken
 
     cosine = cos_ref[...]
     sine = sin_ref[...]
@@ -198,7 +197,7 @@
         x = columns(at)
         return (x * cosine + pltpu.roll(x, head_dim // 2, 1) * sine).astype(BF16).astype(F32)
 
-    for h in range(heads // 2):
+    for h in range(taken * group):
         q = turned((first * group + h) * head_dim)
         for s in range(steps):
             for r in range(rows):
@@ -254,22 +253,24 @@
                     total[w, i : i + 1, col : col + head_dim] = out[s * group + g : s * group + g + 1]
 
     scores, ready = compare(0), None
-    for k in range(kv_heads // 2):
-        following = compare(k + 1) if k + 1 < kv_heads // 2 else None
+    for k in range(taken):
+        following = compare(k + 1) if k + 1 < taken else None
         made = weigh(k, scores)
         if ready:
             combine(*ready)
         ready, scores = (k, made), following
     combine(*ready)
-    for d in range(near):
-        outs[d][...] = total[lax.bitwise_xor(lax.rem(here, near), d)].astype(BF16)
+    for d in range(span):
+        outs[d][:, :slice_width] = total[lax.rem(lax.bitwise_xor(here, low + d), span)].astype(BF16)
+        if far:
+            outs[d][:, slice_width:] = jnp.zeros((steps * rows, LANES), BF16)
 
 
 def join_kernel(order, *refs):
     per = refs[0].shape[0]
     scratch = refs[-1]
     for d, ref in zip(order, refs):
-        scratch[d * per : (d + 1) * per] = ref[...].astype(F32)
+        scratch[d * per : (d + 1) * per] = ref[:, : scratch.shape[1]].astype(F32)
     refs[-2][...] = scratch[...].astype(BF16)
 
 
@@ -358,7 +359,7 @@
     half = np.arange(head_dim) % (head_dim // 2)
     freqs = np.asarray(rope_base ** (-2.0 * half / head_dim), np.float32)[None]
     qkv_split = depth // 2
-    quarter = slice_width // 4
+    ends = [slice_width // 8, slice_width * 3 // 8]
 
     (qkv_near,) = fetch([(qkv_weight, 0, qkv_split)], [])
     with jax.named_scope("gather_tokens"):
@@ -384,7 +385,7 @@
         flops=2 * tokens * depth * width, size=2 * depth * width,
     )
     keys, values, out_first, cosine, sine, mask = fetch(
-        [(key_cache, 0, rows), (cache_of_values, 0, rows), (out_weight, 0, quarter)],
+        [(key_cache, 0, rows), (cache_of_values, 0, rows), (out_weight, 0, ends[0])],
         [partial[0]],
         (steps, lengths, jnp.asarray(freqs)),
     )
@@ -397,40 +398,40 @@
         specs=[whole()] * narrow + [hbm()],
         size=4 * tokens * width,
     )
-    (out_second,) = fetch([(out_weight, quarter, quarter)], [normed[0]])
+    (out_second,) = fetch([(out_weight, ends[0], ends[1] - ends[0])], [normed[0]])
     with jax.named_scope("columns_to_owner"):
         mine = [swap(p, "wide", d) if d else p for d, p in enumerate(normed)]
     common = [mask, cosine, sine, resident(keys), resident(values)]
-    scratch = [
-        pltpu.VMEM((kv_heads // 2, rows, steps * heads // kv_heads, head_dim), F32),
-        pltpu.VMEM((wide // 2, per, slice_width), F32),
-    ]
     arrived, inputs, extra = {}, mine, [out_second]
-    for far in (True, False):
+    for low, span in ((wide // 2, wide // 2), (wide // 4, wide // 4), (0, wide // 4)):
+        far = 2 * low == wide
         results = call(
-            functools.partial(attend_kernel, wide, steps, slice_width, far), "attend",
-            [shape((per, slice_width), BF16)] * (wide // 2) + ([shape((per, width * wide), F32)] if far else []),
+            functools.partial(attend_kernel, wide, steps, slice_width, low, span), "attend",
+            [shape((per, slice_width + LANES * far), BF16)] * span
+            + ([shape((per, width * wide), F32)] if far else []),
             inputs + common + extra,
-            ([pltpu.VMEM((wide, per, width), F32)] if far else []) + scratch,
+            ([pltpu.VMEM((wide, per, width), F32)] if far else [])
+            + [
+                pltpu.VMEM((kv_heads * span // wide, rows, steps * heads // kv_heads, head_dim), F32),
+                pltpu.VMEM((span, per, slice_width), F32),
+            ],
             [whole()] * (len(inputs) + 5) + [hbm()] * len(extra),
-            flops=2 * per * heads * slots * head_dim,
-            size=2 * rows * kv_heads * slots * head_dim,
-            exps=per * heads * slots // 2,
+            flops=4 * per * heads * slots * head_dim * span // wide,
+            size=4 * rows * kv_heads * slots * head_dim * span // wide,
+            exps=per * heads * slots * span // wide,
         )
         with jax.named_scope("heads_to_weights"):
-            outs = results[: wide // 2]
-            if not far:
-                outs, arrived = lax.optimization_barrier((outs, arrived))
-            for i in range(wide // 2):
-                d = i + wide // 2 * far
-                arrived[d] = swap(outs[i], "wide", d) if d else outs[i]
-        inputs, extra = [results[-1]], []
+            for i in range(span):
+                d = low + i
+                arrived[d] = swap(results[i], "wide", d) if d else results[i]
+        if far:
+            inputs, extra = [results[-1]], []
     joined = call(
         functools.partial(join_kernel, list(arrived)), "join", shape((per * wide, slice_width), BF16),
         list(arrived.values()),
         [pltpu.VMEM((per * wide, slice_width), F32)], size=4 * per * wide * slice_width,
     )
-    (out_last,) = fetch([(out_weight, 2 * quarter, 2 * quarter)], [joined])
+    (out_last,) = fetch([(out_weight, ends[1], slice_width - ends[1])], [joined])
     with jax.named_scope("gather_over_narrow"):
         spread = [swap(joined, "narrow", e) if e else joined for e in reversed(range(narrow))]
     weights = [resident(out_first), resident(out_second), resident(out_last)]

time: 54.4 us -> 53.2 us (0.978)
  waiting for transfers between devices: 9.12 us -> 7.6 us
  starting transfers between devices: 19 us -> 19.6 us
    ppermute x19, waiting for transfers between devices: 9.12 us -> 7.6 us  [swap(): return lax.ppermute(array, axis, [(i, i ^ distance) for i in range(size)])]
    ppermute x19, starting transfers between devices: 19 us -> 19.6 us  [swap(): return lax.ppermute(array, axis, [(i, i ^ distance) for i in range(size)])]
    pallas_call x10 -> x11, Pallas kernels: 11.4 us -> 11.6 us  [call(): pl.pallas_call(kernel, out_shape=outs, in_specs=specs or [whole()] * len(...]
  transfers between devices with their start and end apart: 19 -> 19, of which waited for: 9 -> 7; matrix products, arithmetic and copies ran while one was open for 0% -> 0% of each run, Pallas kernels for 32% -> 33%
where the time goes in v5:
time: 53.2 us; the launch traced here: 53 us
  Pallas kernels  25.6 us (48%)
  starting transfers between devices  19.6 us (37%)
  waiting for transfers between devices  7.6 us (14%)
    ppermute x19, starting transfers between devices, swap(): return lax.ppermute(array, axis, [(i, i ^ distance) for i in range(size)])  19.6 us
    pallas_call x4, Pallas kernels, fetch(): pl.pallas_call(functools.partial(fetch_kernel, [(at, n) for _, at, n in s...  14 us
    pallas_call x11, Pallas kernels, call(): pl.pallas_call(kernel, out_shape=outs, in_specs=specs or [whole()] * len(...  11.6 us
    ppermute x19, waiting for transfers between devices, swap(): return lax.ppermute(array, axis, [(i, i ^ distance) for i in range(size)])  7.6 us
  transfers between devices with their start and end apart: 19, of which 7 were waited for; matrix products, arithmetic and copies ran while one was open for 0% of the time, Pallas kernels for 33%

profile of v5, /device:TPU:0, one launch (start us, length us, event | category | flops | bytes accessed | tf_op | source)
XLA Modules:
  0.0 53.0 jit_solution(7060570546679229970)
XLA Ops:
  0.0 2.9 %collective-permute-start.1 = (bf16[16,4096]{1,0:T(8,128)(2,1)}, bf16[16,4096]{1,0:T(8,128)(2,1)S(1)}, u32[]{:S(2)}, u32[]{:S(2)}) collective-permute-start(bf16[16,4096]{1,0:T(8,128)(2,1)} %bitcast.3), channel_id=1, source_target_pairs={{0,8},{4,12},{8,0},{12,4},{1,9},{5,13},{9,1},{13,5},{2,10},{6,14},... | collective-permute-start | bytes 393224 | tf_op jit(solution)/shard_map/gather_tokens/ppermute | solution.py:44
  2.9 0.0 collective-permute-start
  2.9 3.7 %fetch.4.refs_5_ = bf16[2048,2304]{1,0:T(8,128)(2,1)S(1)} custom-call(bf16[4096,2304]{1,0:T(8,128)(2,1)} %refs_6_.1), custom_call_target="tpu_custom_call" | custom-call | bytes 18874368 | tf_op jit(solution)/shard_map/fetch/pallas_call | solution.py:89
  6.6 0.0 collective-permute-done.1.refs_2_
  6.7 0.5 %collective-permute-start.2 = (bf16[16,4096]{1,0:T(8,128)(2,1)S(1)}, bf16[16,4096]{1,0:T(8,128)(2,1)S(1)}, u32[]{:S(2)}, u32[]{:S(2)}) collective-permute-start(bf16[16,4096]{1,0:T(8,128)(2,1)S(1)} %collective-permute-done.1.refs_2_), channel_id=1, source_target_pairs={{0,4},{4,0},{8,12},{12,8},{1,5},{5,1},{9,13},{13,9},{2,6},{6,2},{1... | collective-permute-start | bytes 393224 | tf_op jit(solution)/shard_map/gather_tokens/ppermute | solution.py:44
  7.2 0.0 copy-start.1
  7.3 0.0 copy-start.2
  7.3 0.0 collective-permute-done.refs_1_
  7.3 0.9 %collective-permute-done.2.refs_3_ = bf16[16,4096]{1,0:T(8,128)(2,1)S(1)} collective-permute-done((bf16[16,4096]{1,0:T(8,128)(2,1)S(1)}, bf16[16,4096]{1,0:T(8,128)(2,1)S(1)}, u32[]{:S(2)}, u32[]{:S(2)}) %collective-permute-start.2) | collective-permute-done | bytes 131104 | tf_op jit(solution)/shard_map/gather_tokens/ppermute | solution.py:44
  8.2 4.5 %project.1 = (bf16[16,2432]{1,0:T(8,128)(2,1)S(1)}, bf16[16,2432]{1,0:T(8,128)(2,1)S(1)}, bf16[16,2432]{1,0:T(8,128)(2,1)S(1)}, bf16[16,2432]{1,0:T(8,128)(2,1)S(1)}) custom-call(bf16[16,4096]{1,0:T(8,128)(2,1)S(1)} %bitcast.5, bf16[16,4096]{1,0:T(8,128)(2,1)S(1)} %collective-permute-done.refs_1_, bf16[16,4096]{1,0:T(8,128)(2,1)S(1)} %collective-permute-done.1.refs_2_, ...), custom_call_target="tpu_custom_call" | custom-call | flops 1207959552 | bytes 18874368 | tf_op jit(solution)/shard_map/project/pallas_call | solution.py:334
  12.7 3.7 %collective-permute-start.3 = (bf16[16,2432]{1,0:T(8,128)(2,1)S(1)}, bf16[16,2432]{1,0:T(8,128)(2,1)S(1)}, u32[]{:S(2)}, u32[]{:S(2)}) collective-permute-start(bf16[16,2432]{1,0:T(8,128)(2,1)S(1)} %get-tuple-element.35), channel_id=1, source_target_pairs={{0,3},{1,2},{2,1},{3,0},{4,7},{5,6},{6,5},{7,4},{8,11},{9,10},{10,... | collective-permute-start | bytes 233480 | tf_op jit(solution)/shard_map/sum_over_narrow/ppermute | solution.py:44
  16.4 0.8 %collective-permute-start.5 = (bf16[16,2432]{1,0:T(8,128)(2,1)S(1)}, bf16[16,2432]{1,0:T(8,128)(2,1)S(1)}, u32[]{:S(2)}, u32[]{:S(2)}) collective-permute-start(bf16[16,2432]{1,0:T(8,128)(2,1)S(1)} %get-tuple-element.37), channel_id=1, source_target_pairs={{0,1},{1,0},{2,3},{3,2},{4,5},{5,4},{6,7},{7,6},{8,9},{9,8},{10,11... | collective-permute-start | bytes 233480 | tf_op jit(solution)/shard_map/sum_over_narrow/ppermute | solution.py:44
  17.2 4.1 %fetch.5 = (bf16[2,4,2048,128]{3,2,1,0:T(8,128)(2,1)S(1)}, bf16[2,4,2048,128]{3,2,1,0:T(8,128)(2,1)S(1)}, bf16[256,4096]{1,0:T(8,128)(2,1)S(1)}, f32[4,128]{1,0:...) custom-call(bf16[2,4,2048,128]{3,2,1,0:T(8,128)(2,1)} %refs_0_.5, bf16[2,4,2048,128]{3,2,1,0:T(8,128)(2,1)} %refs_1_.1, ...), custom_call_target="tpu_custom_call" | custom-call | bytes 20971520 | tf_op jit(solution)/shard_map/fetch/pallas_call | solution.py:89
  21.3 0.0 collective-permute-done.3.refs_0_
  21.3 2.1 %collective-permute-done.4.refs_1_ = bf16[16,2432]{1,0:T(8,128)(2,1)S(1)} collective-permute-done((bf16[16,2432]{1,0:T(8,128)(2,1)S(1)}, bf16[16,2432]{1,0:T(8,128)(2,1)S(1)}, u32[]{:S(2)}, u32[]{:S(2)}) %collective-permute-start.4) | collective-permute-done | bytes 77856 | tf_op jit(solution)/shard_map/sum_over_narrow/ppermute | solution.py:44
  23.4 0.2 normalize.1
  23.6 0.1 collective-permute-start.6
  23.7 1.4 %collective-permute-start.7 = (bf16[4,2304]{1,0:T(4,128)(2,1)S(1)}, bf16[4,2304]{1,0:T(4,128)(2,1)S(1)}, u32[]{:S(2)}, u32[]{:S(2)}) collective-permute-start(bf16[4,2304]{1,0:T(4,128)(2,1)S(1)} %get-tuple-element.42), channel_id=1, source_target_pairs={{0,8},{4,12},{8,0},{12,4},{1,9},{5,13},{9,1},{13,5},{2,10},{6,14},... | collective-permute-start | bytes 55304 | tf_op jit(solution)/shard_map/columns_to_owner/ppermute | solution.py:44
  25.0 0.5 collective-permute-start.8
  25.5 2.2 %fetch.6.refs_9_.refs_5_.refs_2_ = bf16[512,4096]{1,0:T(8,128)(2,1)S(1)} custom-call(bf16[2048,4096]{1,0:T(8,128)(2,1)} %refs_0_.7, bf16[4,2304]{1,0:T(4,128)(2,1)S(1)} %get-tuple-element.40.refs_1_.refs_0_), custom_call_target="tpu_custom_call" | custom-call | bytes 8388608 | tf_op jit(solution)/shard_map/fetch/pallas_call | solution.py:89
  27.7 0.0 collective-permute-done.7.refs_2_
  27.7 0.5 collective-permute-done.8.refs_3_
  28.2 1.3 %attend.3 = (bf16[4,2176]{1,0:T(4,128)(2,1)S(1)}, bf16[4,2176]{1,0:T(4,128)(2,1)S(1)}, f32[4,9216]{1,0:T(4,128)S(1)}) custom-call(bf16[4,2304]{1,0:T(4,128)(2,1)S(1)} %get-tuple-element.40.refs_1_.refs_0_, bf16[4,2304]{1,0:T(4,128)(2,1)S(1)} %collective-permute-done.6.refs_1_, bf16[4,2304]{1,0:T(4,128)(2,1)S(1)} %collective-permute-done.7.refs_2_, ...), custom_call_target="tpu_custom_call" | custom-call | flops 134217728 | bytes 4194304 | tf_op jit(solution)/shard_map/attend/pallas_call | solution.py:334
  29.5 0.9 %collective-permute-start.9 = (bf16[4,2176]{1,0:T(4,128)(2,1)S(1)}, bf16[4,2176]{1,0:T(4,128)(2,1)S(1)}, u32[]{:S(2)}, u32[]{:S(2)}) collective-permute-start(bf16[4,2176]{1,0:T(4,128)(2,1)S(1)} %get-tuple-element.48), channel_id=1, source_target_pairs={{0,8},{4,12},{8,0},{12,4},{1,9},{5,13},{9,1},{13,5},{2,10},{6,14},... | collective-permute-start | bytes 52232 | tf_op jit(solution)/shard_map/heads_to_weights/ppermute | solution.py:44
  30.4 0.7 %collective-permute-start.10 = (bf16[4,2176]{1,0:T(4,128)(2,1)S(1)}, bf16[4,2176]{1,0:T(4,128)(2,1)S(1)}, u32[]{:S(2)}, u32[]{:S(2)}) collective-permute-start(bf16[4,2176]{1,0:T(4,128)(2,1)S(1)} %get-tuple-element.49), channel_id=1, source_target_pairs={{0,12},{4,8},{8,4},{12,0},{1,13},{5,9},{9,5},{13,1},{2,14},{6,10},... | collective-permute-start | bytes 52232 | tf_op jit(solution)/shard_map/heads_to_weights/ppermute | solution.py:44
  31.1 0.8 %attend.4 = bf16[4,2048]{1,0:T(4,128)(2,1)S(1)} custom-call(f32[4,9216]{1,0:T(4,128)S(1)} %get-tuple-element.50.refs_0_, f32[2,2048]{1,0:T(2,128)S(1)} %get-tuple-element.44.refs_4_.refs_1_, f32[4,128]{1,0:T(4,128)S(1)} %get-tuple-element.39.refs_4_.refs_5_.refs_2_, f32[4,128]{1,0:T(4,128)S(1)} %get-tuple-element.45.refs_6_.refs_3_, ...), custom_call_target="tpu_custom_call" | custom-call | flops 67108864 | bytes 2097152 | tf_op jit(solution)/shard_map/attend/pallas_call | solution.py:334
  31.9 0.7 %collective-permute-start.11 = (bf16[4,2048]{1,0:T(4,128)(2,1)S(1)}, bf16[4,2048]{1,0:T(4,128)(2,1)S(1)}, u32[]{:S(2)}, u32[]{:S(2)}) collective-permute-start(bf16[4,2048]{1,0:T(4,128)(2,1)S(1)} %attend.4), channel_id=1, source_target_pairs={{0,4},{4,0},{8,12},{12,8},{1,5},{5,1},{9,13},{13,9},{2,6},{6,2},{1... | collective-permute-start | bytes 49160 | tf_op jit(solution)/shard_map/heads_to_weights/ppermute | solution.py:44
  32.6 0.8 %attend.5.refs_3_ = bf16[4,2048]{1,0:T(4,128)(2,1)S(1)} custom-call(f32[4,9216]{1,0:T(4,128)S(1)} %get-tuple-element.50.refs_0_, f32[2,2048]{1,0:T(2,128)S(1)} %get-tuple-element.44.refs_4_.refs_1_, f32[4,128]{1,0:T(4,128)S(1)} %get-tuple-element.39.refs_4_.refs_5_.refs_2_, f32[4,128]{1,0:T(4,128)S(1)} %get-tuple-element.45.refs_6_.refs_3_, ...), custom_call_target="tpu_custom_call" | custom-call | flops 67108864 | bytes 2097152 | tf_op jit(solution)/shard_map/attend/pallas_call | solution.py:334
  33.4 0.0 collective-permute-done.11.refs_2_
  33.5 0.0 collective-permute-done.9.refs_0_
  33.5 0.1 collective-permute-done.10.refs_1_
  33.6 2.5 %collective-permute-start.12 = (bf16[16,2048]{1,0:T(8,128)(2,1)S(1)}, bf16[16,2048]{1,0:T(8,128)(2,1)S(1)}, u32[]{:S(2)}, u32[]{:S(2)}) collective-permute-start(bf16[16,2048]{1,0:T(8,128)(2,1)S(1)} %join.1.refs_1_.refs_3_), channel_id=1, source_target_pairs={{0,3},{1,2},{2,1},{3,0},{4,7},{5,6},{6,5},{7,4},{8,11},{9,10},{10,... | collective-permute-start | bytes 196616 | tf_op jit(solution)/shard_map/gather_over_narrow/ppermute | solution.py:44
  36.2 0.0 collective-permute-start.13
  36.2 1.9 %collective-permute-start.14 = (bf16[16,2048]{1,0:T(8,128)(2,1)S(1)}, bf16[16,2048]{1,0:T(8,128)(2,1)S(1)}, u32[]{:S(2)}, u32[]{:S(2)}) collective-permute-start(bf16[16,2048]{1,0:T(8,128)(2,1)S(1)} %join.1.refs_1_.refs_3_), channel_id=1, source_target_pairs={{0,1},{1,0},{2,3},{3,2},{4,5},{5,4},{6,7},{7,6},{8,9},{9,8},{10,11... | collective-permute-start | bytes 196616 | tf_op jit(solution)/shard_map/gather_over_narrow/ppermute | solution.py:44
  38.1 4.0 %fetch.7.refs_6_.refs_3_ = bf16[1280,4096]{1,0:T(8,128)(2,1)S(1)} custom-call(bf16[2048,4096]{1,0:T(8,128)(2,1)} %refs_0_.7, bf16[16,2048]{1,0:T(8,128)(2,1)S(1)} %join.1.refs_1_.refs_3_), custom_call_target="tpu_custom_call" | custom-call | bytes 20971520 | tf_op jit(solution)/shard_map/fetch/pallas_call | solution.py:89
  42.1 0.0 collective-permute-done.12.refs_0_
  42.1 0.5 collective-permute-done.13.refs_1_
  42.6 1.7 %output.2 = (bf16[64,2048]{1,0:T(8,128)(2,1)S(1)}, f32[32,2048]{1,0:T(8,128)S(1)}, bf16[32,2048]{1,0:T(8,128)(2,1)S(1)}) custom-call(bf16[16,2048]{1,0:T(8,128)(2,1)S(1)} %collective-permute-done.12.refs_0_, bf16[16,2048]{1,0:T(8,128)(2,1)S(1)} %collective-permute-done.13.refs_1_, bf16[16,2048]{1,0:T(8,128)(2,1)S(1)} %collective-permute-done.14.refs_2_, ...), custom_call_target="tpu_custom_call" | custom-call | flops 536870912 | bytes 8388608 | tf_op jit(solution)/shard_map/output/pallas_call | solution.py:334
  44.3 0.1 collective-permute-start.15
  44.5 1.6 %output.3 = (f32[32,2048]{1,0:T(8,128)S(1)}, bf16[32,2048]{1,0:T(8,128)(2,1)S(1)}) custom-call(bf16[64,2048]{1,0:T(8,128)(2,1)S(1)} %get-tuple-element.56.refs_0_, bf16[256,4096]{1,0:T(8,128)(2,1)S(1)} %get-tuple-element.51.refs_4_.refs_1_, bf16[512,4096]{1,0:T(8,128)(2,1)S(1)} %fetch.6.refs_9_.refs_5_.refs_2_, bf16[1280,4096]{1,0:T(8,128)(2,1)S(1)} %fetch.7.refs_6_.refs_3_), custom_call_target="tpu_custom_call" | custom-call | flops 536870912 | bytes 8388608 | tf_op jit(solution)/shard_map/output/pallas_call | solution.py:334
  46.0 0.5 collective-permute-start.17
  46.5 0.0 collective-permute-done.15.other_ref
  46.6 1.4 %collective-permute-start.16 = (bf16[16,2048]{1,0:T(8,128)(2,1)S(1)}, bf16[16,2048]{1,0:T(8,128)(2,1)S(1)}, u32[]{:S(2)}, u32[]{:S(2)}) collective-permute-start(bf16[16,2048]{1,0:T(8,128)(2,1)S(1)} %get-tuple-element.55), channel_id=1, source_target_pairs={{0,8},{4,12},{8,0},{12,4},{1,9},{5,13},{9,1},{13,5},{2,10},{6,14},... | collective-permute-start | bytes 196616 | tf_op jit(solution)/shard_map/sum_over_wide/ppermute | solution.py:44
  47.9 0.0 collective-permute-done.17.other_ref
  48.0 1.0 %collective-permute-start.18 = (bf16[16,2048]{1,0:T(8,128)(2,1)S(1)}, bf16[16,2048]{1,0:T(8,128)(2,1)S(1)}, u32[]{:S(2)}, u32[]{:S(2)}) collective-permute-start(bf16[16,2048]{1,0:T(8,128)(2,1)S(1)} %get-tuple-element.60), channel_id=1, source_target_pairs={{0,8},{4,12},{8,0},{12,4},{1,9},{5,13},{9,1},{13,5},{2,10},{6,14},... | collective-permute-start | bytes 196616 | tf_op jit(solution)/shard_map/sum_over_wide/ppermute | solution.py:44
  48.9 2.4 %collective-permute-done.16.refs_1_ = bf16[16,2048]{1,0:T(8,128)(2,1)S(1)} collective-permute-done((bf16[16,2048]{1,0:T(8,128)(2,1)S(1)}, bf16[16,2048]{1,0:T(8,128)(2,1)S(1)}, u32[]{:S(2)}, u32[]{:S(2)}) %collective-permute-start.16) | collective-permute-done | bytes 65568 | tf_op jit(solution)/shard_map/sum_over_wide/ppermute | solution.py:44
  51.3 1.0 %collective-permute-done.18.refs_3_ = bf16[16,2048]{1,0:T(8,128)(2,1)S(1)} collective-permute-done((bf16[16,2048]{1,0:T(8,128)(2,1)S(1)}, bf16[16,2048]{1,0:T(8,128)(2,1)S(1)}, u32[]{:S(2)}, u32[]{:S(2)}) %collective-permute-start.18) | collective-permute-done | bytes 65568 | tf_op jit(solution)/shard_map/sum_over_wide/ppermute | solution.py:44
  52.3 0.7 %total.1 = bf16[16,4096]{1,0:T(8,128)(2,1)} custom-call(f32[16,2048]{1,0:T(8,128)S(1)} %get-tuple-element.54.refs_0_, bf16[16,2048]{1,0:T(8,128)(2,1)S(1)} %collective-permute-done.16.refs_1_, f32[16,2048]{1,0:T(8,128)S(1)} %get-tuple-element.59.refs_2_, bf16[16,2048]{1,0:T(8,128)(2,1)S(1)} %collective-permute-done.18.refs_3_), custom_call_target="tpu_custom_call" | custom-call | bytes 524288 | tf_op jit(solution)/shard_map/total/pallas_call | solution.py:334
  (14 shorter events, 0.1 us)
Async XLA Ops:
  0.0 7.2 %copy-start.3 = (bf16[4096]{0:T(1024)(128)(2,1)S(1)}, bf16[4096]{0:T(1024)(128)(2,1)}, u32[]{:S(2)}) copy-start(bf16[4096]{0:T(1024)(128)(2,1)} %param.9) | copy-start | bytes 24580
  0.0 8.2 %copy-start = (bf16[2,8,4096]{2,1,0:T(8,128)(2,1)S(1)}, bf16[2,8,4096]{2,1,0:T(8,128)(2,1)}, u32[]{:S(2)}) copy-start(bf16[2,8,4096]{2,1,0:T(8,128)(2,1)} %param.8) | copy-start | bytes 393220
  0.0 6.7 %collective-permute-start.1 = (bf16[16,4096]{1,0:T(8,128)(2,1)}, bf16[16,4096]{1,0:T(8,128)(2,1)S(1)}, u32[]{:S(2)}, u32[]{:S(2)}) collective-permute-start(bf16[16,4096]{1,0:T(8,128)(2,1)} %bitcast.3), channel_id=1, source_target_pairs={{0,8},{4,12},{8,0},{12,4},{1,9},{5,13},{9,1},{13,5},{2,10},{6,14},... | collective-permute-start | bytes 393224 | tf_op jit(solution)/shard_map/gather_tokens/ppermute | solution.py:44
  2.9 4.3 %collective-permute-start = (bf16[16,4096]{1,0:T(8,128)(2,1)}, bf16[16,4096]{1,0:T(8,128)(2,1)S(1)}, u32[]{:S(2)}, u32[]{:S(2)}) collective-permute-start(bf16[16,4096]{1,0:T(8,128)(2,1)} %bitcast.4), channel_id=1, source_target_pairs={{0,4},{4,0},{8,12},{12,8},{1,5},{5,1},{9,13},{13,9},{2,6},{6,2},{1... | collective-permute-start | bytes 393224 | tf_op jit(solution)/shard_map/gather_tokens/ppermute | solution.py:44
  6.7 1.5 %collective-permute-start.2 = (bf16[16,4096]{1,0:T(8,128)(2,1)S(1)}, bf16[16,4096]{1,0:T(8,128)(2,1)S(1)}, u32[]{:S(2)}, u32[]{:S(2)}) collective-permute-start(bf16[16,4096]{1,0:T(8,128)(2,1)S(1)} %collective-permute-done.1.refs_2_), channel_id=1, source_target_pairs={{0,4},{4,0},{8,12},{12,8},{1,5},{5,1},{9,13},{13,9},{2,6},{6,2},{1... | collective-permute-start | bytes 393224 | tf_op jit(solution)/shard_map/gather_tokens/ppermute | solution.py:44
  7.2 9.9 %copy-start.1 = (s32[2]{0:T(128)S(1)}, s32[2]{0:T(128)}, u32[]{:S(2)}) copy-start(s32[2]{0:T(128)} %param.12) | copy-start | bytes 28
  7.3 9.9 %copy-start.2 = (f32[1,128]{1,0:T(1,128)S(1)}, f32[1,128]{1,0:T(1,128)}, u32[]{:S(2)}) copy-start(f32[1,128]{1,0:T(1,128)} %constant.2.clone.refs_4_) | copy-start | bytes 1540
  12.7 8.6 %collective-permute-start.3 = (bf16[16,2432]{1,0:T(8,128)(2,1)S(1)}, bf16[16,2432]{1,0:T(8,128)(2,1)S(1)}, u32[]{:S(2)}, u32[]{:S(2)}) collective-permute-start(bf16[16,2432]{1,0:T(8,128)(2,1)S(1)} %get-tuple-element.35), channel_id=1, source_target_pairs={{0,3},{1,2},{2,1},{3,0},{4,7},{5,6},{6,5},{7,4},{8,11},{9,10},{10,... | collective-permute-start | bytes 233480 | tf_op jit(solution)/shard_map/sum_over_narrow/ppermute | solution.py:44
  16.4 7.0 %collective-permute-start.4 = (bf16[16,2432]{1,0:T(8,128)(2,1)S(1)}, bf16[16,2432]{1,0:T(8,128)(2,1)S(1)}, u32[]{:S(2)}, u32[]{:S(2)}) collective-permute-start(bf16[16,2432]{1,0:T(8,128)(2,1)S(1)} %get-tuple-element.36), channel_id=1, source_target_pairs={{0,2},{1,3},{2,0},{3,1},{4,6},{5,7},{6,4},{7,5},{8,10},{9,11},{10,... | collective-permute-start | bytes 233480 | tf_op jit(solution)/shard_map/sum_over_narrow/ppermute | solution.py:44
  16.4 7.0 %collective-permute-start.5 = (bf16[16,2432]{1,0:T(8,128)(2,1)S(1)}, bf16[16,2432]{1,0:T(8,128)(2,1)S(1)}, u32[]{:S(2)}, u32[]{:S(2)}) collective-permute-start(bf16[16,2432]{1,0:T(8,128)(2,1)S(1)} %get-tuple-element.37), channel_id=1, source_target_pairs={{0,1},{1,0},{2,3},{3,2},{4,5},{5,4},{6,7},{7,6},{8,9},{9,8},{10,11... | collective-permute-start | bytes 233480 | tf_op jit(solution)/shard_map/sum_over_narrow/ppermute | solution.py:44
  23.6 4.1 %collective-permute-start.6 = (bf16[4,2304]{1,0:T(4,128)(2,1)S(1)}, bf16[4,2304]{1,0:T(4,128)(2,1)S(1)}, u32[]{:S(2)}, u32[]{:S(2)}) collective-permute-start(bf16[4,2304]{1,0:T(4,128)(2,1)S(1)} %get-tuple-element.41), channel_id=1, source_target_pairs={{0,4},{4,0},{8,12},{12,8},{1,5},{5,1},{9,13},{13,9},{2,6},{6,2},{1... | collective-permute-start | bytes 55304 | tf_op jit(solution)/shard_map/columns_to_owner/ppermute | solution.py:44
  23.7 4.1 %collective-permute-start.7 = (bf16[4,2304]{1,0:T(4,128)(2,1)S(1)}, bf16[4,2304]{1,0:T(4,128)(2,1)S(1)}, u32[]{:S(2)}, u32[]{:S(2)}) collective-permute-start(bf16[4,2304]{1,0:T(4,128)(2,1)S(1)} %get-tuple-element.42), channel_id=1, source_target_pairs={{0,8},{4,12},{8,0},{12,4},{1,9},{5,13},{9,1},{13,5},{2,10},{6,14},... | collective-permute-start | bytes 55304 | tf_op jit(solution)/shard_map/columns_to_owner/ppermute | solution.py:44
  25.0 3.2 %collective-permute-start.8 = (bf16[4,2304]{1,0:T(4,128)(2,1)S(1)}, bf16[4,2304]{1,0:T(4,128)(2,1)S(1)}, u32[]{:S(2)}, u32[]{:S(2)}) collective-permute-start(bf16[4,2304]{1,0:T(4,128)(2,1)S(1)} %get-tuple-element.43), channel_id=1, source_target_pairs={{0,12},{4,8},{8,4},{12,0},{1,13},{5,9},{9,5},{13,1},{2,14},{6,10},... | collective-permute-start | bytes 55304 | tf_op jit(solution)/shard_map/columns_to_owner/ppermute | solution.py:44
  29.5 4.0 %collective-permute-start.9 = (bf16[4,2176]{1,0:T(4,128)(2,1)S(1)}, bf16[4,2176]{1,0:T(4,128)(2,1)S(1)}, u32[]{:S(2)}, u32[]{:S(2)}) collective-permute-start(bf16[4,2176]{1,0:T(4,128)(2,1)S(1)} %get-tuple-element.48), channel_id=1, source_target_pairs={{0,8},{4,12},{8,0},{12,4},{1,9},{5,13},{9,1},{13,5},{2,10},{6,14},... | collective-permute-start | bytes 52232 | tf_op jit(solution)/shard_map/heads_to_weights/ppermute | solution.py:44
  30.4 3.2 %collective-permute-start.10 = (bf16[4,2176]{1,0:T(4,128)(2,1)S(1)}, bf16[4,2176]{1,0:T(4,128)(2,1)S(1)}, u32[]{:S(2)}, u32[]{:S(2)}) collective-permute-start(bf16[4,2176]{1,0:T(4,128)(2,1)S(1)} %get-tuple-element.49), channel_id=1, source_target_pairs={{0,12},{4,8},{8,4},{12,0},{1,13},{5,9},{9,5},{13,1},{2,14},{6,10},... | collective-permute-start | bytes 52232 | tf_op jit(solution)/shard_map/heads_to_weights/ppermute | solution.py:44
  31.9 1.5 %collective-permute-start.11 = (bf16[4,2048]{1,0:T(4,128)(2,1)S(1)}, bf16[4,2048]{1,0:T(4,128)(2,1)S(1)}, u32[]{:S(2)}, u32[]{:S(2)}) collective-permute-start(bf16[4,2048]{1,0:T(4,128)(2,1)S(1)} %attend.4), channel_id=1, source_target_pairs={{0,4},{4,0},{8,12},{12,8},{1,5},{5,1},{9,13},{13,9},{2,6},{6,2},{1... | collective-permute-start | bytes 49160 | tf_op jit(solution)/shard_map/heads_to_weights/ppermute | solution.py:44
  33.6 8.5 %collective-permute-start.12 = (bf16[16,2048]{1,0:T(8,128)(2,1)S(1)}, bf16[16,2048]{1,0:T(8,128)(2,1)S(1)}, u32[]{:S(2)}, u32[]{:S(2)}) collective-permute-start(bf16[16,2048]{1,0:T(8,128)(2,1)S(1)} %join.1.refs_1_.refs_3_), channel_id=1, source_target_pairs={{0,3},{1,2},{2,1},{3,0},{4,7},{5,6},{6,5},{7,4},{8,11},{9,10},{10,... | collective-permute-start | bytes 196616 | tf_op jit(solution)/shard_map/gather_over_narrow/ppermute | solution.py:44
  36.2 6.4 %collective-permute-start.13 = (bf16[16,2048]{1,0:T(8,128)(2,1)S(1)}, bf16[16,2048]{1,0:T(8,128)(2,1)S(1)}, u32[]{:S(2)}, u32[]{:S(2)}) collective-permute-start(bf16[16,2048]{1,0:T(8,128)(2,1)S(1)} %join.1.refs_1_.refs_3_), channel_id=1, source_target_pairs={{0,2},{1,3},{2,0},{3,1},{4,6},{5,7},{6,4},{7,5},{8,10},{9,11},{10,... | collective-permute-start | bytes 196616 | tf_op jit(solution)/shard_map/gather_over_narrow/ppermute | solution.py:44
  36.2 6.4 %collective-permute-start.14 = (bf16[16,2048]{1,0:T(8,128)(2,1)S(1)}, bf16[16,2048]{1,0:T(8,128)(2,1)S(1)}, u32[]{:S(2)}, u32[]{:S(2)}) collective-permute-start(bf16[16,2048]{1,0:T(8,128)(2,1)S(1)} %join.1.refs_1_.refs_3_), channel_id=1, source_target_pairs={{0,1},{1,0},{2,3},{3,2},{4,5},{5,4},{6,7},{7,6},{8,9},{9,8},{10,11... | collective-permute-start | bytes 196616 | tf_op jit(solution)/shard_map/gather_over_narrow/ppermute | solution.py:44
  44.3 2.2 %collective-permute-start.15 = (bf16[32,2048]{1,0:T(8,128)(2,1)S(1)}, bf16[32,2048]{1,0:T(8,128)(2,1)S(1)}, u32[]{:S(2)}, u32[]{:S(2)}) collective-permute-start(bf16[32,2048]{1,0:T(8,128)(2,1)S(1)} %get-tuple-element.53), channel_id=1, source_target_pairs={{0,4},{4,0},{8,12},{12,8},{1,5},{5,1},{9,13},{13,9},{2,6},{6,2},{1... | collective-permute-start | bytes 393224 | tf_op jit(solution)/shard_map/sum_over_wide/ppermute | solution.py:44
  46.0 1.9 %collective-permute-start.17 = (bf16[32,2048]{1,0:T(8,128)(2,1)S(1)}, bf16[32,2048]{1,0:T(8,128)(2,1)S(1)}, u32[]{:S(2)}, u32[]{:S(2)}) collective-permute-start(bf16[32,2048]{1,0:T(8,128)(2,1)S(1)} %get-tuple-element.58), channel_id=1, source_target_pairs={{0,4},{4,0},{8,12},{12,8},{1,5},{5,1},{9,13},{13,9},{2,6},{6,2},{1... | collective-permute-start | bytes 393224 | tf_op jit(solution)/shard_map/sum_over_wide/ppermute | solution.py:44
  46.6 4.7 %collective-permute-start.16 = (bf16[16,2048]{1,0:T(8,128)(2,1)S(1)}, bf16[16,2048]{1,0:T(8,128)(2,1)S(1)}, u32[]{:S(2)}, u32[]{:S(2)}) collective-permute-start(bf16[16,2048]{1,0:T(8,128)(2,1)S(1)} %get-tuple-element.55), channel_id=1, source_target_pairs={{0,8},{4,12},{8,0},{12,4},{1,9},{5,13},{9,1},{13,5},{2,10},{6,14},... | collective-permute-start | bytes 196616 | tf_op jit(solution)/shard_map/sum_over_wide/ppermute | solution.py:44
  48.0 4.3 %collective-permute-start.18 = (bf16[16,2048]{1,0:T(8,128)(2,1)S(1)}, bf16[16,2048]{1,0:T(8,128)(2,1)S(1)}, u32[]{:S(2)}, u32[]{:S(2)}) collective-permute-start(bf16[16,2048]{1,0:T(8,128)(2,1)S(1)} %get-tuple-element.60), channel_id=1, source_target_pairs={{0,8},{4,12},{8,0},{12,4},{1,9},{5,13},{9,1},{13,5},{2,10},{6,14},... | collective-permute-start | bytes 196616 | tf_op jit(solution)/shard_map/sum_over_wide/ppermute | solution.py:44
